TPU v7x, 32 devices: a whole 2x2x4 slice. The times are simulated.
32 devices in a mesh: loop: 16 (over z, x, core), tp: 2 (over y).
Axes of the slice: x: 2, y: 2, z: 4, core: 2. Of those that a mesh axis runs over, the one named last changes fastest.
Arguments:
- mixer_in: bfloat16 [2048, 8192], P('loop', 'tp'), may hold values from -6 to 6
- gate_in: bfloat16 [2048, 8192], P('loop', 'tp'), may hold values from -6 to 6
- residual_in: bfloat16 [2048, 4096], P('loop', 'tp'), may hold values from -6 to 6
- conv_weight: float32 [4, 8192], P(None, 'tp'), may hold values from -3 to 3
- conv_bias: float32 [8192], P('tp'), may hold values from -3 to 3
- state_proj: bfloat16 [8192, 288], P('tp'), may hold values from -0.046875 to 0.046875
- step_proj: bfloat16 [256, 8192], P(None, 'tp'), may hold values from -0.375 to 0.375
- step_bias: float32 [8192], P('tp'), may hold values from -4 to -1
- decay_rate: float32 [16, 8192], P(None, 'tp'), may hold values from 2.4414063e-05 to 4
- skip_gain: float32 [8192], P('tp'), may hold values from 0.25 to 4
- out_proj: bfloat16 [8192, 4096], P('tp', 'loop'), may hold values from -0.09375 to 0.09375
- segment_ids: int32 [2048], replicated, may hold values from 0 to 1, never falling along the last dimension, each value on 1 to 1920 neighbouring positions
- gate_weight: bfloat16 [16, 4096, 6144], P('loop', None, 'tp'), may hold values from -0.09375 to 0.09375
- up_weight: bfloat16 [16, 4096, 6144], P('loop', None, 'tp'), may hold values from -0.09375 to 0.09375
- down_weight: bfloat16 [16, 6144, 4096], P('loop', 'tp'), may hold values from -0.078125 to 0.078125
- routes: int32 [2048, 2], P('loop'), may hold values from 0 to 7, all different within a row; in each aligned block of 128 rows (0 to 127, 128 to 255, ...) at most 40 rows name the same one
- route_weight: float32 [2048, 2], P('loop'), may hold values from 0.2 to 1
- keep_mask: int32 [16, 8], P('loop'), may hold values 0 or 1
Outputs:
- layer_out: bfloat16 [2048, 4096], P('loop', 'tp')
Inputs may be any that keep to these rules, and one draw needn't show every extreme that they name: `routes`: in each aligned block of 128 rows, the rows of one device, no expert is named by more than 40 rows.
All inputs are finite; a program needn't handle non-finite values. No bound on the sum of `keep_mask` on one device may be relied on, other than what follows from the above.
Results may differ from a plain program's by a relative error of at most 0.014.
Values may be sent and summed in bfloat16 or wider, within the bound.
No kernel may reach another device: no remote copies, remote signals or barrier semaphores. Data moves between devices by JAX's collectives and lax.ppermute only.
A program may use at most 512 MiB of HBM per device.

v0:
```python
import jax
import jax.numpy as jnp
from jax import lax
from jax.sharding import PartitionSpec as P

NSTATE = 16
RANK = 256
EXPERTS = 8
TOPK = 2
CAP = 40


def shifted(x, axis, by):
    size = lax.axis_size(axis)
    pairs = [(i, i + by) for i in range(size) if 0 <= i + by < size]
    return lax.ppermute(x, axis, pairs)


def carried_in(value, axis, join, neutral):
    count, mine = (lax.axis_size(axis), lax.axis_index(axis))
    pieces = jax.tree.map(lambda part: lax.all_gather(part, axis), value)
    total = jax.tree.map(
        lambda part, zero: jnp.full_like(part, 0) + jnp.asarray(zero, part.dtype), value, neutral
    )

    def lap(position, total):
        longer = join(total, jax.tree.map(lambda part: part[position], pieces))
        return jax.tree.map(lambda new, old: jnp.where(position < mine, new, old), longer, total)

    return lax.fori_loop(0, count - 1, lap, total)


def combine_pair(earlier, later):
    return (earlier[0] * later[0], later[0] * earlier[1] + later[1])


def per_device(
    mixer_in,
    gate_in,
    residual_in,
    conv_weight,
    conv_bias,
    state_proj,
    step_proj,
    step_bias,
    decay_rate,
    skip_gain,
    out_proj,
    segment_ids,
    gate_weight,
    up_weight,
    down_weight,
    routes,
    route_weight,
    keep_mask,
):
    tokens = mixer_in.shape[0]
    channels = mixer_in.shape[1]
    conv_taps = conv_weight.shape[0]
    rim_rows = shifted(mixer_in[tokens - (conv_taps - 1) :], "loop", 1)
    extended = jnp.concatenate([rim_rows, mixer_in], axis=0)
    conv_sum = jnp.broadcast_to(conv_bias[None, :], (tokens, channels))
    for offset in range(conv_taps):
        conv_sum = conv_sum + conv_weight[offset][None, :] * extended[
            offset : offset + tokens
        ].astype(jnp.float32)
    conved = jax.nn.silu(conv_sum).astype(jnp.bfloat16)
    block_start = lax.axis_index("loop") * tokens
    local_ids = lax.dynamic_slice_in_dim(segment_ids, block_start, tokens)
    before_start = jnp.maximum(block_start - 1, 0)
    before_id = lax.dynamic_slice_in_dim(segment_ids, before_start, 1)
    previous = jnp.where(block_start > 0, before_id, local_ids[:1])
    earlier_ids = jnp.concatenate([previous, local_ids[:-1]])
    kept = (local_ids == earlier_ids).astype(jnp.float32)
    projected = lax.psum(jnp.dot(conved, state_proj, preferred_element_type=jnp.float32), "tp")
    low_rank = projected[:, :RANK].astype(jnp.bfloat16)
    in_gain = projected[:, RANK : RANK + NSTATE]
    out_gain = projected[:, RANK + NSTATE :]
    step_size = jax.nn.softplus(
        jnp.dot(low_rank, step_proj, preferred_element_type=jnp.float32) + step_bias[None, :]
    )
    conved_f = conved.astype(jnp.float32)
    factor = kept[:, None, None] * jnp.exp(-step_size[:, None, :] * decay_rate[None, :, :])
    driven = (step_size * conved_f)[:, None, :] * in_gain[:, :, None]
    cum_factor, cum_state = lax.associative_scan(combine_pair, (factor, driven), axis=0)
    carried = carried_in(
        (cum_factor[-1], cum_state[-1]),
        "loop",
        combine_pair,
        (jnp.ones_like(cum_factor[-1]), jnp.zeros_like(cum_state[-1])),
    )
    states = cum_factor * carried[1][None, :, :] + cum_state
    scanned = jnp.sum(out_gain[:, :, None] * states, axis=1)
    mixer_y = scanned + skip_gain[None, :] * conved_f
    gated = (mixer_y * jax.nn.silu(gate_in.astype(jnp.float32))).astype(jnp.bfloat16)
    partial_mix = jnp.dot(
        gated,
        lax.all_gather(out_proj, "loop", axis=1, tiled=True),
        preferred_element_type=jnp.float32,
    )
    mixed_out = lax.psum_scatter(partial_mix, "tp", scatter_dimension=1, tiled=True)
    hidden_in = (residual_in.astype(jnp.float32) + mixed_out).astype(jnp.bfloat16)
    groups = lax.axis_size("loop")
    quarters = groups // EXPERTS
    flat_routes = routes.reshape(-1)
    expert_ids = jnp.arange(EXPERTS, dtype=jnp.int32)
    onehot = (flat_routes[:, None] == expert_ids[None, :]).astype(jnp.int32)
    slot_index = jnp.sum(jnp.cumsum(onehot, axis=0) * onehot, axis=1) - 1
    target = flat_routes * CAP + slot_index
    selector = (jnp.arange(EXPERTS * CAP, dtype=jnp.int32)[:, None] == target[None, :]).astype(
        jnp.float32
    )
    gather_matrix = jnp.sum(selector.reshape(EXPERTS * CAP, tokens, TOPK), axis=2)
    keep_weight = jnp.sum(onehot.astype(jnp.float32) * keep_mask.astype(jnp.float32), axis=1)
    weights = route_weight.reshape(-1) * keep_weight
    weighted = jnp.sum((selector * weights[None, :]).reshape(EXPERTS * CAP, tokens, TOPK), axis=2)
    source = lax.all_gather(hidden_in, "tp", axis=1, tiled=True)
    feature_count = source.shape[1]
    packed = jnp.dot(
        gather_matrix.astype(jnp.bfloat16), source, preferred_element_type=jnp.float32
    ).astype(jnp.bfloat16)
    outgoing = jnp.broadcast_to(
        packed.reshape(EXPERTS, 1, CAP, feature_count), (EXPERTS, quarters, CAP, feature_count)
    ).reshape(groups, CAP, feature_count)
    arrived = lax.all_to_all(outgoing, "loop", split_axis=0, concat_axis=0, tiled=True)
    slot_count = arrived.shape[1]
    slot_rows = arrived.reshape(groups * slot_count, arrived.shape[2])
    gate_value = jnp.dot(slot_rows, gate_weight[0], preferred_element_type=jnp.float32)
    up_value = jnp.dot(slot_rows, up_weight[0], preferred_element_type=jnp.float32)
    hidden = (jax.nn.silu(gate_value) * up_value).astype(jnp.bfloat16)
    partial_out = jnp.dot(hidden, down_weight[0], preferred_element_type=jnp.float32)
    shares = lax.psum_scatter(
        partial_out.astype(jnp.bfloat16), "tp", scatter_dimension=1, tiled=True
    )
    returned = lax.all_to_all(
        shares.reshape(groups, slot_count, shares.shape[1]),
        "loop",
        split_axis=0,
        concat_axis=0,
        tiled=True,
    )
    local_width = returned.shape[2]
    summed = jnp.sum(
        returned.astype(jnp.float32).reshape(EXPERTS, quarters, CAP, local_width), axis=1
    ).reshape(EXPERTS * CAP, local_width)
    expert_sum = jnp.dot(
        weighted.T, summed, precision=lax.Precision.HIGHEST, preferred_element_type=jnp.float32
    )
    return (hidden_in.astype(jnp.float32) + expert_sum).astype(jnp.bfloat16)


def solution(mesh):
    return jax.shard_map(
        per_device,
        mesh=mesh,
        in_specs=(
            P("loop", "tp"),
            P("loop", "tp"),
            P("loop", "tp"),
            P(None, "tp"),
            P("tp"),
            P("tp", None),
            P(None, "tp"),
            P("tp"),
            P(None, "tp"),
            P("tp"),
            P("tp", "loop"),
            P(),
            P("loop", None, "tp"),
            P("loop", None, "tp"),
            P("loop", "tp", None),
            P("loop", None),
            P("loop", None),
            P("loop", None),
        ),
        out_specs=P("loop", "tp"),
        check_vma=False,
    )
```

profile of v0, /device:TPU:0, one launch (start us, length us, event | category | flops | bytes accessed | tf_op | source)
XLA Modules:
  0.0 1389.5 jit_solution(8110898471831145311)
XLA Ops:
  19.5 22.7 %all-reduce.30.cloned.1.call-done = f32[128,288]{0,1:T(8,128)} async-done(((f32[128,288]{0,1:T(8,128)}), f32[128,288]{0,1:T(8,128)}) %all-reduce.30.cloned.1.call-update) | async-done | bytes 147472 | tf_op jit(solution)/shard_map/psum | solution.py:75
  47.0 22.4 %exponential_multiply_fusion = (f32[128,16,4096]{2,1,0:T(8,128)}, f32[128,16,4096]{2,1,0:T(8,128)}) fusion(f32[16,4096]{1,0:T(8,128)S(1)} %copy-done.23, f32[128,4096]{1,0:T(8,128)S(1)} %get-tuple-element.150, f32[128]{0:T(128)S(1)} %compare_convert_fusion, f32[128,16]{1,0:T(8,128)S(1)} %copy.47, f32[128,4096]{1,0:T(8,128)S(1)} %get-tuple-element.151), kind=kLoop, calls=%fused_computation.4 | loop fusion | flops 25165824 | bytes 71574016 | tf_op jit(solution)/shard_map/mul | solution.py:83
  69.4 34.6 %slice_multiply_fusion = (f32[64,16,4096]{2,1,0:T(8,128)}, f32[64,16,4096]{2,1,0:T(8,128)}) fusion(f32[128,16,4096]{2,1,0:T(8,128)} %get-tuple-element.168, f32[128,16,4096]{2,1,0:T(8,128)} %get-tuple-element.169), kind=kLoop, calls=%fused_computation.15 | loop fusion | flops 12582912 | bytes 100663296 | tf_op jit(solution)/shard_map/mul | solution.py:34
  104.0 19.1 %slice_multiply_fusion.1 = (f32[32,16,4096]{2,1,0:T(8,128)}, f32[32,16,4096]{2,1,0:T(8,128)}) fusion(f32[64,16,4096]{2,1,0:T(8,128)} %get-tuple-element.132, f32[64,16,4096]{2,1,0:T(8,128)} %get-tuple-element.133), kind=kLoop, calls=%fused_computation.22 | loop fusion | flops 6291456 | bytes 50331648 | tf_op jit(solution)/shard_map/mul | solution.py:34
  242.5 13.4 pad.108
  269.3 13.4 pad.95
  287.2 13.4 pad.94
  311.8 22.5 %add_multiply_fusion.3 = (f32[31,16,4096]{2,1,0:T(8,128)}, f32[31,16,4096]{2,1,0:T(8,128)}) fusion(f32[32,16,4096]{2,1,0:T(8,128)} %pad.95, f32[32,16,4096]{2,1,0:T(8,128)} %pad.94, f32[64,16,4096]{2,1,0:T(8,128)} %get-tuple-element.132, f32[64,16,4096]{2,1,0:T(8,128)} %get-tuple-element.133, f32[32,16,4096]{2,1,0:T(8,128)} %pad.109, f32[32,16,4096]{2,1,0:T(8,128)} %pad.108), kind=kLoop, calls=%fused_computation.25 | loop fusion | flops 10158080 | bytes 65011712 | tf_op jit(solution)/shard_map/mul | solution.py:34
  353.9 24.9 %pad.110 = f32[64,16,4096]{2,1,0:T(8,128)} pad(f32[32,16,4096]{2,1,0:T(8,128)} %pad_maximum_fusion.3, f32[]{:T(128)} %constant.56.clone.1), padding=0_1_1x0_0_0x0_0_0 | pad | bytes 25165828 | tf_op jit(solution)/shard_map/pad | solution.py:85
  378.8 24.9 %pad.111 = f32[64,16,4096]{2,1,0:T(8,128)} pad(f32[32,16,4096]{2,1,0:T(8,128)} %add.268, f32[]{:T(128)} %constant.56.clone.1), padding=1_0_1x0_0_0x0_0_0 | pad | bytes 25165828 | tf_op jit(solution)/shard_map/pad | solution.py:85
  403.7 17.9 %add.270 = f32[64,16,4096]{2,1,0:T(8,128)} add(f32[64,16,4096]{2,1,0:T(8,128)} %pad.110, f32[64,16,4096]{2,1,0:T(8,128)} %pad.111) | non-fusion elementwise | flops 4194304 | bytes 50331648 | tf_op jit(solution)/shard_map/add | solution.py:85
  421.6 48.1 %pad.113 = f32[128,16,4096]{2,1,0:T(8,128)} pad(f32[64,16,4096]{2,1,0:T(8,128)} %add.270, f32[]{:T(128)} %constant.56.clone.1), padding=1_0_1x0_0_0x0_0_0 | pad | bytes 50331652 | tf_op jit(solution)/shard_map/pad | solution.py:85
  477.3 24.9 %pad.96 = f32[64,16,4096]{2,1,0:T(8,128)} pad(f32[32,16,4096]{2,1,0:T(8,128)} %pad_maximum_fusion.2, f32[]{:T(128)} %constant.56.clone.1), padding=0_1_1x0_0_0x0_0_0 | pad | bytes 25165828 | tf_op jit(solution)/shard_map/pad | solution.py:85
  502.2 24.9 %pad.97 = f32[64,16,4096]{2,1,0:T(8,128)} pad(f32[32,16,4096]{2,1,0:T(8,128)} %add.250, f32[]{:T(128)} %constant.56.clone.1), padding=1_0_1x0_0_0x0_0_0 | pad | bytes 25165828 | tf_op jit(solution)/shard_map/pad | solution.py:85
  527.1 43.9 %add_multiply_fusion.1 = (f32[63,16,4096]{2,1,0:T(8,128)}, f32[63,16,4096]{2,1,0:T(8,128)}) fusion(f32[64,16,4096]{2,1,0:T(8,128)} %pad.97, f32[64,16,4096]{2,1,0:T(8,128)} %pad.96, f32[128,16,4096]{2,1,0:T(8,128)} %get-tuple-element.168, f32[128,16,4096]{2,1,0:T(8,128)} %get-tuple-element.169, f32[64,16,4096]{2,1,0:T(8,128)} %pad.111, f32[64,16,4096]{2,1,0:T(8,128)} %pad.110), kind=kLoop, calls=%fused_computation.18 | loop fusion | flops 20643840 | bytes 132120576 | tf_op jit(solution)/shard_map/mul | solution.py:34
  582.5 47.9 %pad.112 = f32[128,16,4096]{2,1,0:T(8,128)} pad(f32[64,16,4096]{2,1,0:T(8,128)} %pad_maximum_fusion.1, f32[]{:T(128)} %constant.56.clone.1), padding=0_1_1x0_0_0x0_0_0 | pad | bytes 50331652 | tf_op jit(solution)/shard_map/pad | solution.py:85
  632.2 18.1 %add.251 = f32[64,16,4096]{2,1,0:T(8,128)} add(f32[64,16,4096]{2,1,0:T(8,128)} %pad.96, f32[64,16,4096]{2,1,0:T(8,128)} %pad.97) | non-fusion elementwise | flops 4194304 | bytes 50331648 | tf_op jit(solution)/shard_map/add | solution.py:85
  651.3 48.1 %pad.99 = f32[128,16,4096]{2,1,0:T(8,128)} pad(f32[64,16,4096]{2,1,0:T(8,128)} %add.251, f32[]{:T(128)} %constant.56.clone.1), padding=1_0_1x0_0_0x0_0_0 | pad | bytes 50331652 | tf_op jit(solution)/shard_map/pad | solution.py:85
  710.9 47.9 %pad.98 = f32[128,16,4096]{2,1,0:T(8,128)} pad(f32[64,16,4096]{2,1,0:T(8,128)} %pad_maximum_fusion, f32[]{:T(128)} %constant.56.clone.1), padding=0_1_1x0_0_0x0_0_0 | pad | bytes 50331652 | tf_op jit(solution)/shard_map/pad | solution.py:85
  761.4 50.0 %all-gather.5.cloned.1.call-done = f32[16,16,4096]{2,1,0:T(8,128)} async-done(((f32[1,16,4096]{2,1,0:T(8,128)}), f32[16,16,4096]{2,1,0:T(8,128)}) %all-gather.5.cloned.1.call-update) | async-done | bytes 4194320 | tf_op jit(solution)/shard_map/all_gather | solution.py:21
  811.4 19.3 %while.14 = (s32[]{:T(128)}, f32[16,4096]{1,0:T(8,128)S(1)}, s32[]{:T(128)}, f32[16,16,4096]{2,1,0:T(8,128)}, f32[16,16,4096]{2,1,0:T(8,128)}, /*index=5*/s32[]{:T(128)}, s32[]{:T(128)}) while((s32[]{:T(128)}, f32[16,4096]{1,0:T(8,128)S(1)}, s32[]{:T(128)}, f32[16,16,4096]{2,1,0:T(8,128)}, f32[16,16,4096]{2,1,0:T(8,128)}, ...), condition=%wide.region_2.3_spmd.clone, body=%wide.region_1.2_spmd.clone.sunk | while | flops 262148 | bytes 1048677 | solution.py:30
  830.7 46.7 %multiply_reduce_fusion = f32[128,4096]{1,0:T(8,128)} fusion(f32[128,16,4096]{2,1,0:T(8,128)} %pad.112, f32[128,16,4096]{2,1,0:T(8,128)} %pad.113, f32[128,16,4096]{2,1,0:T(8,128)} %pad.98, f32[128,16,4096]{2,1,0:T(8,128)} %pad.99, f32[16,4096]{1,0:T(8,128)S(1)} %get-tuple-element.99, f32[128,16]{1,0:T(8,128)S(1)} %copy.46), kind=kLoop, calls=%fused_computation.3 | loop fusion | flops 49807360 | bytes 136585216 | tf_op jit(solution)/shard_map/reduce_sum | solution.py:93
  877.4 110.8 %all-gather.9.cloned.1.call-done = bf16[4096,4096]{1,0:T(8,128)(2,1)} async-done(((bf16[4096,256]{1,0:T(8,128)(2,1)}), bf16[4096,4096]{1,0:T(8,128)(2,1)}) %all-gather.9.cloned.1.call-update) | async-done | bytes 33554448 | tf_op jit(solution)/shard_map/all_gather | solution.py:98
  988.2 17.4 %fusion.28 = f32[128,4096]{1,0:T(8,128)} fusion(bf16[4096,4096]{1,0:T(8,128)(2,1)} %all-gather.9.cloned.1.call-done, f32[128,4096]{1,0:T(8,128)} %multiply_reduce_fusion, bf16[128,4096]{1,0:T(8,128)(2,1)S(1)} %copy-done.17, bf16[128,4096]{1,0:T(8,128)(2,1)S(1)} %copy-done.27, f32[4096]{0:T(1024)S(1)} %copy-done.29), kind=kOutput, calls=%fused_computation.64 | convolution fusion | flops 4300210176 | bytes 39862272 | tf_op jit(solution)/shard_map/dot_general | solution.py:96
  1006.6 30.0 %reduce-scatter.3.cloned.1.call-done = f32[128,2048]{1,0:T(8,128)} async-done(((f32[128,4096]{1,0:T(8,128)}), f32[128,2048]{1,0:T(8,128)}) %reduce-scatter.3.cloned.1.call-update) | async-done | bytes 1048592 | tf_op jit(solution)/shard_map/reduce_scatter | solution.py:101
  1039.9 20.3 %all-gather.11.cloned.1.call-done = bf16[128,4096]{1,0:T(8,128)(2,1)} async-done(((bf16[128,2048]{1,0:T(8,128)(2,1)}), bf16[128,4096]{1,0:T(8,128)(2,1)}) %all-gather.11.cloned.1.call-update) | async-done | bytes 1048592 | tf_op jit(solution)/shard_map/all_gather | solution.py:117
  1062.9 120.6 %all_to_all.10 = bf16[16,40,4096]{2,1,0:T(8,128)(2,1)S(1)} all-to-all(bf16[16,40,4096]{2,1,0:T(8,128)(2,1)S(1)} %bitcast.68), channel_id=1, replica_groups=mesh['loop'=16,'tp'=2] {'loop'}, dimensions={0} | all-to-all | bytes 10485760 | tf_op jit(solution)/shard_map/all_to_all | solution.py:125
  1183.5 19.7 %fusion.5 = f32[640,3072]{1,0:T(8,128)S(1)} fusion(bf16[640,4096]{1,0:T(8,128)(2,1)S(1)} %bitcast.71, bf16[1,4096,3072]{2,1,0:T(8,128)(2,1)} %param.32), kind=kOutput, calls=%fused_computation.9 | convolution fusion | flops 16106127360 | bytes 38273024 | tf_op jit(solution)/shard_map/dot_general | solution.py:128
  1203.2 21.8 %multiply_convert_fusion.clone.4 = bf16[640,3072]{1,0:T(8,128)(2,1)} fusion(f32[640,3072]{1,0:T(8,128)S(1)} %fusion.5, bf16[640,4096]{1,0:T(8,128)(2,1)S(1)} %bitcast.72, bf16[1,4096,3072]{2,1,0:T(8,128)(2,1)} %param.33), kind=kOutput, calls=%fused_computation.26.clone.clone.clone.1 | convolution fusion | flops 16117923840 | bytes 42205184 | tf_op jit(solution)/shard_map/dot_general | solution.py:129
  1224.9 24.0 %fusion.9 = bf16[640,4096]{1,0:T(8,128)(2,1)} fusion(bf16[1,3072,4096]{2,1,0:T(8,128)(2,1)} %param.34, bf16[640,3072]{1,0:T(8,128)(2,1)} %multiply_convert_fusion.clone.4), kind=kOutput, calls=%fused_computation.27 | convolution fusion | flops 16108748800 | bytes 34340864 | tf_op jit(solution)/shard_map/dot_general | solution.py:131
  1249.0 65.6 %reduce-scatter.5.cloned.1.call-done = bf16[640,2048]{1,0:T(8,128)(2,1)} async-done(((bf16[640,4096]{1,0:T(8,128)(2,1)}), bf16[640,2048]{1,0:T(8,128)(2,1)}) %reduce-scatter.5.cloned.1.call-update) | async-done | bytes 2621456 | tf_op jit(solution)/shard_map/reduce_scatter | solution.py:132
  1314.6 64.4 %all_to_all.11 = bf16[16,40,2048]{2,1,0:T(8,128)(2,1)S(1)} all-to-all(bf16[16,40,2048]{2,1,0:T(8,128)(2,1)} %bitcast.73), channel_id=1, replica_groups=mesh['loop'=16,'tp'=2] {'loop'}, dimensions={0} | all-to-all | bytes 5242880 | tf_op jit(solution)/shard_map/all_to_all | solution.py:135
  (186 shorter events, 250.3 us)
Async XLA Ops:
  6.5 7.9 copy-start
  6.5 37.1 %copy-start.28 = (f32[4096]{0:T(1024)S(1)}, f32[4096]{0:T(1024)}, u32[]{:S(2)}) copy-start(f32[4096]{0:T(1024)} %param.27) | copy-start | bytes 49156
  6.5 35.7 %all-reduce.30.cloned.1.call-start = ((), (), s32[]{:S(2)}) async-start(), calls=%async_computation.4 | async-start | bytes 294912 | tf_op jit(solution)/shard_map/psum | solution.py:75
  7.6 3.4 collective-permute-start
  14.4 32.5 %copy-start.16 = (bf16[128,4096]{1,0:T(8,128)(2,1)}, bf16[128,4096]{1,0:T(8,128)(2,1)S(1)}, u32[]{:S(2)}) copy-start(bf16[128,4096]{1,0:T(8,128)(2,1)S(1)} %multiply_convert_fusion.1) | copy-start | bytes 3145732
  15.9 31.1 %copy-start.23 = (f32[16,4096]{1,0:T(8,128)S(1)}, f32[16,4096]{1,0:T(8,128)}, u32[]{:S(2)}) copy-start(f32[16,4096]{1,0:T(8,128)} %param.28) | copy-start | bytes 786436
  15.9 745.5 %all-gather.7.cloned.1.call-start = ((), (), s32[]{:S(2)}) async-start(), calls=%async_computation.6 | async-start | bytes 4456448 | tf_op jit(solution)/shard_map/all_gather | solution.py:21
  153.1 5.5 copy-start.13
  153.1 5.5 copy-start.14
  155.6 7.5 copy-start.21
  159.7 6.6 copy-start.18
  190.8 7.7 copy-start.11
  206.6 7.7 copy-start.12
  219.2 6.4 copy-start.2
  219.2 7.4 copy-start.3
  219.2 8.6 copy-start.4
  227.9 7.0 copy-start.5
  632.2 179.2 %all-gather.5.cloned.1.call-start = ((), (), s32[]{:S(2)}) async-start(), calls=%async_computation.5 | async-start | bytes 4456448 | tf_op jit(solution)/shard_map/all_gather | solution.py:21
  710.9 50.3 %copy-start.24 = (f32[128,16]{0,1:T(8,128)S(1)}, f32[128,16]{0,1:T(8,128)}, u32[]{:S(2)}) copy-start(f32[128,16]{0,1:T(8,128)} %get-tuple-element.162) | copy-start | bytes 24580
  760.6 227.6 %all-gather.9.cloned.1.call-start = ((), (), s32[]{:S(2)}) async-start(), calls=%async_computation.7 | async-start | bytes 35651584 | tf_op jit(solution)/shard_map/all_gather | solution.py:98
  761.2 275.4 %reduce-scatter.3.cloned.1.call-start = ((), (), s32[]{:S(2)}) async-start(), calls=%async_computation.8 | async-start | bytes 3145728 | tf_op jit(solution)/shard_map/reduce_scatter | solution.py:101
  830.7 157.6 %copy-start.17 = (bf16[128,4096]{1,0:T(8,128)(2,1)S(1)}, bf16[128,4096]{1,0:T(8,128)(2,1)}, u32[]{:S(2)}) copy-start(bf16[128,4096]{1,0:T(8,128)(2,1)} %copy-done.16) | copy-start | bytes 3145732
  830.7 157.6 %copy-start.27 = (bf16[128,4096]{1,0:T(8,128)(2,1)S(1)}, bf16[128,4096]{1,0:T(8,128)(2,1)}, u32[]{:S(2)}) copy-start(bf16[128,4096]{1,0:T(8,128)(2,1)} %param.21) | copy-start | bytes 3145732
  830.7 157.6 %copy-start.29 = (f32[4096]{0:T(1024)S(1)}, f32[4096]{0:T(1024)}, u32[]{:S(2)}) copy-start(f32[4096]{0:T(1024)} %param.29) | copy-start | bytes 49156
  877.4 128.4 %copy-start.25 = (s32[128,2]{0,1:T(2,128)S(1)}, s32[128,2]{0,1:T(2,128)}, u32[]{:S(2)}) copy-start(s32[128,2]{0,1:T(2,128)} %param.35) | copy-start | bytes 3076
  877.4 159.2 %copy-start.22 = (bf16[128,2048]{1,0:T(8,128)(2,1)S(1)}, bf16[128,2048]{1,0:T(8,128)(2,1)}, u32[]{:S(2)}) copy-start(bf16[128,2048]{1,0:T(8,128)(2,1)} %param.22) | copy-start | bytes 1572868
  1005.7 33.8 %copy-start.30 = (s32[1,8]{1,0:T(1,128)S(1)}, s32[1,8]{1,0:T(1,128)}, u32[]{:S(2)}) copy-start(s32[1,8]{1,0:T(1,128)} %param.37) | copy-start | bytes 100
  1005.7 34.1 %copy-start.26 = (f32[128,2]{0,1:T(2,128)S(1)}, f32[128,2]{0,1:T(2,128)}, u32[]{:S(2)}) copy-start(f32[128,2]{0,1:T(2,128)} %param.36) | copy-start | bytes 3076
  1005.7 54.5 %all-gather.11.cloned.1.call-start = ((), (), s32[]{:S(2)}) async-start(), calls=%async_computation.9 | async-start | bytes 1572864 | tf_op jit(solution)/shard_map/all_gather | solution.py:117
  1038.7 275.8 %reduce-scatter.5.cloned.1.call-start = ((), (), s32[]{:S(2)}) async-start(), calls=%async_computation.10 | async-start | bytes 7864320 | tf_op jit(solution)/shard_map/reduce_scatter | solution.py:132
  1314.5 65.1 %copy-start.15 = (bf16[128,2048]{1,0:T(8,128)(2,1)S(1)}, bf16[128,2048]{1,0:T(8,128)(2,1)}, u32[]{:S(2)}) copy-start(bf16[128,2048]{1,0:T(8,128)(2,1)} %add_convert_fusion) | copy-start | bytes 1572868
  1314.6 67.9 %copy-start.1 = (bf16[4096,288]{0,1:T(8,128)(2,1)S(1)}, bf16[4096,288]{0,1:T(8,128)(2,1)}, u32[]{:S(2)}) copy-start(bf16[4096,288]{0,1:T(8,128)(2,1)} %param.25) | copy-start | bytes 7077892
  (7 other events, 26.5 us)
Sparse Core Ops, SparseCore 0:
  16.0 26.1 all-reduce.29
  632.3 50.5 all-gather.6
  760.7 50.5 all-gather.4
  812.7 175.4 all-gather.8
  1005.8 30.7 reduce-scatter.2
  1038.8 21.2 all-gather.10
  1249.1 65.4 reduce-scatter.4
where the time goes:
time: 1400 us; the launch traced here: 1390 us
  local copies, waits for them, and re-layouts  413 us (30%)
  other arithmetic  381 us (27%)
  waiting for transfers between devices  300 us (21%)
  blocking collectives  185 us (13%)
  matrix products  92.5 us (7%)
  between operations  14.7 us (1%)
    pad x24, local copies, waits for them, and re-layouts, per_device(): lax.associative_scan(combine_pair, (factor, driven), axis=0)  392 us
    mul x12, other arithmetic, combine_pair(): return (earlier[0] * later[0], later[0] * earlier[1] + later[1])  149 us
    all_to_all x1, blocking collectives, per_device(): lax.all_to_all(outgoing, 'loop', split_axis=0, concat_axis=0, tiled=True)  121 us
    all_gather x1, waiting for transfers between devices, per_device(): lax.all_gather(out_proj, 'loop', axis=1, tiled=True)  111 us
    add x14, other arithmetic, per_device(): lax.associative_scan(combine_pair, (factor, driven), axis=0)  81.2 us
    reduce_scatter x1, waiting for transfers between devices, per_device(): lax.psum_scatter(partial_out.astype(jnp.bfloat16), 'tp', scatter_dimensio...  65.6 us
    all_to_all x1, blocking collectives, per_device(): lax.all_to_all(shares.reshape(groups, slot_count, shares.shape[1]), 'loop...  64.4 us
    concatenate x12, other arithmetic, per_device(): lax.associative_scan(combine_pair, (factor, driven), axis=0)  54.4 us
  transfers between devices with their start and end apart: 8, of which 6 were waited for; matrix products, arithmetic and copies ran while one was open for 14% of the time, Pallas kernels for 0%

commit v1 on v0

v1 whole, which is shorter than its diff:
```python
import math

import jax
import jax.numpy as jnp
from jax import lax
from jax.experimental import pallas as pl
from jax.experimental.pallas import tpu as pltpu
from jax.sharding import PartitionSpec as P

NSTATE = 16
RANK = 256
EXPERTS = 8
TOPK = 2
CAP = 40
LANES = 128
SUBLANES = 8
RESET = 1e30
LOG2E = math.log2(math.e)
VMEM = 40 * 1024 * 1024


def shifted(x, axis, by):
    size = lax.axis_size(axis)
    pairs = [(i, i + by) for i in range(size) if 0 <= i + by < size]
    return lax.ppermute(x, axis, pairs)


def rotated(x, axis, by):
    size = lax.axis_size(axis)
    return lax.ppermute(x, axis, [(i, (i + by) % size) for i in range(size)])


def scan_end_kernel(
    low_ref, proj_ref, bias_ref, decay_ref, conved_ref, gain_ref, kept_ref,
    step_ref, end_ref, sd_ref, u_ref,
):
    tokens, width = step_ref.shape
    chunk = end_ref.shape[2]
    step = jax.nn.softplus(
        jnp.dot(low_ref[...], proj_ref[...], preferred_element_type=jnp.float32) + bias_ref[...]
    )
    step_ref[...] = step
    sd = jnp.where(kept_ref[...] > 0, step, RESET)
    sd_ref[...] = sd.reshape(sd_ref.shape)
    total = jnp.sum(sd, axis=0, keepdims=True)
    u_ref[...] = (step * conved_ref[...].astype(jnp.float32)).reshape(u_ref.shape)
    cols = [slice(i, i + LANES) for i in range(0, width, LANES)]
    rates = [decay_ref[:, c] * -LOG2E for c in cols]

    def advance(i, state):
        for r in range(SUBLANES):
            gain = gain_ref[i * SUBLANES + r]
            state = tuple(
                jnp.exp2(sd_ref[i, r : r + 1, c] * rate) * h + u_ref[i, r : r + 1, c] * gain
                for c, rate, h in zip(cols, rates, state)
            )
        return state

    zero = tuple(jnp.zeros((NSTATE, LANES), jnp.float32) for _ in cols)
    state = jnp.concatenate(lax.fori_loop(0, tokens // SUBLANES, advance, zero), axis=1)
    high = total.astype(jnp.bfloat16).astype(jnp.float32)
    row = lax.broadcasted_iota(jnp.int32, (NSTATE, width), 0)
    tail = jnp.where(row == 0, high, total - high)
    for k in range(width // chunk):
        part = slice(k * chunk, (k + 1) * chunk)
        end_ref[k, :NSTATE, :] = state[:, part].astype(end_ref.dtype)
        end_ref[k, NSTATE:, :] = tail[:, part].astype(end_ref.dtype)


def carry_kernel(ends_ref, decay_ref, carry_ref):
    rate = decay_ref[...] * -LOG2E
    state = jnp.zeros(rate.shape, jnp.float32)
    for block in range(ends_ref.shape[0]):
        carry_ref[block] = state.astype(carry_ref.dtype)
        tail = ends_ref[block, NSTATE:, :].astype(jnp.float32)
        total = tail[0:1] + tail[1:2]
        end = ends_ref[block, :NSTATE, :].astype(jnp.float32)
        state = jnp.exp2(total * rate) * state + end


def scan_kernel(
    step_ref, decay_ref, conved_ref, gain_ref, kept_ref, carry_ref, pick_ref, skip_ref, gate_ref,
    gated_ref, sd_ref, u_ref, states_ref,
):
    tokens, width = step_ref.shape
    step = step_ref[...]
    conved = conved_ref[...].astype(jnp.float32)
    sd_ref[...] = jnp.where(kept_ref[...] > 0, step, RESET).reshape(sd_ref.shape)
    u_ref[...] = (step * conved).reshape(u_ref.shape)
    cols = [slice(i, i + LANES) for i in range(0, width, LANES)]
    rates = [decay_ref[:, c] * -LOG2E for c in cols]

    def advance(i, state):
        for r in range(SUBLANES):
            gain = gain_ref[i * SUBLANES + r]
            state = tuple(
                jnp.exp2(sd_ref[i, r : r + 1, c] * rate) * h + u_ref[i, r : r + 1, c] * gain
                for c, rate, h in zip(cols, rates, state)
            )
            rows = pl.ds(pl.multiple_of((i * SUBLANES + r) * NSTATE, NSTATE), NSTATE)
            for c, h in zip(cols, state):
                states_ref[rows, c] = h.astype(states_ref.dtype)
        return state

    carry = [carry_ref[k].astype(jnp.float32) for k in range(carry_ref.shape[0])]
    carry = jnp.concatenate(carry, axis=1)
    lax.fori_loop(0, tokens // SUBLANES, advance, tuple(carry[:, c] for c in cols))
    scanned = jnp.dot(pick_ref[...], states_ref[...], preferred_element_type=jnp.float32)
    mixer_y = scanned + skip_ref[...] * conved
    gated_ref[...] = (mixer_y * jax.nn.silu(gate_ref[...].astype(jnp.float32))).astype(
        gated_ref.dtype
    )


def whole(shape):
    return pl.BlockSpec(shape, lambda i: (0,) * len(shape))


def scan_end(low_rank, step_proj, step_bias, decay_rate, conved, gain, kept, groups):
    tokens, channels = conved.shape
    rank = low_rank.shape[1]
    width = min(512, channels)
    chunk = channels // groups
    part = lambda rows: pl.BlockSpec((rows, width), lambda i: (0, i))
    return pl.pallas_call(
        scan_end_kernel,
        grid=(channels // width,),
        in_specs=[
            whole((tokens, rank)), part(rank), part(1), part(NSTATE), part(tokens),
            whole((tokens, NSTATE, LANES)), whole((tokens, 1)),
        ],
        out_specs=[
            part(tokens),
            pl.BlockSpec((width // chunk, 2 * NSTATE, chunk), lambda i: (i, 0, 0)),
        ],
        out_shape=[
            jax.ShapeDtypeStruct((tokens, channels), jnp.float32),
            jax.ShapeDtypeStruct((groups, 2 * NSTATE, chunk), jnp.bfloat16),
        ],
        scratch_shapes=[
            pltpu.VMEM((tokens // SUBLANES, SUBLANES, width), jnp.float32),
            pltpu.VMEM((tokens // SUBLANES, SUBLANES, width), jnp.float32),
        ],
        compiler_params=pltpu.CompilerParams(vmem_limit_bytes=VMEM),
        cost_estimate=pl.CostEstimate(
            flops=5 * tokens * NSTATE * channels,
            bytes_accessed=8 * tokens * channels,
            transcendentals=tokens * NSTATE * channels,
        ),
        name="scan_end",
    )(low_rank, step_proj, step_bias[None, :], decay_rate, conved, gain, kept)


def carries(ends, decay_rate):
    groups, _, chunk = ends.shape
    return pl.pallas_call(
        carry_kernel,
        out_shape=jax.ShapeDtypeStruct((groups, NSTATE, chunk), jnp.bfloat16),
        name="carries",
    )(ends, decay_rate)


def scan_gated(step, decay_rate, conved, gain, kept, carry, pick, skip_gain, gate_in):
    tokens, channels = conved.shape
    width = min(512, channels)
    chunk = carry.shape[2]
    part = lambda rows: pl.BlockSpec((rows, width), lambda i: (0, i))
    return pl.pallas_call(
        scan_kernel,
        grid=(channels // width,),
        in_specs=[
            part(tokens), part(NSTATE), part(tokens), whole((tokens, NSTATE, LANES)),
            whole((tokens, 1)),
            pl.BlockSpec((width // chunk, NSTATE, chunk), lambda i: (i, 0, 0)),
            whole(pick.shape), part(1), part(tokens),
        ],
        out_specs=part(tokens),
        scratch_shapes=[
            pltpu.VMEM((tokens // SUBLANES, SUBLANES, width), jnp.float32),
            pltpu.VMEM((tokens // SUBLANES, SUBLANES, width), jnp.float32),
            pltpu.VMEM((tokens * NSTATE, width), jnp.bfloat16),
        ],
        out_shape=jax.ShapeDtypeStruct((tokens, channels), jnp.bfloat16),
        compiler_params=pltpu.CompilerParams(vmem_limit_bytes=VMEM),
        cost_estimate=pl.CostEstimate(
            flops=7 * tokens * NSTATE * channels,
            bytes_accessed=12 * tokens * channels,
            transcendentals=tokens * NSTATE * channels,
        ),
        name="scan_gated",
    )(step, decay_rate, conved, gain, kept, carry, pick, skip_gain[None, :], gate_in)


def summed_over(x, axis):
    total = x
    for by in range(1, lax.axis_size(axis)):
        total = total + rotated(x, axis, by)
    return total


def scattered_sum(parts, axis, mine):
    size = parts.shape[0]
    take = lambda k: lax.dynamic_index_in_dim(parts, k % size, 0, keepdims=False)
    total = take(mine).astype(jnp.float32)
    for by in range(1, size):
        sent = rotated(take(mine + by).astype(jnp.bfloat16), axis, by)
        total = total + sent.astype(jnp.float32)
    return total


def gathered(x, axis, mine, dim):
    size = lax.axis_size(axis)
    shape = x.shape[:dim] + (size * x.shape[dim],) + x.shape[dim + 1 :]
    out = jnp.zeros(shape, x.dtype)
    out = lax.dynamic_update_slice_in_dim(out, x, mine * x.shape[dim], dim)
    for by in range(1, size):
        source = lax.rem(mine + size - by, size)
        out = lax.dynamic_update_slice_in_dim(
            out, rotated(x, axis, by), source * x.shape[dim], dim
        )
    return out


def teams_swapped(x, members):
    groups = lax.axis_size("loop")
    out = [x[0]]
    for s in range(1, x.shape[0]):
        out.append(
            lax.ppermute(
                x[s],
                "loop",
                [(i, ((i // members) ^ s) * members + i % members) for i in range(groups)],
            )
        )
    return jnp.stack(out)


def per_device(
    mixer_in,
    gate_in,
    residual_in,
    conv_weight,
    conv_bias,
    state_proj,
    step_proj,
    step_bias,
    decay_rate,
    skip_gain,
    out_proj,
    segment_ids,
    gate_weight,
    up_weight,
    down_weight,
    routes,
    route_weight,
    keep_mask,
):
    tokens = mixer_in.shape[0]
    channels = mixer_in.shape[1]
    groups = lax.axis_size("loop")
    position = lax.axis_index("loop")
    shard = lax.axis_index("tp")
    shards = lax.axis_size("tp")
    conv_taps = conv_weight.shape[0]
    rim_rows = shifted(mixer_in[tokens - (conv_taps - 1) :], "loop", 1)
    extended = jnp.concatenate([rim_rows, mixer_in], axis=0)
    conv_sum = jnp.broadcast_to(conv_bias[None, :], (tokens, channels))
    for offset in range(conv_taps):
        conv_sum = conv_sum + conv_weight[offset][None, :] * extended[
            offset : offset + tokens
        ].astype(jnp.float32)
    conved = jax.nn.silu(conv_sum).astype(jnp.bfloat16)
    block_start = position * tokens
    local_ids = lax.dynamic_slice_in_dim(segment_ids, block_start, tokens)
    before_start = jnp.maximum(block_start - 1, 0)
    before_id = lax.dynamic_slice_in_dim(segment_ids, before_start, 1)
    previous = jnp.where(block_start > 0, before_id, local_ids[:1])
    earlier_ids = jnp.concatenate([previous, local_ids[:-1]])
    kept = (local_ids == earlier_ids).astype(jnp.float32)[:, None]
    projected = summed_over(
        jnp.dot(conved, state_proj, preferred_element_type=jnp.float32), "tp"
    )
    low_rank = projected[:, :RANK].astype(jnp.bfloat16)
    in_gain = projected[:, RANK : RANK + NSTATE]
    out_gain = projected[:, RANK + NSTATE :]
    gain = jnp.broadcast_to(in_gain[:, :, None], (tokens, NSTATE, LANES))
    state_rows = jnp.arange(tokens * NSTATE, dtype=jnp.int32)
    spread = state_rows[None, :] % NSTATE == jnp.arange(NSTATE, dtype=jnp.int32)[:, None]
    pick = jnp.where(
        state_rows[None, :] // NSTATE == jnp.arange(tokens, dtype=jnp.int32)[:, None],
        jnp.dot(
            out_gain.astype(jnp.bfloat16),
            spread.astype(jnp.bfloat16),
            preferred_element_type=jnp.float32,
        ),
        0.0,
    ).astype(jnp.bfloat16)
    step_size, end_state = scan_end(
        low_rank, step_proj, step_bias, decay_rate, conved, gain, kept, groups
    )
    ends = lax.all_to_all(end_state, "loop", 0, 0, tiled=True)
    chunk = channels // groups
    own_rates = lax.dynamic_slice_in_dim(decay_rate, position * chunk, chunk, 1)
    carry = lax.all_to_all(carries(ends, own_rates), "loop", 0, 0, tiled=True)
    gated = scan_gated(
        step_size, decay_rate, conved, gain, kept, carry, pick, skip_gain, gate_in
    )
    partial_mix = jnp.dot(
        gated,
        lax.all_gather(out_proj, "loop", axis=1, tiled=True),
        preferred_element_type=jnp.float32,
    )
    features = partial_mix.shape[1]
    width = features // shards
    mixed_out = scattered_sum(
        jnp.stack([partial_mix[:, k * width : (k + 1) * width] for k in range(shards)]),
        "tp",
        shard,
    )
    hidden_in = (residual_in.astype(jnp.float32) + mixed_out).astype(jnp.bfloat16)

    members = groups // EXPERTS
    team, member = position // members, position % members
    flat_routes = routes.reshape(-1)
    expert_ids = jnp.arange(EXPERTS, dtype=jnp.int32)
    onehot = (flat_routes[:, None] == expert_ids[None, :]).astype(jnp.int32)
    slot_index = jnp.sum(jnp.cumsum(onehot, axis=0) * onehot, axis=1) - 1
    target = (flat_routes ^ team) * CAP + slot_index
    selector = (jnp.arange(EXPERTS * CAP, dtype=jnp.int32)[:, None] == target[None, :]).astype(
        jnp.float32
    )
    gather_matrix = jnp.sum(selector.reshape(EXPERTS * CAP, tokens, TOPK), axis=2)
    keep_weight = jnp.sum(onehot.astype(jnp.float32) * keep_mask.astype(jnp.float32), axis=1)
    weights = route_weight.reshape(-1) * keep_weight
    weighted = jnp.sum((selector * weights[None, :]).reshape(EXPERTS * CAP, tokens, TOPK), axis=2)
    packed = jnp.dot(
        gather_matrix.astype(jnp.bfloat16), hidden_in, preferred_element_type=jnp.float32
    ).astype(jnp.bfloat16)
    arrived = teams_swapped(packed.reshape(EXPERTS, CAP, width), members)
    rows = EXPERTS * CAP
    arrived = gathered(arrived.reshape(rows, width), "tp", shard, 1)

    def from_member(by):
        pairs = [
            (i, i // members * members + (i + by) % members) for i in range(groups)
        ]
        return lambda x: lax.ppermute(x, "loop", pairs)

    slot_rows = jnp.concatenate(
        [arrived] + [from_member(by)(arrived) for by in range(1, members)], axis=0
    )
    gate_value = jnp.dot(slot_rows, gate_weight[0], preferred_element_type=jnp.float32)
    up_value = jnp.dot(slot_rows, up_weight[0], preferred_element_type=jnp.float32)
    hidden = (jax.nn.silu(gate_value) * up_value).astype(jnp.bfloat16)
    partial_out = jnp.dot(hidden, down_weight[0], preferred_element_type=jnp.float32)
    partial_out = partial_out.astype(jnp.bfloat16).reshape(members, rows, features)
    member_sum = partial_out[0].astype(jnp.float32)
    for by in range(1, members):
        back = from_member(members - by)(partial_out[by])
        member_sum = member_sum + back.astype(jnp.float32)
    shares = scattered_sum(
        jnp.stack([member_sum[:, k * width : (k + 1) * width] for k in range(shards)]),
        "tp",
        shard,
    )
    returned = teams_swapped(
        shares.astype(jnp.bfloat16).reshape(EXPERTS, CAP, width), members
    ).reshape(rows, width)
    expert_sum = jnp.dot(
        weighted.T,
        returned.astype(jnp.float32),
        precision=lax.Precision.HIGHEST,
        preferred_element_type=jnp.float32,
    )
    return (hidden_in.astype(jnp.float32) + expert_sum).astype(jnp.bfloat16)


def solution(mesh):
    return jax.shard_map(
        per_device,
        mesh=mesh,
        in_specs=(
            P("loop", "tp"),
            P("loop", "tp"),
            P("loop", "tp"),
            P(None, "tp"),
            P("tp"),
            P("tp", None),
            P(None, "tp"),
            P("tp"),
            P(None, "tp"),
            P("tp"),
            P("tp", "loop"),
            P(),
            P("loop", None, "tp"),
            P("loop", None, "tp"),
            P("loop", "tp", None),
            P("loop", None),
            P("loop", None),
            P("loop", None),
        ),
        out_specs=P("loop", "tp"),
        check_vma=False,
    )
```

time: 1400 us -> 438 us (0.31)
  local copies, waits for them, and re-layouts: 413 us -> 25 us
  other arithmetic: 381 us -> 10.3 us
  blocking collectives: 185 us -> 0 us
  waiting for transfers between devices: 300 us -> 229 us
  starting transfers between devices: 2.82 us -> 49.7 us
  Pallas kernels: 0 us -> 26.2 us
    pad x24 -> x0, local copies, waits for them, and re-layouts: 392 us -> none  [per_device(): lax.associative_scan(combine_pair, (factor, driven), axis=0)]
    all_to_all x2 -> x0, blocking collectives: 185 us -> none  [the longest x1 121 us: per_device(): lax.all_to_all(outgoing, 'loop', split_axis=0, concat_axis=0, tiled=True)]
    mul x13 -> x0, other arithmetic: 171 us -> none  [the longest x12 149 us: combine_pair(): return (earlier[0] * later[0], later[0] * earlier[1] + later[1])]
    ppermute x0 -> x20, waiting for transfers between devices: none -> 111 us  [the longest x4 69.2 us: rotated(): return lax.ppermute(x, axis, [(i, (i + by) % size) for i in range(size)])]
    reduce_scatter x2 -> x0, waiting for transfers between devices: 95.5 us -> none  [the longest x1 65.6 us: per_device(): lax.psum_scatter(partial_out.astype(jnp.bfloat16), 'tp', scatter_dimensio...]
    add x15 -> x2, other arithmetic: 81.2 us -> 0.97 us  [the longest x1 0.96 us: per_device(): member_sum = member_sum + back.astype(jnp.float32)]
    all_gather x3 -> x0, waiting for transfers between devices: 70.3 us -> none  [the longest x2 50 us: carried_in(): pieces = jax.tree.map(lambda part: lax.all_gather(part, axis), value)]
    concatenate x12 -> x0, other arithmetic: 54.4 us -> none  [per_device(): lax.associative_scan(combine_pair, (factor, driven), axis=0)]
  transfers between devices with their start and end apart: 8 -> 24, of which waited for: 6 -> 14; matrix products, arithmetic and copies ran while one was open for 14% -> 5% of each run, Pallas kernels for 0% -> 6%
where the time goes in v1:
time: 438 us; the launch traced here: 435 us
  waiting for transfers between devices  229 us (52%)
  matrix products  80.2 us (18%)
  starting transfers between devices  49.7 us (11%)
  Pallas kernels  26.2 us (6%)
  local copies, waits for them, and re-layouts  25 us (6%)
  between operations  14.5 us (3%)
  other arithmetic  10.3 us (2%)
    all_gather x1, waiting for transfers between devices, per_device(): lax.all_gather(out_proj, 'loop', axis=1, tiled=True)  95.2 us
    ppermute x4, waiting for transfers between devices, rotated(): return lax.ppermute(x, axis, [(i, (i + by) % size) for i in range(size)])  69.2 us
    ppermute x14, starting transfers between devices, teams_swapped(): lax.ppermute(x[s], 'loop', [(i, (i // members ^ s) * members + i % member...  31.9 us
    ppermute x14, waiting for transfers between devices, teams_swapped(): lax.ppermute(x[s], 'loop', [(i, (i // members ^ s) * members + i % member...  31.8 us
    dot_general x1, matrix products, per_device(): jnp.dot(slot_rows, up_weight[0], preferred_element_type=jnp.float32)  21.4 us
    dot_general x1, matrix products, per_device(): jnp.dot(slot_rows, gate_weight[0], preferred_element_type=jnp.float32)  21 us
    dot_general x1, matrix products, per_device(): jnp.dot(hidden, down_weight[0], preferred_element_type=jnp.float32)  19.7 us
    unnamed x53, local copies, waits for them, and re-layouts  14.9 us
  transfers between devices with their start and end apart: 24, of which 14 were waited for; matrix products, arithmetic and copies ran while one was open for 5% of the time, Pallas kernels for 6%

profile of v1, /device:TPU:0, one launch (start us, length us, event | category | flops | bytes accessed | tf_op | source)
XLA Modules:
  0.0 434.9 jit_solution(12436750769591145952)
XLA Ops:
  8.2 2.4 collective-permute-start
  16.3 3.9 multiply_convert_fusion.2.conved_ref
  21.9 2.4 collective-permute-start.1
  24.9 4.3 collective-permute-done.1
  33.0 11.2 %scan_end.1 = (f32[128,4096]{1,0:T(8,128)S(1)}, bf16[16,32,256]{2,1,0:T(8,128)(2,1)}) custom-call(bf16[128,256]{1,0:T(8,128)(2,1)S(1)} %slice.178.low_ref, bf16[256,4096]{1,0:T(8,128)(2,1)S(1)} %copy-done.4, f32[1,4096]{1,0:T(1,128)S(1)} %bitcast.111, f32[16,4096]{1,0:T(8,128)S(1)} %copy-done.2, bf16[128,4096]{1,0:T(8,128)(2,1)S(1)} %multiply_convert_fusion.2.conved_ref, ...), custom_call_target="tpu_custom_call" | custom-call | flops 41943040 | bytes 4194304 | tf_op jit(solution)/shard_map/scan_end/pallas_call | solution.py:125
  45.5 6.7 %all-to-all-start = ((bf16[16,32,256]{2,1,0:T(8,128)(2,1)}), bf16[16,32,256]{2,1,0:T(8,128)(2,1)S(1)}, u32[]{:S(2)}, u32[]{:S(2)}) async-start(bf16[16,32,256]{2,1,0:T(8,128)(2,1)} %get-tuple-element.8), calls=%async_computation | async-start | bytes 524288 | tf_op jit(solution)/shard_map/all_to_all | solution.py:301
  53.4 13.5 %all-to-all-done.ends_ref = bf16[16,32,256]{2,1,0:T(8,128)(2,1)S(1)} async-done(((bf16[16,32,256]{2,1,0:T(8,128)(2,1)}), bf16[16,32,256]{2,1,0:T(8,128)(2,1)S(1)}, u32[]{:S(2)}, u32[]{:S(2)}) %all-to-all-start) | async-done | bytes 262176 | tf_op jit(solution)/shard_map/all_to_all | solution.py:301
  69.2 3.7 all-to-all-start.1
  74.1 9.0 %all-to-all-done.1.carry_ref = bf16[16,16,256]{2,1,0:T(8,128)(2,1)S(1)} async-done(((bf16[16,16,256]{2,1,0:T(8,128)(2,1)}), bf16[16,16,256]{2,1,0:T(8,128)(2,1)S(1)}, u32[]{:S(2)}, u32[]{:S(2)}) %all-to-all-start.1) | async-done | bytes 131104 | tf_op jit(solution)/shard_map/all_to_all | solution.py:304
  87.9 13.3 %scan_gated.1 = bf16[128,4096]{1,0:T(8,128)(2,1)S(1)} custom-call(f32[128,4096]{1,0:T(8,128)S(1)} %copy-done.10, f32[16,4096]{1,0:T(8,128)S(1)} %copy-done.3, bf16[128,4096]{1,0:T(8,128)(2,1)S(1)} %multiply_convert_fusion.2.conved_ref, f32[128,16,128]{2,1,0:T(8,128)S(1)} %broadcast_in_dim.20.gain_ref, f32[128,1]{1,0:T(8,128)S(1)} %copy.45.kept_ref, ...), custom_call_target="tpu_custom_call" | custom-call | flops 58720256 | bytes 6291456 | tf_op jit(solution)/shard_map/scan_gated/pallas_call | solution.py:168
  101.2 95.2 %all-gather.2.cloned.1.call-done = bf16[4096,4096]{1,0:T(8,128)(2,1)} async-done(((bf16[4096,256]{1,0:T(8,128)(2,1)}), bf16[4096,4096]{1,0:T(8,128)(2,1)}) %all-gather.2.cloned.1.call-update) | async-done | bytes 33554448 | tf_op jit(solution)/shard_map/all_gather | solution.py:310
  196.4 12.9 %fusion.56 = f32[128,4096]{1,0:T(8,128)S(1)} fusion(bf16[128,4096]{1,0:T(8,128)(2,1)S(1)} %scan_gated.1, bf16[4096,4096]{1,0:T(8,128)(2,1)} %all-gather.2.cloned.1.call-done), kind=kOutput, calls=%fused_computation.108 | convolution fusion | flops 4294967296 | bytes 36700160 | tf_op jit(solution)/shard_map/dot_general | solution.py:308
  211.5 12.4 %collective-permute-done.2 = bf16[128,2048]{1,0:T(8,128)(2,1)} collective-permute-done((bf16[128,2048]{1,0:T(8,128)(2,1)S(1)}, bf16[128,2048]{1,0:T(8,128)(2,1)}, u32[]{:S(2)}, u32[]{:S(2)}) %collective-permute-start.2) | collective-permute-done | bytes 524320 | tf_op jit(solution)/shard_map/ppermute | solution.py:30
  228.1 2.2 collective-permute-start.4
  230.3 2.7 collective-permute-start.6
  234.4 2.4 collective-permute-start.8
  237.5 3.8 collective-permute-done.4
  244.0 13.0 %collective-permute-done.7 = bf16[40,2048]{1,0:T(8,128)(2,1)S(1)} collective-permute-done((bf16[40,2048]{1,0:T(8,128)(2,1)S(1)}, bf16[40,2048]{1,0:T(8,128)(2,1)S(1)}, u32[]{:S(2)}, u32[]{:S(2)}) %collective-permute-start.7) | collective-permute-done | bytes 163872 | tf_op jit(solution)/shard_map/ppermute | solution.py:229
  261.7 22.0 %collective-permute-done.10 = bf16[320,2048]{1,0:T(8,128)(2,1)S(1)} collective-permute-done((bf16[320,2048]{1,0:T(8,128)(2,1)}, bf16[320,2048]{1,0:T(8,128)(2,1)S(1)}, u32[]{:S(2)}, u32[]{:S(2)}) %collective-permute-start.10) | collective-permute-done | bytes 1310752 | tf_op jit(solution)/shard_map/ppermute | solution.py:30
  283.9 4.9 %collective-permute-done.11 = bf16[320,4096]{1,0:T(8,128)(2,1)S(1)} collective-permute-done((bf16[320,4096]{1,0:T(8,128)(2,1)S(1)}, bf16[320,4096]{1,0:T(8,128)(2,1)S(1)}, u32[]{:S(2)}, u32[]{:S(2)}) %collective-permute-start.11) | collective-permute-done | bytes 2621472 | tf_op jit(solution)/shard_map/ppermute | solution.py:347
  288.8 21.0 %fusion.4 = f32[640,3072]{1,0:T(8,128)} fusion(bf16[1,4096,3072]{2,1,0:T(8,128)(2,1)} %param.30, bf16[320,4096]{1,0:T(8,128)(2,1)S(1)} %collective-permute-done.11, bf16[320,4096]{1,0:T(8,128)(2,1)S(1)} %constant_dynamic-update-slice_fusion), kind=kOutput, calls=%fused_computation.4 | convolution fusion | flops 16116613120 | bytes 38273024 | tf_op jit(solution)/shard_map/dot_general | solution.py:352
  309.8 21.4 %multiply_convert_fusion.5 = bf16[640,3072]{1,0:T(8,128)(2,1)S(1)} fusion(f32[640,3072]{1,0:T(8,128)} %fusion.4, bf16[1,4096,3072]{2,1,0:T(8,128)(2,1)} %param.31, bf16[320,4096]{1,0:T(8,128)(2,1)S(1)} %collective-permute-done.11, bf16[320,4096]{1,0:T(8,128)(2,1)S(1)} %constant_dynamic-update-slice_fusion), kind=kOutput, calls=%fused_computation.6.clone.clone.1 | convolution fusion | flops 16128409600 | bytes 42205184 | tf_op jit(solution)/shard_map/dot_general | solution.py:353
  331.1 19.7 %fusion.6 = bf16[640,4096]{1,0:T(8,128)(2,1)S(1)} fusion(bf16[1,3072,4096]{2,1,0:T(8,128)(2,1)} %param.32, bf16[640,3072]{1,0:T(8,128)(2,1)S(1)} %multiply_convert_fusion.5), kind=kOutput, calls=%fused_computation.7 | convolution fusion | flops 16108748800 | bytes 34340864 | tf_op jit(solution)/shard_map/dot_general | solution.py:355
  351.4 4.8 %collective-permute-done.12 = bf16[320,4096]{1,0:T(8,128)(2,1)S(1)} collective-permute-done((bf16[320,4096]{1,0:T(8,128)(2,1)S(1)}, bf16[320,4096]{1,0:T(8,128)(2,1)S(1)}, u32[]{:S(2)}, u32[]{:S(2)}) %collective-permute-start.12) | collective-permute-done | bytes 2621472 | tf_op jit(solution)/shard_map/ppermute | solution.py:347
  358.6 30.5 %collective-permute-done.13 = bf16[320,2048]{1,0:T(8,128)(2,1)S(1)} collective-permute-done((bf16[320,2048]{1,0:T(8,128)(2,1)S(1)}, bf16[320,2048]{1,0:T(8,128)(2,1)S(1)}, u32[]{:S(2)}, u32[]{:S(2)}) %collective-permute-start.13) | collective-permute-done | bytes 1310752 | tf_op jit(solution)/shard_map/ppermute | solution.py:30
  391.2 8.0 %collective-permute-start.15 = (bf16[40,2048]{1,0:T(8,128)(2,1)S(1)}, bf16[40,2048]{1,0:T(8,128)(2,1)S(1)}, u32[]{:S(2)}, u32[]{:S(2)}) collective-permute-start(bf16[40,2048]{1,0:T(8,128)(2,1)S(1)} %get-tuple-element.22), channel_id=1, source_target_pairs={{0,8},{2,10},{4,12},{6,14},{8,0},{10,2},{12,4},{14,6},{16,24},{18,... | collective-permute-start | bytes 491528 | tf_op jit(solution)/shard_map/ppermute | solution.py:229
  400.8 1.9 collective-permute-start.17
  403.6 1.8 collective-permute-start.19
  405.5 2.1 collective-permute-done.15
  407.6 5.5 %collective-permute-start.20 = (bf16[40,2048]{1,0:T(8,128)(2,1)S(1)}, bf16[40,2048]{1,0:T(8,128)(2,1)S(1)}, u32[]{:S(2)}, u32[]{:S(2)}) collective-permute-start(bf16[40,2048]{1,0:T(8,128)(2,1)S(1)} %get-tuple-element.17), channel_id=1, source_target_pairs={{0,28},{2,30},{4,24},{6,26},{8,20},{10,22},{12,16},{14,18},{16,12}... | collective-permute-start | bytes 491528 | tf_op jit(solution)/shard_map/ppermute | solution.py:229
  413.1 9.7 %collective-permute-done.17 = bf16[40,2048]{1,0:T(8,128)(2,1)S(1)} collective-permute-done((bf16[40,2048]{1,0:T(8,128)(2,1)S(1)}, bf16[40,2048]{1,0:T(8,128)(2,1)S(1)}, u32[]{:S(2)}, u32[]{:S(2)}) %collective-permute-start.17) | collective-permute-done | bytes 163872 | tf_op jit(solution)/shard_map/ppermute | solution.py:229
  422.9 3.3 collective-permute-done.18
  (127 shorter events, 49.0 us)
Async XLA Ops:
  6.5 13.6 %copy-start = (bf16[4096,288]{0,1:T(8,128)(2,1)S(1)}, bf16[4096,288]{0,1:T(8,128)(2,1)}, u32[]{:S(2)}) copy-start(bf16[4096,288]{0,1:T(8,128)(2,1)} %param.23) | copy-start | bytes 7077892
  6.5 6.7 %copy-start.12 = (f32[4,4096]{1,0:T(4,128)S(1)}, f32[4,4096]{1,0:T(4,128)}, u32[]{:S(2)}) copy-start(f32[4,4096]{1,0:T(4,128)} %param.21) | copy-start | bytes 196612
  6.5 8.2 %copy-start.14 = (s32[128,2]{0,1:T(2,128)S(1)}, s32[128,2]{0,1:T(2,128)}, u32[]{:S(2)}) copy-start(s32[128,2]{0,1:T(2,128)} %param.33) | copy-start | bytes 3076
  6.5 189.8 %all-gather.2.cloned.1.call-start = ((), (), s32[]{:S(2)}) async-start(), calls=%async_computation.2 | async-start | bytes 35651584 | tf_op jit(solution)/shard_map/all_gather | solution.py:310
  8.2 7.5 %collective-permute-start = (bf16[3,4096]{1,0:T(4,128)(2,1)S(1)}, bf16[3,4096]{1,0:T(4,128)(2,1)S(1)}, u32[]{:S(2)}, u32[]{:S(2)}) collective-permute-start(bf16[3,4096]{1,0:T(4,128)(2,1)S(1)} %slice.136), channel_id=1, source_target_pairs={{0,2},{2,4},{4,6},{6,8},{8,10},{10,12},{12,14},{14,16},{16,18},{18... | collective-permute-start | bytes 73736 | tf_op jit(solution)/shard_map/ppermute | solution.py:25
  20.2 4.1 copy-start.16
  20.2 10.3 %copy-start.6 = (f32[4096]{0:T(1024)S(1)}, f32[4096]{0:T(1024)}, u32[]{:S(2)}) copy-start(f32[4096]{0:T(1024)} %param.25) | copy-start | bytes 49156
  21.9 7.2 %collective-permute-start.1 = (f32[128,288]{1,0:T(8,128)}, f32[128,288]{1,0:T(8,128)S(1)}, u32[]{:S(2)}, u32[]{:S(2)}) collective-permute-start(f32[128,288]{1,0:T(8,128)} %fusion.55), channel_id=1, source_target_pairs={{0,1},{1,0},{2,3},{3,2},{4,5},{5,4},{6,7},{7,6},{8,9},{9,8},{10,11... | collective-permute-start | bytes 442376 | tf_op jit(solution)/shard_map/ppermute | solution.py:30
  45.5 37.6 %copy-start.7 = (f32[4096]{0:T(1024)S(1)}, f32[4096]{0:T(1024)}, u32[]{:S(2)}) copy-start(f32[4096]{0:T(1024)} %param.27) | copy-start | bytes 49156
  45.5 21.3 %all-to-all-start = ((bf16[16,32,256]{2,1,0:T(8,128)(2,1)}), bf16[16,32,256]{2,1,0:T(8,128)(2,1)S(1)}, u32[]{:S(2)}, u32[]{:S(2)}) async-start(bf16[16,32,256]{2,1,0:T(8,128)(2,1)} %get-tuple-element.8), calls=%async_computation | async-start | bytes 524288 | tf_op jit(solution)/shard_map/all_to_all | solution.py:301
  69.2 13.9 %all-to-all-start.1 = ((bf16[16,16,256]{2,1,0:T(8,128)(2,1)}), bf16[16,16,256]{2,1,0:T(8,128)(2,1)S(1)}, u32[]{:S(2)}, u32[]{:S(2)}) async-start(bf16[16,16,256]{2,1,0:T(8,128)(2,1)} %carries.1), calls=%async_computation.1 | async-start | bytes 262144 | tf_op jit(solution)/shard_map/all_to_all | solution.py:304
  209.4 1.9 copy-start.15
  209.6 14.3 %collective-permute-start.2 = (bf16[128,2048]{1,0:T(8,128)(2,1)S(1)}, bf16[128,2048]{1,0:T(8,128)(2,1)}, u32[]{:S(2)}, u32[]{:S(2)}) collective-permute-start(bf16[128,2048]{1,0:T(8,128)(2,1)S(1)} %fusion.31), channel_id=1, source_target_pairs={{0,1},{1,0},{2,3},{3,2},{4,5},{5,4},{6,7},{7,6},{8,9},{9,8},{10,11... | collective-permute-start | bytes 1572872 | tf_op jit(solution)/shard_map/ppermute | solution.py:30
  226.0 8.4 %collective-permute-start.3 = (bf16[40,2048]{1,0:T(8,128)(2,1)S(1)}, bf16[40,2048]{1,0:T(8,128)(2,1)S(1)}, u32[]{:S(2)}, u32[]{:S(2)}) collective-permute-start(bf16[40,2048]{1,0:T(8,128)(2,1)S(1)} %get-tuple-element.30), channel_id=1, source_target_pairs={{0,4},{2,6},{4,0},{6,2},{8,12},{10,14},{12,8},{14,10},{16,20},{18,... | collective-permute-start | bytes 491528 | tf_op jit(solution)/shard_map/ppermute | solution.py:229
  228.1 13.2 %collective-permute-start.4 = (bf16[40,2048]{1,0:T(8,128)(2,1)S(1)}, bf16[40,2048]{1,0:T(8,128)(2,1)S(1)}, u32[]{:S(2)}, u32[]{:S(2)}) collective-permute-start(bf16[40,2048]{1,0:T(8,128)(2,1)S(1)} %get-tuple-element.29), channel_id=1, source_target_pairs={{0,8},{2,10},{4,12},{6,14},{8,0},{10,2},{12,4},{14,6},{16,24},{18,... | collective-permute-start | bytes 491528 | tf_op jit(solution)/shard_map/ppermute | solution.py:229
  230.3 12.4 %collective-permute-start.5 = (bf16[40,2048]{1,0:T(8,128)(2,1)S(1)}, bf16[40,2048]{1,0:T(8,128)(2,1)S(1)}, u32[]{:S(2)}, u32[]{:S(2)}) collective-permute-start(bf16[40,2048]{1,0:T(8,128)(2,1)S(1)} %get-tuple-element.28), channel_id=1, source_target_pairs={{0,12},{2,14},{4,8},{6,10},{8,4},{10,6},{12,0},{14,2},{16,28},{18,... | collective-permute-start | bytes 491528 | tf_op jit(solution)/shard_map/ppermute | solution.py:229
  230.3 13.1 %collective-permute-start.6 = (bf16[40,2048]{1,0:T(8,128)(2,1)S(1)}, bf16[40,2048]{1,0:T(8,128)(2,1)S(1)}, u32[]{:S(2)}, u32[]{:S(2)}) collective-permute-start(bf16[40,2048]{1,0:T(8,128)(2,1)S(1)} %get-tuple-element.27), channel_id=1, source_target_pairs={{0,16},{2,18},{4,20},{6,22},{8,24},{10,26},{12,28},{14,30},{16,0},... | collective-permute-start | bytes 491528 | tf_op jit(solution)/shard_map/ppermute | solution.py:229
  233.0 24.0 %collective-permute-start.7 = (bf16[40,2048]{1,0:T(8,128)(2,1)S(1)}, bf16[40,2048]{1,0:T(8,128)(2,1)S(1)}, u32[]{:S(2)}, u32[]{:S(2)}) collective-permute-start(bf16[40,2048]{1,0:T(8,128)(2,1)S(1)} %get-tuple-element.26), channel_id=1, source_target_pairs={{0,20},{2,22},{4,16},{6,18},{8,28},{10,30},{12,24},{14,26},{16,4},... | collective-permute-start | bytes 491528 | tf_op jit(solution)/shard_map/ppermute | solution.py:229
  234.4 23.3 %collective-permute-start.8 = (bf16[40,2048]{1,0:T(8,128)(2,1)S(1)}, bf16[40,2048]{1,0:T(8,128)(2,1)S(1)}, u32[]{:S(2)}, u32[]{:S(2)}) collective-permute-start(bf16[40,2048]{1,0:T(8,128)(2,1)S(1)} %get-tuple-element.25), channel_id=1, source_target_pairs={{0,24},{2,26},{4,28},{6,30},{8,16},{10,18},{12,20},{14,22},{16,8},... | collective-permute-start | bytes 491528 | tf_op jit(solution)/shard_map/ppermute | solution.py:229
  241.2 17.1 %collective-permute-start.9 = (bf16[40,2048]{1,0:T(8,128)(2,1)S(1)}, bf16[40,2048]{1,0:T(8,128)(2,1)S(1)}, u32[]{:S(2)}, u32[]{:S(2)}) collective-permute-start(bf16[40,2048]{1,0:T(8,128)(2,1)S(1)} %get-tuple-element.24), channel_id=1, source_target_pairs={{0,28},{2,30},{4,24},{6,26},{8,20},{10,22},{12,16},{14,18},{16,12}... | collective-permute-start | bytes 491528 | tf_op jit(solution)/shard_map/ppermute | solution.py:229
  259.1 24.6 %collective-permute-start.10 = (bf16[320,2048]{1,0:T(8,128)(2,1)}, bf16[320,2048]{1,0:T(8,128)(2,1)S(1)}, u32[]{:S(2)}, u32[]{:S(2)}) collective-permute-start(bf16[320,2048]{1,0:T(8,128)(2,1)} %bitcast.23), channel_id=1, source_target_pairs={{0,1},{1,0},{2,3},{3,2},{4,5},{5,4},{6,7},{7,6},{8,9},{9,8},{10,11... | collective-permute-start | bytes 3932168 | tf_op jit(solution)/shard_map/ppermute | solution.py:30
  283.8 5.0 %collective-permute-start.11 = (bf16[320,4096]{1,0:T(8,128)(2,1)S(1)}, bf16[320,4096]{1,0:T(8,128)(2,1)S(1)}, u32[]{:S(2)}, u32[]{:S(2)}) collective-permute-start(bf16[320,4096]{1,0:T(8,128)(2,1)S(1)} %constant_dynamic-update-slice_fusion), channel_id=1, source_target_pairs={{0,2},{2,0},{4,6},{6,4},{8,10},{10,8},{12,14},{14,12},{16,18},{18,... | collective-permute-start | bytes 7864328 | tf_op jit(solution)/shard_map/ppermute | solution.py:347
  351.2 5.0 %collective-permute-start.12 = (bf16[320,4096]{1,0:T(8,128)(2,1)S(1)}, bf16[320,4096]{1,0:T(8,128)(2,1)S(1)}, u32[]{:S(2)}, u32[]{:S(2)}) collective-permute-start(bf16[320,4096]{1,0:T(8,128)(2,1)S(1)} %slice.193), channel_id=1, source_target_pairs={{0,2},{2,0},{4,6},{6,4},{8,10},{10,8},{12,14},{14,12},{16,18},{18,... | collective-permute-start | bytes 7864328 | tf_op jit(solution)/shard_map/ppermute | solution.py:347
  358.2 30.9 %collective-permute-start.13 = (bf16[320,2048]{1,0:T(8,128)(2,1)S(1)}, bf16[320,2048]{1,0:T(8,128)(2,1)S(1)}, u32[]{:S(2)}, u32[]{:S(2)}) collective-permute-start(bf16[320,2048]{1,0:T(8,128)(2,1)S(1)} %fusion.21), channel_id=1, source_target_pairs={{0,1},{1,0},{2,3},{3,2},{4,5},{5,4},{6,7},{7,6},{8,9},{9,8},{10,11... | collective-permute-start | bytes 3932168 | tf_op jit(solution)/shard_map/ppermute | solution.py:30
  389.9 13.7 %collective-permute-start.14 = (bf16[40,2048]{1,0:T(8,128)(2,1)S(1)}, bf16[40,2048]{1,0:T(8,128)(2,1)S(1)}, u32[]{:S(2)}, u32[]{:S(2)}) collective-permute-start(bf16[40,2048]{1,0:T(8,128)(2,1)S(1)} %get-tuple-element.23), channel_id=1, source_target_pairs={{0,4},{2,6},{4,0},{6,2},{8,12},{10,14},{12,8},{14,10},{16,20},{18,... | collective-permute-start | bytes 491528 | tf_op jit(solution)/shard_map/ppermute | solution.py:229
  391.2 16.4 %collective-permute-start.15 = (bf16[40,2048]{1,0:T(8,128)(2,1)S(1)}, bf16[40,2048]{1,0:T(8,128)(2,1)S(1)}, u32[]{:S(2)}, u32[]{:S(2)}) collective-permute-start(bf16[40,2048]{1,0:T(8,128)(2,1)S(1)} %get-tuple-element.22), channel_id=1, source_target_pairs={{0,8},{2,10},{4,12},{6,14},{8,0},{10,2},{12,4},{14,6},{16,24},{18,... | collective-permute-start | bytes 491528 | tf_op jit(solution)/shard_map/ppermute | solution.py:229
  399.2 13.9 %collective-permute-start.16 = (bf16[40,2048]{1,0:T(8,128)(2,1)S(1)}, bf16[40,2048]{1,0:T(8,128)(2,1)S(1)}, u32[]{:S(2)}, u32[]{:S(2)}) collective-permute-start(bf16[40,2048]{1,0:T(8,128)(2,1)S(1)} %get-tuple-element.21), channel_id=1, source_target_pairs={{0,12},{2,14},{4,8},{6,10},{8,4},{10,6},{12,0},{14,2},{16,28},{18,... | collective-permute-start | bytes 491528 | tf_op jit(solution)/shard_map/ppermute | solution.py:229
  400.8 22.1 %collective-permute-start.17 = (bf16[40,2048]{1,0:T(8,128)(2,1)S(1)}, bf16[40,2048]{1,0:T(8,128)(2,1)S(1)}, u32[]{:S(2)}, u32[]{:S(2)}) collective-permute-start(bf16[40,2048]{1,0:T(8,128)(2,1)S(1)} %get-tuple-element.20), channel_id=1, source_target_pairs={{0,16},{2,18},{4,20},{6,22},{8,24},{10,26},{12,28},{14,30},{16,0},... | collective-permute-start | bytes 491528 | tf_op jit(solution)/shard_map/ppermute | solution.py:229
  402.7 23.4 %collective-permute-start.18 = (bf16[40,2048]{1,0:T(8,128)(2,1)S(1)}, bf16[40,2048]{1,0:T(8,128)(2,1)S(1)}, u32[]{:S(2)}, u32[]{:S(2)}) collective-permute-start(bf16[40,2048]{1,0:T(8,128)(2,1)S(1)} %get-tuple-element.19), channel_id=1, source_target_pairs={{0,20},{2,22},{4,16},{6,18},{8,28},{10,30},{12,24},{14,26},{16,4},... | collective-permute-start | bytes 491528 | tf_op jit(solution)/shard_map/ppermute | solution.py:229
  403.6 22.5 %collective-permute-start.19 = (bf16[40,2048]{1,0:T(8,128)(2,1)S(1)}, bf16[40,2048]{1,0:T(8,128)(2,1)S(1)}, u32[]{:S(2)}, u32[]{:S(2)}) collective-permute-start(bf16[40,2048]{1,0:T(8,128)(2,1)S(1)} %get-tuple-element.18), channel_id=1, source_target_pairs={{0,24},{2,26},{4,28},{6,30},{8,16},{10,18},{12,20},{14,22},{16,8},... | collective-permute-start | bytes 491528 | tf_op jit(solution)/shard_map/ppermute | solution.py:229
  407.6 18.6 %collective-permute-start.20 = (bf16[40,2048]{1,0:T(8,128)(2,1)S(1)}, bf16[40,2048]{1,0:T(8,128)(2,1)S(1)}, u32[]{:S(2)}, u32[]{:S(2)}) collective-permute-start(bf16[40,2048]{1,0:T(8,128)(2,1)S(1)} %get-tuple-element.17), channel_id=1, source_target_pairs={{0,28},{2,30},{4,24},{6,26},{8,20},{10,22},{12,16},{14,18},{16,12}... | collective-permute-start | bytes 491528 | tf_op jit(solution)/shard_map/ppermute | solution.py:229
  413.1 14.9 %copy-start.1 = (bf16[4096,288]{0,1:T(8,128)(2,1)S(1)}, bf16[4096,288]{0,1:T(8,128)(2,1)}, u32[]{:S(2)}) copy-start(bf16[4096,288]{0,1:T(8,128)(2,1)} %param.23) | copy-start | bytes 7077892
  (11 other events, 13.3 us)
Sparse Core Ops, SparseCore 0:
  8.9 187.4 all-gather.1

commit v2 on v1

--- a/solution.py
+++ b/solution.py
@@ -221,18 +221,54 @@
     return out
 
 
-def teams_swapped(x, members):
+def across(x, mask):
+    return lax.ppermute(x, "loop", [(i, i ^ mask) for i in range(lax.axis_size("loop"))])
+
+
+def teams_swapped(x, first, members):
     groups = lax.axis_size("loop")
-    out = [x[0]]
-    for s in range(1, x.shape[0]):
-        out.append(
-            lax.ppermute(
-                x[s],
-                "loop",
-                [(i, ((i // members) ^ s) * members + i % members) for i in range(groups)],
+    out = []
+    for k in range(x.shape[0]):
+        s = first + k
+        if s == 0:
+            out.append(x[k])
+            continue
+        pairs = [(i, ((i // members) ^ s) * members + i % members) for i in range(groups)]
+        out.append(lax.ppermute(x[k], "loop", pairs))
+    return jnp.concatenate(out, axis=0)
+
+
+def hidden_kernel(low_ref, gather_ref, residual_ref, *refs):
+    pieces, (hidden_ref, packed_ref) = refs[:-2], refs[-2:]
+    for m, piece_ref in enumerate(pieces):
+        block = piece_ref.shape[1] // 2
+        for dc in range(2):
+            place = low_ref[0] ^ (2 * m + dc)
+            cols = pl.ds(pl.multiple_of(place * block, block), block)
+            mixed = piece_ref[:, dc * block : (dc + 1) * block].astype(jnp.float32)
+            hidden_ref[:, cols] = (residual_ref[:, cols].astype(jnp.float32) + mixed).astype(
+                hidden_ref.dtype
             )
-        )
-    return jnp.stack(out)
+    packed_ref[...] = jnp.dot(
+        gather_ref[...], hidden_ref[...], preferred_element_type=jnp.float32
+    ).astype(packed_ref.dtype)
+
+
+def hidden_and_packed(low, gather_matrix, residual_in, pieces):
+    vmem = pl.BlockSpec(memory_space=pltpu.VMEM)
+    return pl.pallas_call(
+        hidden_kernel,
+        in_specs=[pl.BlockSpec(memory_space=pltpu.SMEM)] + [vmem] * (2 + len(pieces)),
+        out_specs=[vmem, vmem],
+        out_shape=[
+            jax.ShapeDtypeStruct(residual_in.shape, jnp.bfloat16),
+            jax.ShapeDtypeStruct(
+                (gather_matrix.shape[0], residual_in.shape[1]), jnp.bfloat16
+            ),
+        ],
+        compiler_params=pltpu.CompilerParams(vmem_limit_bytes=VMEM),
+        name="hidden_and_packed",
+    )(low, gather_matrix, residual_in, *pieces)
 
 
 def per_device(
@@ -261,6 +297,14 @@
     position = lax.axis_index("loop")
     shard = lax.axis_index("tp")
     shards = lax.axis_size("tp")
+    low = groups // shards
+    own_columns = lax.all_gather(
+        out_proj,
+        "loop",
+        axis=1,
+        tiled=True,
+        axis_index_groups=[[i + low * high for high in range(shards)] for i in range(low)],
+    )
     conv_taps = conv_weight.shape[0]
     rim_rows = shifted(mixer_in[tokens - (conv_taps - 1) :], "loop", 1)
     extended = jnp.concatenate([rim_rows, mixer_in], axis=0)
@@ -305,19 +349,29 @@
     gated = scan_gated(
         step_size, decay_rate, conved, gain, kept, carry, pick, skip_gain, gate_in
     )
-    partial_mix = jnp.dot(
-        gated,
-        lax.all_gather(out_proj, "loop", axis=1, tiled=True),
-        preferred_element_type=jnp.float32,
-    )
-    features = partial_mix.shape[1]
-    width = features // shards
-    mixed_out = scattered_sum(
-        jnp.stack([partial_mix[:, k * width : (k + 1) * width] for k in range(shards)]),
-        "tp",
-        shard,
-    )
-    hidden_in = (residual_in.astype(jnp.float32) + mixed_out).astype(jnp.bfloat16)
+    own_low = position % low
+    tokens_of = [gated] + [across(gated, m) for m in range(2, low, 2)]
+    own_columns, tokens_of = lax.optimization_barrier((own_columns, tokens_of))
+    other_columns = across(own_columns, 1)
+    all_tokens = jnp.concatenate(tokens_of, axis=0)
+    block = out_proj.shape[1]
+    halves = [
+        jnp.dot(all_tokens, columns, preferred_element_type=jnp.float32)
+        for columns in (own_columns, other_columns)
+    ]
+    for_shard = lambda t: jnp.concatenate(
+        [lax.dynamic_slice_in_dim(part, t * block, block, 1) for part in halves], axis=1
+    )
+    mixed_out = for_shard(shard)
+    for by in range(1, shards):
+        sent = for_shard((shard + by) % shards).astype(jnp.bfloat16)
+        mixed_out = mixed_out + rotated(sent, "tp", by).astype(jnp.float32)
+    pieces = [mixed_out[:tokens]]
+    for k in range(1, len(tokens_of)):
+        rows_out = mixed_out[k * tokens : (k + 1) * tokens].astype(jnp.bfloat16)
+        pieces.append(across(rows_out, 2 * k))
+    width = residual_in.shape[1]
+    features = width * shards
 
     members = groups // EXPERTS
     team, member = position // members, position % members
@@ -333,10 +387,10 @@
     keep_weight = jnp.sum(onehot.astype(jnp.float32) * keep_mask.astype(jnp.float32), axis=1)
     weights = route_weight.reshape(-1) * keep_weight
     weighted = jnp.sum((selector * weights[None, :]).reshape(EXPERTS * CAP, tokens, TOPK), axis=2)
-    packed = jnp.dot(
-        gather_matrix.astype(jnp.bfloat16), hidden_in, preferred_element_type=jnp.float32
-    ).astype(jnp.bfloat16)
-    arrived = teams_swapped(packed.reshape(EXPERTS, CAP, width), members)
+    hidden_in, packed = hidden_and_packed(
+        own_low.astype(jnp.int32)[None], gather_matrix.astype(jnp.bfloat16), residual_in, pieces
+    )
+    arrived = teams_swapped(packed.reshape(EXPERTS, CAP, width), 0, members)
     rows = EXPERTS * CAP
     arrived = gathered(arrived.reshape(rows, width), "tp", shard, 1)
 
@@ -364,7 +418,7 @@
         shard,
     )
     returned = teams_swapped(
-        shares.astype(jnp.bfloat16).reshape(EXPERTS, CAP, width), members
+        shares.astype(jnp.bfloat16).reshape(EXPERTS, CAP, width), 0, members
     ).reshape(rows, width)
     expert_sum = jnp.dot(
         weighted.T,

time: 438 us -> 425 us (0.970)
  waiting for transfers between devices: 229 us -> 205 us
  starting transfers between devices: 49.7 us -> 59.3 us
  matrix products: 80.2 us -> 73.6 us
  other arithmetic: 10.3 us -> 16.2 us
    all_gather x1, waiting for transfers between devices: 95.2 us -> 0.01 us  [per_device(): lax.all_gather(out_proj, 'loop', axis=1, tiled=True, axis_index_groups=[[...]
    ppermute x14 -> x21, waiting for transfers between devices: 31.8 us -> 96.8 us  [the longest x7 61 us: across(): lax.ppermute(x, 'loop', [(i, i ^ mask) for i in range(lax.axis_size('loop...]
    all_to_all x1, waiting for transfers between devices: 13.5 us -> 27.2 us  [per_device(): ends = lax.all_to_all(end_state, 'loop', 0, 0, tiled=True)]
    dot_general x2, matrix products: 13.4 us -> 6.83 us  [per_device(): jnp.dot(all_tokens, columns, preferred_element_type=jnp.float32)]
    ppermute x4, waiting for transfers between devices: 69.2 us -> 63.2 us  [rotated(): return lax.ppermute(x, axis, [(i, (i + by) % size) for i in range(size)])]
    ppermute x14 -> x21, starting transfers between devices: 31.9 us -> 37.7 us  [the longest x14 30.5 us: teams_swapped(): out.append(lax.ppermute(x[k], 'loop', pairs))]
    unnamed x53 -> x56, local copies, waits for them, and re-layouts: 14.9 us -> 13 us
  transfers between devices with their start and end apart: 24 -> 31, of which waited for: 14 -> 22; matrix products, arithmetic and copies ran while one was open for 5% -> 5% of each run, Pallas kernels for 6% -> 6%
where the time goes in v2:
time: 425 us; the launch traced here: 422 us
  waiting for transfers between devices  205 us (48%)
  matrix products  73.6 us (17%)
  starting transfers between devices  59.3 us (14%)
  Pallas kernels  26.8 us (6%)
  local copies, waits for them, and re-layouts  26.3 us (6%)
  other arithmetic  16.2 us (4%)
  between operations  14.6 us (3%)
    ppermute x4, waiting for transfers between devices, rotated(): return lax.ppermute(x, axis, [(i, (i + by) % size) for i in range(size)])  63.2 us
    ppermute x7, waiting for transfers between devices, across(): lax.ppermute(x, 'loop', [(i, i ^ mask) for i in range(lax.axis_size('loop...  61 us
    ppermute x14, waiting for transfers between devices, teams_swapped(): out.append(lax.ppermute(x[k], 'loop', pairs))  35.8 us
    ppermute x14, starting transfers between devices, teams_swapped(): out.append(lax.ppermute(x[k], 'loop', pairs))  30.5 us
    all_to_all x1, waiting for transfers between devices, per_device(): ends = lax.all_to_all(end_state, 'loop', 0, 0, tiled=True)  27.2 us
    dot_general x1, matrix products, per_device(): jnp.dot(slot_rows, up_weight[0], preferred_element_type=jnp.float32)  21.4 us
    dot_general x1, matrix products, per_device(): jnp.dot(slot_rows, gate_weight[0], preferred_element_type=jnp.float32)  21 us
    dot_general x1, matrix products, per_device(): jnp.dot(hidden, down_weight[0], preferred_element_type=jnp.float32)  19.7 us
  transfers between devices with their start and end apart: 31, of which 22 were waited for; matrix products, arithmetic and copies ran while one was open for 5% of the time, Pallas kernels for 6%

profile of v2, /device:TPU:0, one launch (start us, length us, event | category | flops | bytes accessed | tf_op | source)
XLA Modules:
  0.0 421.5 jit_solution(15153192623739248092)
XLA Ops:
  8.1 2.4 collective-permute-start
  11.6 3.9 multiply_convert_fusion.2.conved_ref
  28.3 11.2 %scan_end.1 = (f32[128,4096]{1,0:T(8,128)S(1)}, bf16[16,32,256]{2,1,0:T(8,128)(2,1)}) custom-call(bf16[128,256]{1,0:T(8,128)(2,1)S(1)} %slice.184.low_ref, bf16[256,4096]{1,0:T(8,128)(2,1)S(1)} %copy-done.5, f32[1,4096]{1,0:T(1,128)S(1)} %bitcast.60, f32[16,4096]{1,0:T(8,128)S(1)} %copy-done.3, bf16[128,4096]{1,0:T(8,128)(2,1)S(1)} %multiply_convert_fusion.2.conved_ref, ...), custom_call_target="tpu_custom_call" | custom-call | flops 41943040 | bytes 4194304 | tf_op jit(solution)/shard_map/scan_end/pallas_call | solution.py:125
  40.9 7.8 %all-to-all-start = ((bf16[16,32,256]{2,1,0:T(8,128)(2,1)}), bf16[16,32,256]{2,1,0:T(8,128)(2,1)S(1)}, u32[]{:S(2)}, u32[]{:S(2)}) async-start(bf16[16,32,256]{2,1,0:T(8,128)(2,1)} %get-tuple-element.15), calls=%async_computation | async-start | bytes 524288 | tf_op jit(solution)/shard_map/all_to_all | solution.py:345
  50.0 27.2 %all-to-all-done.ends_ref = bf16[16,32,256]{2,1,0:T(8,128)(2,1)S(1)} async-done(((bf16[16,32,256]{2,1,0:T(8,128)(2,1)}), bf16[16,32,256]{2,1,0:T(8,128)(2,1)S(1)}, u32[]{:S(2)}, u32[]{:S(2)}) %all-to-all-start) | async-done | bytes 262176 | tf_op jit(solution)/shard_map/all_to_all | solution.py:345
  79.6 4.1 all-to-all-start.1
  84.8 6.8 %all-to-all-done.1.carry_ref = bf16[16,16,256]{2,1,0:T(8,128)(2,1)S(1)} async-done(((bf16[16,16,256]{2,1,0:T(8,128)(2,1)}), bf16[16,16,256]{2,1,0:T(8,128)(2,1)S(1)}, u32[]{:S(2)}, u32[]{:S(2)}) %all-to-all-start.1) | async-done | bytes 131104 | tf_op jit(solution)/shard_map/all_to_all | solution.py:348
  96.4 13.3 %scan_gated.1 = bf16[128,4096]{1,0:T(8,128)(2,1)S(1)} custom-call(f32[128,4096]{1,0:T(8,128)S(1)} %copy-done.11, f32[16,4096]{1,0:T(8,128)S(1)} %copy-done.4, bf16[128,4096]{1,0:T(8,128)(2,1)S(1)} %multiply_convert_fusion.2.conved_ref, f32[128,16,128]{2,1,0:T(8,128)S(1)} %broadcast_in_dim.44.gain_ref, f32[128,1]{1,0:T(8,128)S(1)} %copy.60.kept_ref, ...), custom_call_target="tpu_custom_call" | custom-call | flops 58720256 | bytes 6291456 | tf_op jit(solution)/shard_map/scan_gated/pallas_call | solution.py:168
  113.3 22.0 %collective-permute-done.2 = bf16[128,4096]{1,0:T(8,128)(2,1)S(1)} collective-permute-done((bf16[128,4096]{1,0:T(8,128)(2,1)S(1)}, bf16[128,4096]{1,0:T(8,128)(2,1)S(1)}, u32[]{:S(2)}, u32[]{:S(2)}) %collective-permute-start.2) | collective-permute-done | bytes 1048608 | tf_op jit(solution)/shard_map/ppermute | solution.py:225
  135.3 9.6 %collective-permute-done.3 = bf16[128,4096]{1,0:T(8,128)(2,1)S(1)} collective-permute-done((bf16[128,4096]{1,0:T(8,128)(2,1)S(1)}, bf16[128,4096]{1,0:T(8,128)(2,1)S(1)}, u32[]{:S(2)}, u32[]{:S(2)}) %collective-permute-start.3) | collective-permute-done | bytes 1048608 | tf_op jit(solution)/shard_map/ppermute | solution.py:225
  144.9 23.4 %collective-permute-done.4 = bf16[128,4096]{1,0:T(8,128)(2,1)} collective-permute-done((bf16[128,4096]{1,0:T(8,128)(2,1)S(1)}, bf16[128,4096]{1,0:T(8,128)(2,1)}, u32[]{:S(2)}, u32[]{:S(2)}) %collective-permute-start.4) | collective-permute-done | bytes 1048608 | tf_op jit(solution)/shard_map/ppermute | solution.py:225
  175.9 4.5 %fusion.48 = f32[512,512]{1,0:T(8,128)S(1)} fusion(bf16[512,4096]{1,0:T(8,128)(2,1)S(1)} %constant_dynamic-update-slice_fusion, bf16[4096,512]{1,0:T(8,128)(2,1)} %collective-permute-done.5), kind=kOutput, calls=%fused_computation.103 | convolution fusion | flops 2147483648 | bytes 9437184 | tf_op jit(solution)/shard_map/dot_general | solution.py:359
  183.1 12.5 %collective-permute-done.6 = bf16[512,512]{1,0:T(8,128)(2,1)} collective-permute-done((bf16[512,512]{1,0:T(8,128)(2,1)}, bf16[512,512]{1,0:T(8,128)(2,1)}, u32[]{:S(2)}, u32[]{:S(2)}) %collective-permute-start.6) | collective-permute-done | bytes 524320 | tf_op jit(solution)/shard_map/ppermute | solution.py:30
  197.5 2.9 collective-permute-start.9
  210.2 2.7 collective-permute-start.14
  215.3 3.8 collective-permute-start.16
  220.1 10.4 %collective-permute-done.13 = bf16[40,2048]{1,0:T(8,128)(2,1)S(1)} collective-permute-done((bf16[40,2048]{1,0:T(8,128)(2,1)S(1)}, bf16[40,2048]{1,0:T(8,128)(2,1)S(1)}, u32[]{:S(2)}, u32[]{:S(2)}) %collective-permute-start.13) | collective-permute-done | bytes 163872 | tf_op jit(solution)/shard_map/ppermute | solution.py:237
  230.5 3.8 collective-permute-done.14
  236.5 20.3 %collective-permute-done.17 = bf16[320,2048]{1,0:T(8,128)(2,1)} collective-permute-done((bf16[320,2048]{1,0:T(8,128)(2,1)S(1)}, bf16[320,2048]{1,0:T(8,128)(2,1)}, u32[]{:S(2)}, u32[]{:S(2)}) %collective-permute-start.17) | collective-permute-done | bytes 1310752 | tf_op jit(solution)/shard_map/ppermute | solution.py:30
  258.3 4.9 %collective-permute-done.18 = bf16[320,4096]{1,0:T(8,128)(2,1)S(1)} collective-permute-done((bf16[320,4096]{1,0:T(8,128)(2,1)S(1)}, bf16[320,4096]{1,0:T(8,128)(2,1)S(1)}, u32[]{:S(2)}, u32[]{:S(2)}) %collective-permute-start.18) | collective-permute-done | bytes 2621472 | tf_op jit(solution)/shard_map/ppermute | solution.py:401
  263.2 21.0 %fusion.4 = f32[640,3072]{1,0:T(8,128)} fusion(bf16[1,4096,3072]{2,1,0:T(8,128)(2,1)} %param.30, bf16[320,4096]{1,0:T(8,128)(2,1)S(1)} %collective-permute-done.18, bf16[320,4096]{1,0:T(8,128)(2,1)S(1)} %constant_dynamic-update-slice_fusion.18), kind=kOutput, calls=%fused_computation.4 | convolution fusion | flops 16116613120 | bytes 38273024 | tf_op jit(solution)/shard_map/dot_general | solution.py:406
  284.2 21.4 %multiply_convert_fusion.5 = bf16[640,3072]{1,0:T(8,128)(2,1)S(1)} fusion(f32[640,3072]{1,0:T(8,128)} %fusion.4, bf16[1,4096,3072]{2,1,0:T(8,128)(2,1)} %param.31, bf16[320,4096]{1,0:T(8,128)(2,1)S(1)} %collective-permute-done.18, bf16[320,4096]{1,0:T(8,128)(2,1)S(1)} %constant_dynamic-update-slice_fusion.18), kind=kOutput, calls=%fused_computation.6.clone.clone.1 | convolution fusion | flops 16128409600 | bytes 42205184 | tf_op jit(solution)/shard_map/dot_general | solution.py:407
  305.6 19.7 %fusion.6 = bf16[640,4096]{1,0:T(8,128)(2,1)S(1)} fusion(bf16[1,3072,4096]{2,1,0:T(8,128)(2,1)} %param.32, bf16[640,3072]{1,0:T(8,128)(2,1)S(1)} %multiply_convert_fusion.5), kind=kOutput, calls=%fused_computation.7 | convolution fusion | flops 16108748800 | bytes 34340864 | tf_op jit(solution)/shard_map/dot_general | solution.py:409
  328.7 5.1 %collective-permute-done.19 = bf16[320,4096]{1,0:T(8,128)(2,1)} collective-permute-done((bf16[320,4096]{1,0:T(8,128)(2,1)}, bf16[320,4096]{1,0:T(8,128)(2,1)}, u32[]{:S(2)}, u32[]{:S(2)}) %collective-permute-start.19) | collective-permute-done | bytes 2621472 | tf_op jit(solution)/shard_map/ppermute | solution.py:401
  333.8 3.5 convert_add_fusion
  342.3 29.3 %collective-permute-done.20 = bf16[320,2048]{1,0:T(8,128)(2,1)S(1)} collective-permute-done((bf16[320,2048]{1,0:T(8,128)(2,1)}, bf16[320,2048]{1,0:T(8,128)(2,1)S(1)}, u32[]{:S(2)}, u32[]{:S(2)}) %collective-permute-start.20) | collective-permute-done | bytes 1310752 | tf_op jit(solution)/shard_map/ppermute | solution.py:30
  371.7 2.4 fusion.19
  374.2 4.5 %collective-permute-start.21 = (bf16[40,2048]{1,0:T(8,128)(2,1)S(1)}, bf16[40,2048]{1,0:T(8,128)(2,1)S(1)}, u32[]{:S(2)}, u32[]{:S(2)}) collective-permute-start(bf16[40,2048]{1,0:T(8,128)(2,1)S(1)} %get-tuple-element.37), channel_id=1, source_target_pairs={{0,4},{2,6},{4,0},{6,2},{8,12},{10,14},{12,8},{14,10},{16,20},{18,... | collective-permute-start | bytes 491528 | tf_op jit(solution)/shard_map/ppermute | solution.py:237
  378.8 7.5 %collective-permute-start.22 = (bf16[40,2048]{1,0:T(8,128)(2,1)S(1)}, bf16[40,2048]{1,0:T(8,128)(2,1)S(1)}, u32[]{:S(2)}, u32[]{:S(2)}) collective-permute-start(bf16[40,2048]{1,0:T(8,128)(2,1)S(1)} %get-tuple-element.36), channel_id=1, source_target_pairs={{0,8},{2,10},{4,12},{6,14},{8,0},{10,2},{12,4},{14,6},{16,24},{18,... | collective-permute-start | bytes 491528 | tf_op jit(solution)/shard_map/ppermute | solution.py:237
  391.6 4.8 %collective-permute-done.22 = bf16[40,2048]{1,0:T(8,128)(2,1)S(1)} collective-permute-done((bf16[40,2048]{1,0:T(8,128)(2,1)S(1)}, bf16[40,2048]{1,0:T(8,128)(2,1)S(1)}, u32[]{:S(2)}, u32[]{:S(2)}) %collective-permute-start.22) | collective-permute-done | bytes 163872 | tf_op jit(solution)/shard_map/ppermute | solution.py:237
  398.1 10.2 %collective-permute-done.24 = bf16[40,2048]{1,0:T(8,128)(2,1)S(1)} collective-permute-done((bf16[40,2048]{1,0:T(8,128)(2,1)S(1)}, bf16[40,2048]{1,0:T(8,128)(2,1)S(1)}, u32[]{:S(2)}, u32[]{:S(2)}) %collective-permute-start.24) | collective-permute-done | bytes 163872 | tf_op jit(solution)/shard_map/ppermute | solution.py:237
  408.4 4.4 %collective-permute-done.25 = bf16[40,2048]{1,0:T(8,128)(2,1)S(1)} collective-permute-done((bf16[40,2048]{1,0:T(8,128)(2,1)S(1)}, bf16[40,2048]{1,0:T(8,128)(2,1)S(1)}, u32[]{:S(2)}, u32[]{:S(2)}) %collective-permute-start.25) | collective-permute-done | bytes 163872 | tf_op jit(solution)/shard_map/ppermute | solution.py:237
  (151 shorter events, 75.6 us)
Async XLA Ops:
  6.5 161.8 %all-gather.2.cloned.1.call-start = ((), (), s32[]{:S(2)}) async-start(), calls=%async_computation.2 | async-start | bytes 6291456 | tf_op jit(solution)/shard_map/all_gather | solution.py:301
  8.1 3.4 collective-permute-start
  17.2 7.2 %collective-permute-start.1 = (f32[128,288]{1,0:T(8,128)}, f32[128,288]{1,0:T(8,128)S(1)}, u32[]{:S(2)}, u32[]{:S(2)}) collective-permute-start(f32[128,288]{1,0:T(8,128)} %fusion.46), channel_id=1, source_target_pairs={{0,1},{1,0},{2,3},{3,2},{4,5},{5,4},{6,7},{7,6},{8,9},{9,8},{10,11... | collective-permute-start | bytes 442376 | tf_op jit(solution)/shard_map/ppermute | solution.py:30
  40.9 36.4 %all-to-all-start = ((bf16[16,32,256]{2,1,0:T(8,128)(2,1)}), bf16[16,32,256]{2,1,0:T(8,128)(2,1)S(1)}, u32[]{:S(2)}, u32[]{:S(2)}) async-start(bf16[16,32,256]{2,1,0:T(8,128)(2,1)} %get-tuple-element.15), calls=%async_computation | async-start | bytes 524288 | tf_op jit(solution)/shard_map/all_to_all | solution.py:345
  79.6 12.0 %all-to-all-start.1 = ((bf16[16,16,256]{2,1,0:T(8,128)(2,1)}), bf16[16,16,256]{2,1,0:T(8,128)(2,1)S(1)}, u32[]{:S(2)}, u32[]{:S(2)}) async-start(bf16[16,16,256]{2,1,0:T(8,128)(2,1)} %carries.1), calls=%async_computation.1 | async-start | bytes 262144 | tf_op jit(solution)/shard_map/all_to_all | solution.py:348
  96.4 72.0 %copy-start.16 = (s32[128,2]{0,1:T(2,128)S(1)}, s32[128,2]{0,1:T(2,128)}, u32[]{:S(2)}) copy-start(s32[128,2]{0,1:T(2,128)} %param.33) | copy-start | bytes 3076
  109.7 25.6 %collective-permute-start.2 = (bf16[128,4096]{1,0:T(8,128)(2,1)S(1)}, bf16[128,4096]{1,0:T(8,128)(2,1)S(1)}, u32[]{:S(2)}, u32[]{:S(2)}) collective-permute-start(bf16[128,4096]{1,0:T(8,128)(2,1)S(1)} %scan_gated.1), channel_id=1, source_target_pairs={{0,4},{2,6},{4,0},{6,2},{8,12},{10,14},{12,8},{14,10},{16,20},{18,... | collective-permute-start | bytes 3145736 | tf_op jit(solution)/shard_map/ppermute | solution.py:225
  110.7 34.3 %collective-permute-start.3 = (bf16[128,4096]{1,0:T(8,128)(2,1)S(1)}, bf16[128,4096]{1,0:T(8,128)(2,1)S(1)}, u32[]{:S(2)}, u32[]{:S(2)}) collective-permute-start(bf16[128,4096]{1,0:T(8,128)(2,1)S(1)} %scan_gated.1), channel_id=1, source_target_pairs={{0,8},{2,10},{4,12},{6,14},{8,0},{10,2},{12,4},{14,6},{16,24},{18,... | collective-permute-start | bytes 3145736 | tf_op jit(solution)/shard_map/ppermute | solution.py:225
  111.9 56.5 %collective-permute-start.4 = (bf16[128,4096]{1,0:T(8,128)(2,1)S(1)}, bf16[128,4096]{1,0:T(8,128)(2,1)}, u32[]{:S(2)}, u32[]{:S(2)}) collective-permute-start(bf16[128,4096]{1,0:T(8,128)(2,1)S(1)} %scan_gated.1), channel_id=1, source_target_pairs={{0,12},{2,14},{4,8},{6,10},{8,4},{10,6},{12,0},{14,2},{16,28},{18,... | collective-permute-start | bytes 3145736 | tf_op jit(solution)/shard_map/ppermute | solution.py:225
  168.4 7.5 %collective-permute-start.5 = (bf16[4096,512]{1,0:T(8,128)(2,1)}, bf16[4096,512]{1,0:T(8,128)(2,1)}, u32[]{:S(2)}, u32[]{:S(2)}) collective-permute-start(bf16[4096,512]{1,0:T(8,128)(2,1)} %all-gather.2.cloned.1.call-done), channel_id=1, source_target_pairs={{0,2},{2,0},{4,6},{6,4},{8,10},{10,8},{12,14},{14,12},{16,18},{18,... | collective-permute-start | bytes 12582920 | tf_op jit(solution)/shard_map/ppermute | solution.py:225
  181.3 14.3 %collective-permute-start.6 = (bf16[512,512]{1,0:T(8,128)(2,1)}, bf16[512,512]{1,0:T(8,128)(2,1)}, u32[]{:S(2)}, u32[]{:S(2)}) collective-permute-start(bf16[512,512]{1,0:T(8,128)(2,1)} %pad_maximum_fusion.5), channel_id=1, source_target_pairs={{0,1},{1,0},{2,3},{3,2},{4,5},{5,4},{6,7},{7,6},{8,9},{9,8},{10,11... | collective-permute-start | bytes 1572872 | tf_op jit(solution)/shard_map/ppermute | solution.py:30
  196.8 6.1 %collective-permute-start.7 = (bf16[128,512]{1,0:T(8,128)(2,1)S(1)}, bf16[128,512]{1,0:T(8,128)(2,1)S(1)}, u32[]{:S(2)}, u32[]{:S(2)}) collective-permute-start(bf16[128,512]{1,0:T(8,128)(2,1)S(1)} %get-tuple-element.49), channel_id=1, source_target_pairs={{0,4},{2,6},{4,0},{6,2},{8,12},{10,14},{12,8},{14,10},{16,20},{18,... | collective-permute-start | bytes 393224 | tf_op jit(solution)/shard_map/ppermute | solution.py:225
  197.5 5.8 %collective-permute-start.8 = (bf16[128,512]{1,0:T(8,128)(2,1)S(1)}, bf16[128,512]{1,0:T(8,128)(2,1)S(1)}, u32[]{:S(2)}, u32[]{:S(2)}) collective-permute-start(bf16[128,512]{1,0:T(8,128)(2,1)S(1)} %get-tuple-element.48), channel_id=1, source_target_pairs={{0,8},{2,10},{4,12},{6,14},{8,0},{10,2},{12,4},{14,6},{16,24},{18,... | collective-permute-start | bytes 393224 | tf_op jit(solution)/shard_map/ppermute | solution.py:225
  197.5 8.1 %collective-permute-start.9 = (bf16[128,512]{1,0:T(8,128)(2,1)S(1)}, bf16[128,512]{1,0:T(8,128)(2,1)S(1)}, u32[]{:S(2)}, u32[]{:S(2)}) collective-permute-start(bf16[128,512]{1,0:T(8,128)(2,1)S(1)} %get-tuple-element.47), channel_id=1, source_target_pairs={{0,12},{2,14},{4,8},{6,10},{8,4},{10,6},{12,0},{14,2},{16,28},{18,... | collective-permute-start | bytes 393224 | tf_op jit(solution)/shard_map/ppermute | solution.py:225
  206.4 6.5 %collective-permute-start.10 = (bf16[40,2048]{1,0:T(8,128)(2,1)S(1)}, bf16[40,2048]{1,0:T(8,128)(2,1)S(1)}, u32[]{:S(2)}, u32[]{:S(2)}) collective-permute-start(bf16[40,2048]{1,0:T(8,128)(2,1)S(1)} %get-tuple-element.45), channel_id=1, source_target_pairs={{0,4},{2,6},{4,0},{6,2},{8,12},{10,14},{12,8},{14,10},{16,20},{18,... | collective-permute-start | bytes 491528 | tf_op jit(solution)/shard_map/ppermute | solution.py:237
  207.0 8.3 %collective-permute-start.11 = (bf16[40,2048]{1,0:T(8,128)(2,1)S(1)}, bf16[40,2048]{1,0:T(8,128)(2,1)S(1)}, u32[]{:S(2)}, u32[]{:S(2)}) collective-permute-start(bf16[40,2048]{1,0:T(8,128)(2,1)S(1)} %get-tuple-element.44), channel_id=1, source_target_pairs={{0,8},{2,10},{4,12},{6,14},{8,0},{10,2},{12,4},{14,6},{16,24},{18,... | collective-permute-start | bytes 491528 | tf_op jit(solution)/shard_map/ppermute | solution.py:237
  207.7 12.4 %collective-permute-start.12 = (bf16[40,2048]{1,0:T(8,128)(2,1)S(1)}, bf16[40,2048]{1,0:T(8,128)(2,1)S(1)}, u32[]{:S(2)}, u32[]{:S(2)}) collective-permute-start(bf16[40,2048]{1,0:T(8,128)(2,1)S(1)} %get-tuple-element.43), channel_id=1, source_target_pairs={{0,12},{2,14},{4,8},{6,10},{8,4},{10,6},{12,0},{14,2},{16,28},{18,... | collective-permute-start | bytes 491528 | tf_op jit(solution)/shard_map/ppermute | solution.py:237
  209.9 20.5 %collective-permute-start.13 = (bf16[40,2048]{1,0:T(8,128)(2,1)S(1)}, bf16[40,2048]{1,0:T(8,128)(2,1)S(1)}, u32[]{:S(2)}, u32[]{:S(2)}) collective-permute-start(bf16[40,2048]{1,0:T(8,128)(2,1)S(1)} %get-tuple-element.42), channel_id=1, source_target_pairs={{0,16},{2,18},{4,20},{6,22},{8,24},{10,26},{12,28},{14,30},{16,0},... | collective-permute-start | bytes 491528 | tf_op jit(solution)/shard_map/ppermute | solution.py:237
  210.2 24.1 %collective-permute-start.14 = (bf16[40,2048]{1,0:T(8,128)(2,1)S(1)}, bf16[40,2048]{1,0:T(8,128)(2,1)S(1)}, u32[]{:S(2)}, u32[]{:S(2)}) collective-permute-start(bf16[40,2048]{1,0:T(8,128)(2,1)S(1)} %get-tuple-element.41), channel_id=1, source_target_pairs={{0,20},{2,22},{4,16},{6,18},{8,28},{10,30},{12,24},{14,26},{16,4},... | collective-permute-start | bytes 491528 | tf_op jit(solution)/shard_map/ppermute | solution.py:237
  212.9 21.4 %collective-permute-start.15 = (bf16[40,2048]{1,0:T(8,128)(2,1)S(1)}, bf16[40,2048]{1,0:T(8,128)(2,1)S(1)}, u32[]{:S(2)}, u32[]{:S(2)}) collective-permute-start(bf16[40,2048]{1,0:T(8,128)(2,1)S(1)} %get-tuple-element.40), channel_id=1, source_target_pairs={{0,24},{2,26},{4,28},{6,30},{8,16},{10,18},{12,20},{14,22},{16,8},... | collective-permute-start | bytes 491528 | tf_op jit(solution)/shard_map/ppermute | solution.py:237
  215.3 19.0 %collective-permute-start.16 = (bf16[40,2048]{1,0:T(8,128)(2,1)S(1)}, bf16[40,2048]{1,0:T(8,128)(2,1)S(1)}, u32[]{:S(2)}, u32[]{:S(2)}) collective-permute-start(bf16[40,2048]{1,0:T(8,128)(2,1)S(1)} %get-tuple-element.39), channel_id=1, source_target_pairs={{0,28},{2,30},{4,24},{6,26},{8,20},{10,22},{12,16},{14,18},{16,12}... | collective-permute-start | bytes 491528 | tf_op jit(solution)/shard_map/ppermute | solution.py:237
  234.4 22.4 %collective-permute-start.17 = (bf16[320,2048]{1,0:T(8,128)(2,1)S(1)}, bf16[320,2048]{1,0:T(8,128)(2,1)}, u32[]{:S(2)}, u32[]{:S(2)}) collective-permute-start(bf16[320,2048]{1,0:T(8,128)(2,1)S(1)} %constant_dynamic-update-slice_fusion.4), channel_id=1, source_target_pairs={{0,1},{1,0},{2,3},{3,2},{4,5},{5,4},{6,7},{7,6},{8,9},{9,8},{10,11... | collective-permute-start | bytes 3932168 | tf_op jit(solution)/shard_map/ppermute | solution.py:30
  258.2 5.0 %collective-permute-start.18 = (bf16[320,4096]{1,0:T(8,128)(2,1)S(1)}, bf16[320,4096]{1,0:T(8,128)(2,1)S(1)}, u32[]{:S(2)}, u32[]{:S(2)}) collective-permute-start(bf16[320,4096]{1,0:T(8,128)(2,1)S(1)} %constant_dynamic-update-slice_fusion.18), channel_id=1, source_target_pairs={{0,2},{2,0},{4,6},{6,4},{8,10},{10,8},{12,14},{14,12},{16,18},{18,... | collective-permute-start | bytes 7864328 | tf_op jit(solution)/shard_map/ppermute | solution.py:401
  328.6 5.3 %collective-permute-start.19 = (bf16[320,4096]{1,0:T(8,128)(2,1)}, bf16[320,4096]{1,0:T(8,128)(2,1)}, u32[]{:S(2)}, u32[]{:S(2)}) collective-permute-start(bf16[320,4096]{1,0:T(8,128)(2,1)} %slice.192), channel_id=1, source_target_pairs={{0,2},{2,0},{4,6},{6,4},{8,10},{10,8},{12,14},{14,12},{16,18},{18,... | collective-permute-start | bytes 7864328 | tf_op jit(solution)/shard_map/ppermute | solution.py:401
  340.6 31.0 %collective-permute-start.20 = (bf16[320,2048]{1,0:T(8,128)(2,1)}, bf16[320,2048]{1,0:T(8,128)(2,1)S(1)}, u32[]{:S(2)}, u32[]{:S(2)}) collective-permute-start(bf16[320,2048]{1,0:T(8,128)(2,1)} %fusion.21), channel_id=1, source_target_pairs={{0,1},{1,0},{2,3},{3,2},{4,5},{5,4},{6,7},{7,6},{8,9},{9,8},{10,11... | collective-permute-start | bytes 3932168 | tf_op jit(solution)/shard_map/ppermute | solution.py:30
  374.2 15.9 %collective-permute-start.21 = (bf16[40,2048]{1,0:T(8,128)(2,1)S(1)}, bf16[40,2048]{1,0:T(8,128)(2,1)S(1)}, u32[]{:S(2)}, u32[]{:S(2)}) collective-permute-start(bf16[40,2048]{1,0:T(8,128)(2,1)S(1)} %get-tuple-element.37), channel_id=1, source_target_pairs={{0,4},{2,6},{4,0},{6,2},{8,12},{10,14},{12,8},{14,10},{16,20},{18,... | collective-permute-start | bytes 491528 | tf_op jit(solution)/shard_map/ppermute | solution.py:237
  378.8 17.6 %collective-permute-start.22 = (bf16[40,2048]{1,0:T(8,128)(2,1)S(1)}, bf16[40,2048]{1,0:T(8,128)(2,1)S(1)}, u32[]{:S(2)}, u32[]{:S(2)}) collective-permute-start(bf16[40,2048]{1,0:T(8,128)(2,1)S(1)} %get-tuple-element.36), channel_id=1, source_target_pairs={{0,8},{2,10},{4,12},{6,14},{8,0},{10,2},{12,4},{14,6},{16,24},{18,... | collective-permute-start | bytes 491528 | tf_op jit(solution)/shard_map/ppermute | solution.py:237
  386.3 11.8 %collective-permute-start.23 = (bf16[40,2048]{1,0:T(8,128)(2,1)S(1)}, bf16[40,2048]{1,0:T(8,128)(2,1)S(1)}, u32[]{:S(2)}, u32[]{:S(2)}) collective-permute-start(bf16[40,2048]{1,0:T(8,128)(2,1)S(1)} %get-tuple-element.35), channel_id=1, source_target_pairs={{0,12},{2,14},{4,8},{6,10},{8,4},{10,6},{12,0},{14,2},{16,28},{18,... | collective-permute-start | bytes 491528 | tf_op jit(solution)/shard_map/ppermute | solution.py:237
  386.3 22.1 %collective-permute-start.24 = (bf16[40,2048]{1,0:T(8,128)(2,1)S(1)}, bf16[40,2048]{1,0:T(8,128)(2,1)S(1)}, u32[]{:S(2)}, u32[]{:S(2)}) collective-permute-start(bf16[40,2048]{1,0:T(8,128)(2,1)S(1)} %get-tuple-element.34), channel_id=1, source_target_pairs={{0,16},{2,18},{4,20},{6,22},{8,24},{10,26},{12,28},{14,30},{16,0},... | collective-permute-start | bytes 491528 | tf_op jit(solution)/shard_map/ppermute | solution.py:237
  388.5 24.3 %collective-permute-start.25 = (bf16[40,2048]{1,0:T(8,128)(2,1)S(1)}, bf16[40,2048]{1,0:T(8,128)(2,1)S(1)}, u32[]{:S(2)}, u32[]{:S(2)}) collective-permute-start(bf16[40,2048]{1,0:T(8,128)(2,1)S(1)} %get-tuple-element.33), channel_id=1, source_target_pairs={{0,20},{2,22},{4,16},{6,18},{8,28},{10,30},{12,24},{14,26},{16,4},... | collective-permute-start | bytes 491528 | tf_op jit(solution)/shard_map/ppermute | solution.py:237
  390.1 22.7 %collective-permute-start.26 = (bf16[40,2048]{1,0:T(8,128)(2,1)S(1)}, bf16[40,2048]{1,0:T(8,128)(2,1)S(1)}, u32[]{:S(2)}, u32[]{:S(2)}) collective-permute-start(bf16[40,2048]{1,0:T(8,128)(2,1)S(1)} %get-tuple-element.32), channel_id=1, source_target_pairs={{0,24},{2,26},{4,28},{6,30},{8,16},{10,18},{12,20},{14,22},{16,8},... | collective-permute-start | bytes 491528 | tf_op jit(solution)/shard_map/ppermute | solution.py:237
  396.4 16.4 %collective-permute-start.27 = (bf16[40,2048]{1,0:T(8,128)(2,1)S(1)}, bf16[40,2048]{1,0:T(8,128)(2,1)S(1)}, u32[]{:S(2)}, u32[]{:S(2)}) collective-permute-start(bf16[40,2048]{1,0:T(8,128)(2,1)S(1)} %get-tuple-element.31), channel_id=1, source_target_pairs={{0,28},{2,30},{4,24},{6,26},{8,20},{10,22},{12,16},{14,18},{16,12}... | collective-permute-start | bytes 491528 | tf_op jit(solution)/shard_map/ppermute | solution.py:237
  (19 other events, 191.0 us)
Sparse Core Ops, SparseCore 0:
  8.9 113.7 all-gather.1

commit v3 on v2

--- a/solution.py
+++ b/solution.py
@@ -160,21 +160,23 @@
     )(ends, decay_rate)
 
 
-def scan_gated(step, decay_rate, conved, gain, kept, carry, pick, skip_gain, gate_in):
-    tokens, channels = conved.shape
+def scan_gated(step, decay_rate, conved, gain, kept, carry, pick, skip_gain, gate_in, half):
+    tokens, channels = conved.shape[0], conved.shape[1] // 2
     width = min(512, channels)
     chunk = carry.shape[2]
-    part = lambda rows: pl.BlockSpec((rows, width), lambda i: (0, i))
+    steps = channels // width
+    first = half * steps
+    part = lambda rows: pl.BlockSpec((rows, width), lambda i: (0, first + i))
     return pl.pallas_call(
         scan_kernel,
-        grid=(channels // width,),
+        grid=(steps,),
         in_specs=[
             part(tokens), part(NSTATE), part(tokens), whole((tokens, NSTATE, LANES)),
             whole((tokens, 1)),
-            pl.BlockSpec((width // chunk, NSTATE, chunk), lambda i: (i, 0, 0)),
+            pl.BlockSpec((width // chunk, NSTATE, chunk), lambda i: (first + i, 0, 0)),
             whole(pick.shape), part(1), part(tokens),
         ],
-        out_specs=part(tokens),
+        out_specs=pl.BlockSpec((tokens, width), lambda i: (0, i)),
         scratch_shapes=[
             pltpu.VMEM((tokens // SUBLANES, SUBLANES, width), jnp.float32),
             pltpu.VMEM((tokens // SUBLANES, SUBLANES, width), jnp.float32),
@@ -191,20 +193,42 @@
     )(step, decay_rate, conved, gain, kept, carry, pick, skip_gain[None, :], gate_in)
 
 
+def lower_kernel(shard_ref, hidden_ref, weight_ref, *out_refs):
+    out = jnp.dot(hidden_ref[...], weight_ref[0], preferred_element_type=jnp.float32)
+    rows = out_refs[0].shape[0]
+    for k, out_ref in enumerate(out_refs):
+        out_ref[...] = out[k * rows : (k + 1) * rows].astype(out_ref.dtype)
+
+
+def lowered(hidden, down_weight, shard, width, members):
+    rows, depth = hidden.shape
+    tile = min(1024, width)
+    steps = width // tile
+    out = jax.ShapeDtypeStruct((rows // members, width), jnp.bfloat16)
+    return pl.pallas_call(
+        lower_kernel,
+        grid_spec=pltpu.PrefetchScalarGridSpec(
+            num_scalar_prefetch=1,
+            grid=(steps,),
+            in_specs=[
+                pl.BlockSpec((rows, depth), lambda i, t: (0, 0)),
+                pl.BlockSpec((1, depth, tile), lambda i, t: (0, 0, t[0] * steps + i)),
+            ],
+            out_specs=[pl.BlockSpec((rows // members, tile), lambda i, t: (0, i))] * members,
+        ),
+        out_shape=[out] * members,
+        compiler_params=pltpu.CompilerParams(vmem_limit_bytes=VMEM),
+        cost_estimate=pl.CostEstimate(
+            flops=2 * rows * depth * width, bytes_accessed=2 * depth * width, transcendentals=0
+        ),
+        name="lowered",
+    )(shard.astype(jnp.int32)[None], hidden, down_weight)
+
+
 def summed_over(x, axis):
     total = x
     for by in range(1, lax.axis_size(axis)):
         total = total + rotated(x, axis, by)
-    return total
-
-
-def scattered_sum(parts, axis, mine):
-    size = parts.shape[0]
-    take = lambda k: lax.dynamic_index_in_dim(parts, k % size, 0, keepdims=False)
-    total = take(mine).astype(jnp.float32)
-    for by in range(1, size):
-        sent = rotated(take(mine + by).astype(jnp.bfloat16), axis, by)
-        total = total + sent.astype(jnp.float32)
     return total
 
 
@@ -298,13 +322,7 @@
     shard = lax.axis_index("tp")
     shards = lax.axis_size("tp")
     low = groups // shards
-    own_columns = lax.all_gather(
-        out_proj,
-        "loop",
-        axis=1,
-        tiled=True,
-        axis_index_groups=[[i + low * high for high in range(shards)] for i in range(low)],
-    )
+    columns = [out_proj] + [across(out_proj, low * high) for high in range(1, shards)]
     conv_taps = conv_weight.shape[0]
     rim_rows = shifted(mixer_in[tokens - (conv_taps - 1) :], "loop", 1)
     extended = jnp.concatenate([rim_rows, mixer_in], axis=0)
@@ -346,28 +364,48 @@
     chunk = channels // groups
     own_rates = lax.dynamic_slice_in_dim(decay_rate, position * chunk, chunk, 1)
     carry = lax.all_to_all(carries(ends, own_rates), "loop", 0, 0, tiled=True)
-    gated = scan_gated(
-        step_size, decay_rate, conved, gain, kept, carry, pick, skip_gain, gate_in
-    )
-    own_low = position % low
-    tokens_of = [gated] + [across(gated, m) for m in range(2, low, 2)]
-    own_columns, tokens_of = lax.optimization_barrier((own_columns, tokens_of))
-    other_columns = across(own_columns, 1)
-    all_tokens = jnp.concatenate(tokens_of, axis=0)
-    block = out_proj.shape[1]
-    halves = [
-        jnp.dot(all_tokens, columns, preferred_element_type=jnp.float32)
-        for columns in (own_columns, other_columns)
+    own_low, own_high = position % low, position // low
+    tokens_of = []
+    for half in range(2):
+        gated = scan_gated(
+            step_size, decay_rate, conved, gain, kept, carry, pick, skip_gain, gate_in, half
+        )
+        tokens_of.append(
+            {m: gated if m == 0 else across(gated, m) for m in (0, 2, 4) if m < low}
+        )
+    columns[1:], tokens_of = lax.optimization_barrier((columns[1:], tokens_of))
+    for half, got in enumerate(tokens_of):
+        for m in range(6, low, 2):
+            one = m & -m
+            if one == m:
+                got[m] = across(got[0], m)
+            else:
+                via = one if half == 0 else m ^ one
+                got[m] = across(got[via], m ^ via)
+    all_tokens = [
+        jnp.concatenate([got[m] for m in range(0, low, 2)], axis=0) for got in tokens_of
     ]
-    for_shard = lambda t: jnp.concatenate(
-        [lax.dynamic_slice_in_dim(part, t * block, block, 1) for part in halves], axis=1
-    )
+    depth = channels // 2
+    mixes = []
+    for block in columns:
+        pair = jnp.concatenate([block, across(block, 1)], axis=1)
+        mixes.append(
+            jnp.dot(all_tokens[0], pair[:depth], preferred_element_type=jnp.float32)
+            + jnp.dot(all_tokens[1], pair[depth:], preferred_element_type=jnp.float32)
+        )
+
+    def for_shard(t):
+        mix = mixes[0]
+        for high in range(1, shards):
+            mix = jnp.where((own_high ^ t) == high, mixes[high], mix)
+        return mix
+
     mixed_out = for_shard(shard)
     for by in range(1, shards):
         sent = for_shard((shard + by) % shards).astype(jnp.bfloat16)
         mixed_out = mixed_out + rotated(sent, "tp", by).astype(jnp.float32)
     pieces = [mixed_out[:tokens]]
-    for k in range(1, len(tokens_of)):
+    for k in range(1, low // 2):
         rows_out = mixed_out[k * tokens : (k + 1) * tokens].astype(jnp.bfloat16)
         pieces.append(across(rows_out, 2 * k))
     width = residual_in.shape[1]
@@ -390,9 +428,9 @@
     hidden_in, packed = hidden_and_packed(
         own_low.astype(jnp.int32)[None], gather_matrix.astype(jnp.bfloat16), residual_in, pieces
     )
-    arrived = teams_swapped(packed.reshape(EXPERTS, CAP, width), 0, members)
-    rows = EXPERTS * CAP
-    arrived = gathered(arrived.reshape(rows, width), "tp", shard, 1)
+    packed = packed.reshape(EXPERTS, CAP, width)
+    near = EXPERTS // 2
+    rows = near * CAP
 
     def from_member(by):
         pairs = [
@@ -400,26 +438,50 @@
         ]
         return lambda x: lax.ppermute(x, "loop", pairs)
 
+    parts = [
+        gathered(teams_swapped(packed[first : first + near], first, members), "tp", shard, 1)
+        for first in (near, 0)
+    ]
     slot_rows = jnp.concatenate(
-        [arrived] + [from_member(by)(arrived) for by in range(1, members)], axis=0
+        parts + [from_member(by)(part) for by in range(1, members) for part in parts], axis=0
     )
     gate_value = jnp.dot(slot_rows, gate_weight[0], preferred_element_type=jnp.float32)
     up_value = jnp.dot(slot_rows, up_weight[0], preferred_element_type=jnp.float32)
     hidden = (jax.nn.silu(gate_value) * up_value).astype(jnp.bfloat16)
-    partial_out = jnp.dot(hidden, down_weight[0], preferred_element_type=jnp.float32)
-    partial_out = partial_out.astype(jnp.bfloat16).reshape(members, rows, features)
-    member_sum = partial_out[0].astype(jnp.float32)
-    for by in range(1, members):
-        back = from_member(members - by)(partial_out[by])
-        member_sum = member_sum + back.astype(jnp.float32)
-    shares = scattered_sum(
-        jnp.stack([member_sum[:, k * width : (k + 1) * width] for k in range(shards)]),
-        "tp",
-        shard,
-    )
-    returned = teams_swapped(
-        shares.astype(jnp.bfloat16).reshape(EXPERTS, CAP, width), 0, members
-    ).reshape(rows, width)
+
+    def member_sum(outs):
+        total = outs[0].astype(jnp.float32)
+        for by in range(1, members):
+            total = total + from_member(members - by)(outs[by]).astype(jnp.float32)
+        return total
+
+    def for_shard_of(hidden, t):
+        return lowered(hidden, down_weight, t, width, members)
+
+    sent = [
+        member_sum(for_shard_of(hidden, (shard + by) % shards)).astype(jnp.bfloat16)
+        for by in range(1, shards)
+    ]
+    hidden, sent = lax.optimization_barrier((hidden, sent))
+    far_sums = [rotated(part[:rows], "tp", by) for by, part in enumerate(sent, 1)]
+    own_outs = for_shard_of(hidden, shard)
+    far_sums, own_outs, near_sent = lax.optimization_barrier(
+        (far_sums, own_outs, [part[rows:] for part in sent])
+    )
+    near_sums = [rotated(part, "tp", by) for by, part in enumerate(near_sent, 1)]
+    own_sum = member_sum(own_outs)
+
+    def given_back(first, own, sums):
+        share = own
+        for part in sums:
+            share = share + part.astype(jnp.float32)
+        share = share.astype(jnp.bfloat16).reshape(near, CAP, width)
+        return teams_swapped(share, first, members)
+
+    far_back = given_back(near, own_sum[:rows], far_sums)
+    near_sums, far_back = lax.optimization_barrier((near_sums, far_back))
+    back = [given_back(0, own_sum[rows:], near_sums), far_back]
+    returned = jnp.concatenate(back, axis=0).reshape(EXPERTS * CAP, width)
     expert_sum = jnp.dot(
         weighted.T,
         returned.astype(jnp.float32),

time: 425 us -> 392 us (0.922)
  Pallas kernels: 26.8 us -> 49.6 us
  waiting for transfers between devices: 205 us -> 184 us
  matrix products: 73.6 us -> 57.5 us
  between operations: 14.6 us -> 1.38 us
  local copies, waits for them, and re-layouts: 26.3 us -> 36.9 us
  starting transfers between devices: 59.3 us -> 51 us
  other arithmetic: 16.2 us -> 11.1 us
    all_to_all x1, waiting for transfers between devices: 27.2 us -> 71 us  [per_device(): ends = lax.all_to_all(end_state, 'loop', 0, 0, tiled=True)]
    ppermute x7 -> x12, waiting for transfers between devices: 61 us -> 19.6 us  [across(): lax.ppermute(x, 'loop', [(i, i ^ mask) for i in range(lax.axis_size('loop...]
    ppermute x4 -> x6, waiting for transfers between devices: 63.2 us -> 28.6 us  [rotated(): return lax.ppermute(x, axis, [(i, (i + by) % size) for i in range(size)])]
    pallas_call x1 -> x4, Pallas kernels: 13.3 us -> 36.1 us  [the longest x2 22.8 us: lowered(): pl.pallas_call(lower_kernel, grid_spec=pltpu.PrefetchScalarGridSpec(num_s...]
    dot_general x3 -> x4, matrix products: 26.6 us -> 6.06 us  [the longest x2 3.55 us: per_device(): jnp.dot(all_tokens[0], pair[:depth], preferred_element_type=jnp.float32)]
    ppermute x14, waiting for transfers between devices: 35.8 us -> 49 us  [teams_swapped(): out.append(lax.ppermute(x[k], 'loop', pairs))]
    ppermute x14, starting transfers between devices: 30.5 us -> 18.4 us  [teams_swapped(): out.append(lax.ppermute(x[k], 'loop', pairs))]
    unnamed x56 -> x71, local copies, waits for them, and re-layouts: 13 us -> 25 us
  transfers between devices with their start and end apart: 31 -> 39, of which waited for: 22 -> 27; matrix products, arithmetic and copies ran while one was open for 5% -> 6% of each run, Pallas kernels for 6% -> 10%
where the time goes in v3:
time: 392 us; the launch traced here: 391 us
  waiting for transfers between devices  184 us (47%)
  matrix products  57.5 us (15%)
  starting transfers between devices  51 us (13%)
  Pallas kernels  49.6 us (13%)
  local copies, waits for them, and re-layouts  36.9 us (9%)
  other arithmetic  11.1 us (3%)
    all_to_all x1, waiting for transfers between devices, per_device(): ends = lax.all_to_all(end_state, 'loop', 0, 0, tiled=True)  71 us
    ppermute x14, waiting for transfers between devices, teams_swapped(): out.append(lax.ppermute(x[k], 'loop', pairs))  49 us
    ppermute x6, waiting for transfers between devices, rotated(): return lax.ppermute(x, axis, [(i, (i + by) % size) for i in range(size)])  28.6 us
    dot_general x1, matrix products, per_device(): jnp.dot(slot_rows, up_weight[0], preferred_element_type=jnp.float32)  25.1 us
    unnamed x71, local copies, waits for them, and re-layouts  25 us
    pallas_call x2, Pallas kernels, lowered(): pl.pallas_call(lower_kernel, grid_spec=pltpu.PrefetchScalarGridSpec(num_s...  22.8 us
    dot_general x1, matrix products, per_device(): jnp.dot(slot_rows, gate_weight[0], preferred_element_type=jnp.float32)  21.7 us
    ppermute x12, waiting for transfers between devices, across(): lax.ppermute(x, 'loop', [(i, i ^ mask) for i in range(lax.axis_size('loop...  19.6 us
  transfers between devices with their start and end apart: 39, of which 27 were waited for; matrix products, arithmetic and copies ran while one was open for 6% of the time, Pallas kernels for 10%

profile of v3, /device:TPU:0, one launch (start us, length us, event | category | flops | bytes accessed | tf_op | source)
XLA Modules:
  0.0 391.1 jit_solution(8692558628795541225)
XLA Ops:
  4.5 3.9 multiply_convert_fusion.1.conved_ref
  12.4 5.9 %collective-permute-start = (bf16[4096,256]{1,0:T(8,128)(2,1)}, bf16[4096,256]{1,0:T(8,128)(2,1)}, u32[]{:S(2)}, u32[]{:S(2)}) collective-permute-start(bf16[4096,256]{1,0:T(8,128)(2,1)} %param.28), channel_id=1, source_target_pairs={{0,16},{2,18},{4,20},{6,22},{8,24},{10,26},{12,28},{14,30},{16,0},... | collective-permute-start | bytes 6291464 | tf_op jit(solution)/shard_map/ppermute | solution.py:249
  25.0 11.2 %scan_end.1 = (f32[128,4096]{1,0:T(8,128)S(1)}, bf16[16,32,256]{2,1,0:T(8,128)(2,1)}) custom-call(bf16[128,256]{1,0:T(8,128)(2,1)S(1)} %slice.210.low_ref, bf16[256,4096]{1,0:T(8,128)(2,1)S(1)} %copy-done.5, f32[1,4096]{1,0:T(1,128)S(1)} %bitcast.38, f32[16,4096]{1,0:T(8,128)S(1)} %copy-done.3, bf16[128,4096]{1,0:T(8,128)(2,1)S(1)} %multiply_convert_fusion.1.conved_ref, ...), custom_call_target="tpu_custom_call" | custom-call | flops 41943040 | bytes 4194304 | tf_op jit(solution)/shard_map/scan_end/pallas_call | solution.py:125
  37.5 3.7 all-to-all-start
  41.8 71.0 %all-to-all-done.ends_ref = bf16[16,32,256]{2,1,0:T(8,128)(2,1)S(1)} async-done(((bf16[16,32,256]{2,1,0:T(8,128)(2,1)}), bf16[16,32,256]{2,1,0:T(8,128)(2,1)S(1)}, u32[]{:S(2)}, u32[]{:S(2)}) %all-to-all-start) | async-done | bytes 262176 | tf_op jit(solution)/shard_map/all_to_all | solution.py:363
  115.2 6.0 %all-to-all-start.1 = ((bf16[16,16,256]{2,1,0:T(8,128)(2,1)}), bf16[16,16,256]{2,1,0:T(8,128)(2,1)S(1)}, u32[]{:S(2)}, u32[]{:S(2)}) async-start(bf16[16,16,256]{2,1,0:T(8,128)(2,1)} %carries.1), calls=%async_computation.1 | async-start | bytes 262144 | tf_op jit(solution)/shard_map/all_to_all | solution.py:366
  122.3 6.8 %all-to-all-done.1.carry_ref = bf16[16,16,256]{2,1,0:T(8,128)(2,1)S(1)} async-done(((bf16[16,16,256]{2,1,0:T(8,128)(2,1)}), bf16[16,16,256]{2,1,0:T(8,128)(2,1)S(1)}, u32[]{:S(2)}, u32[]{:S(2)}) %all-to-all-start.1) | async-done | bytes 131104 | tf_op jit(solution)/shard_map/all_to_all | solution.py:366
  133.0 6.7 %scan_gated.2 = bf16[128,2048]{1,0:T(8,128)(2,1)S(1)} custom-call(f32[128,4096]{1,0:T(8,128)S(1)} %copy-done.15, f32[16,4096]{1,0:T(8,128)S(1)} %copy-done.3, bf16[128,4096]{1,0:T(8,128)(2,1)S(1)} %multiply_convert_fusion.1.conved_ref, f32[128,16,128]{2,1,0:T(8,128)S(1)} %broadcast_in_dim.48.gain_ref, f32[128,1]{1,0:T(8,128)S(1)} %copy.51.kept_ref, ...), custom_call_target="tpu_custom_call" | custom-call | flops 29360128 | bytes 3145728 | tf_op jit(solution)/shard_map/scan_gated/pallas_call | solution.py:170
  146.3 6.7 %scan_gated.3 = bf16[128,2048]{1,0:T(8,128)(2,1)S(1)} custom-call(f32[128,4096]{1,0:T(8,128)S(1)} %copy-done.16, f32[16,4096]{1,0:T(8,128)S(1)} %copy-done.4, bf16[128,4096]{1,0:T(8,128)(2,1)S(1)} %multiply_convert_fusion.1.conved_ref, f32[128,16,128]{2,1,0:T(8,128)S(1)} %broadcast_in_dim.48.gain_ref, f32[128,1]{1,0:T(8,128)S(1)} %copy.51.kept_ref, ...), custom_call_target="tpu_custom_call" | custom-call | flops 29360128 | bytes 3145728 | tf_op jit(solution)/shard_map/scan_gated/pallas_call | solution.py:170
  158.5 8.7 %collective-permute-done.5 = bf16[128,2048]{1,0:T(8,128)(2,1)S(1)} collective-permute-done((bf16[128,2048]{1,0:T(8,128)(2,1)S(1)}, bf16[128,2048]{1,0:T(8,128)(2,1)S(1)}, u32[]{:S(2)}, u32[]{:S(2)}) %collective-permute-start.5) | collective-permute-done | bytes 524320 | tf_op jit(solution)/shard_map/ppermute | solution.py:249
  176.6 5.3 %collective-permute-done.9 = bf16[128,2048]{1,0:T(8,128)(2,1)S(1)} collective-permute-done((bf16[128,2048]{1,0:T(8,128)(2,1)S(1)}, bf16[128,2048]{1,0:T(8,128)(2,1)S(1)}, u32[]{:S(2)}, u32[]{:S(2)}) %collective-permute-start.9) | collective-permute-done | bytes 524320 | tf_op jit(solution)/shard_map/ppermute | solution.py:249
  189.5 11.5 %collective-permute-done.11 = bf16[512,512]{1,0:T(8,128)(2,1)S(1)} collective-permute-done((bf16[512,512]{1,0:T(8,128)(2,1)S(1)}, bf16[512,512]{1,0:T(8,128)(2,1)S(1)}, u32[]{:S(2)}, u32[]{:S(2)}) %collective-permute-start.11) | collective-permute-done | bytes 524320 | tf_op jit(solution)/shard_map/ppermute | solution.py:30
  220.9 6.0 %collective-permute-done.21 = bf16[40,2048]{1,0:T(8,128)(2,1)S(1)} collective-permute-done((bf16[40,2048]{1,0:T(8,128)(2,1)S(1)}, bf16[40,2048]{1,0:T(8,128)(2,1)S(1)}, u32[]{:S(2)}, u32[]{:S(2)}) %collective-permute-start.21) | collective-permute-done | bytes 163872 | tf_op jit(solution)/shard_map/ppermute | solution.py:261
  229.6 3.6 collective-permute-done.15
  233.2 5.3 %collective-permute-done.16 = bf16[40,2048]{1,0:T(8,128)(2,1)S(1)} collective-permute-done((bf16[40,2048]{1,0:T(8,128)(2,1)}, bf16[40,2048]{1,0:T(8,128)(2,1)S(1)}, u32[]{:S(2)}, u32[]{:S(2)}) %collective-permute-start.16) | collective-permute-done | bytes 163872 | tf_op jit(solution)/shard_map/ppermute | solution.py:261
  240.1 5.3 %collective-permute-done.23 = bf16[160,2048]{1,0:T(8,128)(2,1)} collective-permute-done((bf16[160,2048]{1,0:T(8,128)(2,1)S(1)}, bf16[160,2048]{1,0:T(8,128)(2,1)}, u32[]{:S(2)}, u32[]{:S(2)}) %collective-permute-start.23) | collective-permute-done | bytes 655392 | tf_op jit(solution)/shard_map/ppermute | solution.py:30
  246.7 7.7 %collective-permute-done.19 = bf16[160,2048]{1,0:T(8,128)(2,1)} collective-permute-done((bf16[160,2048]{1,0:T(8,128)(2,1)S(1)}, bf16[160,2048]{1,0:T(8,128)(2,1)}, u32[]{:S(2)}, u32[]{:S(2)}) %collective-permute-start.19) | collective-permute-done | bytes 655392 | tf_op jit(solution)/shard_map/ppermute | solution.py:30
  255.6 3.0 collective-permute-done.24
  259.7 21.7 %fusion.2 = f32[640,3072]{1,0:T(8,128)} fusion(bf16[1,4096,3072]{2,1,0:T(8,128)(2,1)} %param.30, bf16[160,4096]{1,0:T(8,128)(2,1)S(1)} %collective-permute-done.25, bf16[160,4096]{1,0:T(8,128)(2,1)S(1)} %collective-permute-done.24, bf16[160,4096]{1,0:T(8,128)(2,1)S(1)} %constant_dynamic-update-slice_fusion.20, ...), kind=kOutput, calls=%fused_computation.2 | convolution fusion | flops 16127098880 | bytes 38273024 | tf_op jit(solution)/shard_map/dot_general | solution.py:448
  281.4 25.1 %multiply_convert_fusion.hidden_ref = bf16[640,3072]{1,0:T(8,128)(2,1)} fusion(f32[640,3072]{1,0:T(8,128)} %fusion.2, bf16[1,4096,3072]{2,1,0:T(8,128)(2,1)} %param.31, bf16[160,4096]{1,0:T(8,128)(2,1)} %copy-done.25, bf16[160,4096]{1,0:T(8,128)(2,1)} %copy-done.26, bf16[160,4096]{1,0:T(8,128)(2,1)S(1)} %constant_dynamic-update-slice_fusion.20, ...), kind=kOutput, calls=%fused_computation.4 | convolution fusion | flops 16138895360 | bytes 42205184 | tf_op jit(solution)/shard_map/dot_general | solution.py:449
  308.6 11.4 %lowered.2 = (bf16[320,2048]{1,0:T(8,128)(2,1)S(1)}, bf16[320,2048]{1,0:T(8,128)(2,1)S(1)}) custom-call(s32[1]{0:T(128)} %bitcast.14.shard_ref, bf16[640,3072]{1,0:T(8,128)(2,1)S(1)} %copy-done.10, bf16[1,3072,4096]{2,1,0:T(8,128)(2,1)} %weight_ref.3), custom_call_target="tpu_custom_call" | custom-call | flops 8053063680 | bytes 12582912 | tf_op jit(solution)/shard_map/lowered/pallas_call | solution.py:208
  320.2 2.9 collective-permute-done.26
  325.2 11.4 %lowered.3 = (bf16[320,2048]{1,0:T(8,128)(2,1)S(1)}, bf16[320,2048]{1,0:T(8,128)(2,1)S(1)}) custom-call(s32[1]{0:T(128)} %bitcast.15.shard_ref, bf16[640,3072]{1,0:T(8,128)(2,1)S(1)} %copy-done.11, bf16[1,3072,4096]{2,1,0:T(8,128)(2,1)} %weight_ref.3), custom_call_target="tpu_custom_call" | custom-call | flops 8053063680 | bytes 12582912 | tf_op jit(solution)/shard_map/lowered/pallas_call | solution.py:208
  336.6 4.0 %collective-permute-done.27 = bf16[160,2048]{1,0:T(8,128)(2,1)S(1)} collective-permute-done((bf16[160,2048]{1,0:T(8,128)(2,1)S(1)}, bf16[160,2048]{1,0:T(8,128)(2,1)S(1)}, u32[]{:S(2)}, u32[]{:S(2)}) %collective-permute-start.27) | collective-permute-done | bytes 655392 | tf_op jit(solution)/shard_map/ppermute | solution.py:30
  340.9 2.7 collective-permute-done.28
  344.6 4.6 %collective-permute-start.32 = (bf16[40,2048]{1,0:T(8,128)(2,1)S(1)}, bf16[40,2048]{1,0:T(8,128)(2,1)S(1)}, u32[]{:S(2)}, u32[]{:S(2)}) collective-permute-start(bf16[40,2048]{1,0:T(8,128)(2,1)S(1)} %get-tuple-element.73), channel_id=1, source_target_pairs={{0,24},{2,26},{4,28},{6,30},{8,16},{10,18},{12,20},{14,22},{16,8},... | collective-permute-start | bytes 491528 | tf_op jit(solution)/shard_map/ppermute | solution.py:261
  354.3 3.5 collective-permute-done.32
  357.8 16.7 %collective-permute-done.31 = bf16[40,2048]{1,0:T(8,128)(2,1)S(1)} collective-permute-done((bf16[40,2048]{1,0:T(8,128)(2,1)S(1)}, bf16[40,2048]{1,0:T(8,128)(2,1)S(1)}, u32[]{:S(2)}, u32[]{:S(2)}) %collective-permute-start.31) | collective-permute-done | bytes 163872 | tf_op jit(solution)/shard_map/ppermute | solution.py:261
  374.5 3.4 collective-permute-done.30
  378.9 2.9 collective-permute-start.36
  381.8 2.7 collective-permute-done.34
  386.0 3.1 collective-permute-done.36
  (188 shorter events, 95.3 us)
Async XLA Ops:
  10.1 11.9 %collective-permute-start.2 = (f32[128,288]{1,0:T(8,128)}, f32[128,288]{1,0:T(8,128)S(1)}, u32[]{:S(2)}, u32[]{:S(2)}) collective-permute-start(f32[128,288]{1,0:T(8,128)} %fusion.47), channel_id=1, source_target_pairs={{0,1},{1,0},{2,3},{3,2},{4,5},{5,4},{6,7},{7,6},{8,9},{9,8},{10,11... | collective-permute-start | bytes 442376 | tf_op jit(solution)/shard_map/ppermute | solution.py:30
  12.4 156.2 %collective-permute-start = (bf16[4096,256]{1,0:T(8,128)(2,1)}, bf16[4096,256]{1,0:T(8,128)(2,1)}, u32[]{:S(2)}, u32[]{:S(2)}) collective-permute-start(bf16[4096,256]{1,0:T(8,128)(2,1)} %param.28), channel_id=1, source_target_pairs={{0,16},{2,18},{4,20},{6,22},{8,24},{10,26},{12,28},{14,30},{16,0},... | collective-permute-start | bytes 6291464 | tf_op jit(solution)/shard_map/ppermute | solution.py:249
  37.5 75.3 %all-to-all-start = ((bf16[16,32,256]{2,1,0:T(8,128)(2,1)}), bf16[16,32,256]{2,1,0:T(8,128)(2,1)S(1)}, u32[]{:S(2)}, u32[]{:S(2)}) async-start(bf16[16,32,256]{2,1,0:T(8,128)(2,1)} %get-tuple-element.29), calls=%async_computation | async-start | bytes 524288 | tf_op jit(solution)/shard_map/all_to_all | solution.py:363
  115.2 13.9 %all-to-all-start.1 = ((bf16[16,16,256]{2,1,0:T(8,128)(2,1)}), bf16[16,16,256]{2,1,0:T(8,128)(2,1)S(1)}, u32[]{:S(2)}, u32[]{:S(2)}) async-start(bf16[16,16,256]{2,1,0:T(8,128)(2,1)} %carries.1), calls=%async_computation.1 | async-start | bytes 262144 | tf_op jit(solution)/shard_map/all_to_all | solution.py:366
  139.6 15.0 %collective-permute-start.3 = (bf16[128,2048]{1,0:T(8,128)(2,1)S(1)}, bf16[128,2048]{1,0:T(8,128)(2,1)}, u32[]{:S(2)}, u32[]{:S(2)}) collective-permute-start(bf16[128,2048]{1,0:T(8,128)(2,1)S(1)} %scan_gated.2), channel_id=1, source_target_pairs={{0,4},{2,6},{4,0},{6,2},{8,12},{10,14},{12,8},{14,10},{16,20},{18,... | collective-permute-start | bytes 1572872 | tf_op jit(solution)/shard_map/ppermute | solution.py:249
  139.7 32.9 %collective-permute-start.10 = (bf16[4096,256]{1,0:T(8,128)(2,1)}, bf16[4096,256]{1,0:T(8,128)(2,1)}, u32[]{:S(2)}, u32[]{:S(2)}) collective-permute-start(bf16[4096,256]{1,0:T(8,128)(2,1)} %param.28), channel_id=1, source_target_pairs={{0,2},{2,0},{4,6},{6,4},{8,10},{10,8},{12,14},{14,12},{16,18},{18,... | collective-permute-start | bytes 6291464 | tf_op jit(solution)/shard_map/ppermute | solution.py:249
  141.1 17.4 %collective-permute-start.4 = (bf16[128,2048]{1,0:T(8,128)(2,1)S(1)}, bf16[128,2048]{1,0:T(8,128)(2,1)}, u32[]{:S(2)}, u32[]{:S(2)}) collective-permute-start(bf16[128,2048]{1,0:T(8,128)(2,1)S(1)} %scan_gated.2), channel_id=1, source_target_pairs={{0,8},{2,10},{4,12},{6,14},{8,0},{10,2},{12,4},{14,6},{16,24},{18,... | collective-permute-start | bytes 1572872 | tf_op jit(solution)/shard_map/ppermute | solution.py:249
  153.0 14.2 %collective-permute-start.5 = (bf16[128,2048]{1,0:T(8,128)(2,1)S(1)}, bf16[128,2048]{1,0:T(8,128)(2,1)S(1)}, u32[]{:S(2)}, u32[]{:S(2)}) collective-permute-start(bf16[128,2048]{1,0:T(8,128)(2,1)S(1)} %scan_gated.3), channel_id=1, source_target_pairs={{0,4},{2,6},{4,0},{6,2},{8,12},{10,14},{12,8},{14,10},{16,20},{18,... | collective-permute-start | bytes 1572872 | tf_op jit(solution)/shard_map/ppermute | solution.py:249
  154.6 14.1 %collective-permute-start.6 = (bf16[128,2048]{1,0:T(8,128)(2,1)S(1)}, bf16[128,2048]{1,0:T(8,128)(2,1)S(1)}, u32[]{:S(2)}, u32[]{:S(2)}) collective-permute-start(bf16[128,2048]{1,0:T(8,128)(2,1)S(1)} %scan_gated.3), channel_id=1, source_target_pairs={{0,8},{2,10},{4,12},{6,14},{8,0},{10,2},{12,4},{14,6},{16,24},{18,... | collective-permute-start | bytes 1572872 | tf_op jit(solution)/shard_map/ppermute | solution.py:249
  168.7 13.2 %collective-permute-start.9 = (bf16[128,2048]{1,0:T(8,128)(2,1)S(1)}, bf16[128,2048]{1,0:T(8,128)(2,1)S(1)}, u32[]{:S(2)}, u32[]{:S(2)}) collective-permute-start(bf16[128,2048]{1,0:T(8,128)(2,1)S(1)} %collective-permute-done.6), channel_id=1, source_target_pairs={{0,4},{2,6},{4,0},{6,2},{8,12},{10,14},{12,8},{14,10},{16,20},{18,... | collective-permute-start | bytes 1572872 | tf_op jit(solution)/shard_map/ppermute | solution.py:249
  169.0 13.4 %collective-permute-start.7 = (bf16[128,2048]{1,0:T(8,128)(2,1)}, bf16[128,2048]{1,0:T(8,128)(2,1)S(1)}, u32[]{:S(2)}, u32[]{:S(2)}) collective-permute-start(bf16[128,2048]{1,0:T(8,128)(2,1)} %collective-permute-done.3), channel_id=1, source_target_pairs={{0,8},{2,10},{4,12},{6,14},{8,0},{10,2},{12,4},{14,6},{16,24},{18,... | collective-permute-start | bytes 1572872 | tf_op jit(solution)/shard_map/ppermute | solution.py:249
  170.8 14.2 %collective-permute-start.8 = (bf16[4096,256]{1,0:T(8,128)(2,1)}, bf16[4096,256]{1,0:T(8,128)(2,1)S(1)}, u32[]{:S(2)}, u32[]{:S(2)}) collective-permute-start(bf16[4096,256]{1,0:T(8,128)(2,1)} %collective-permute-done), channel_id=1, source_target_pairs={{0,2},{2,0},{4,6},{6,4},{8,10},{10,8},{12,14},{14,12},{16,18},{18,... | collective-permute-start | bytes 6291464 | tf_op jit(solution)/shard_map/ppermute | solution.py:249
  188.8 12.3 %collective-permute-start.11 = (bf16[512,512]{1,0:T(8,128)(2,1)S(1)}, bf16[512,512]{1,0:T(8,128)(2,1)S(1)}, u32[]{:S(2)}, u32[]{:S(2)}) collective-permute-start(bf16[512,512]{1,0:T(8,128)(2,1)S(1)} %get-tuple-element.84), channel_id=1, source_target_pairs={{0,1},{1,0},{2,3},{3,2},{4,5},{5,4},{6,7},{7,6},{8,9},{9,8},{10,11... | collective-permute-start | bytes 1572872 | tf_op jit(solution)/shard_map/ppermute | solution.py:30
  212.9 7.7 %collective-permute-start.22 = (bf16[40,2048]{1,0:T(8,128)(2,1)S(1)}, bf16[40,2048]{1,0:T(8,128)(2,1)S(1)}, u32[]{:S(2)}, u32[]{:S(2)}) collective-permute-start(bf16[40,2048]{1,0:T(8,128)(2,1)S(1)} %get-tuple-element.60), channel_id=1, source_target_pairs={{0,12},{2,14},{4,8},{6,10},{8,4},{10,6},{12,0},{14,2},{16,28},{18,... | collective-permute-start | bytes 491528 | tf_op jit(solution)/shard_map/ppermute | solution.py:261
  214.3 12.6 %collective-permute-start.21 = (bf16[40,2048]{1,0:T(8,128)(2,1)S(1)}, bf16[40,2048]{1,0:T(8,128)(2,1)S(1)}, u32[]{:S(2)}, u32[]{:S(2)}) collective-permute-start(bf16[40,2048]{1,0:T(8,128)(2,1)S(1)} %get-tuple-element.61), channel_id=1, source_target_pairs={{0,8},{2,10},{4,12},{6,14},{8,0},{10,2},{12,4},{14,6},{16,24},{18,... | collective-permute-start | bytes 491528 | tf_op jit(solution)/shard_map/ppermute | solution.py:261
  215.4 11.6 %collective-permute-start.20 = (bf16[40,2048]{1,0:T(8,128)(2,1)S(1)}, bf16[40,2048]{1,0:T(8,128)(2,1)S(1)}, u32[]{:S(2)}, u32[]{:S(2)}) collective-permute-start(bf16[40,2048]{1,0:T(8,128)(2,1)S(1)} %get-tuple-element.62), channel_id=1, source_target_pairs={{0,4},{2,6},{4,0},{6,2},{8,12},{10,14},{12,8},{14,10},{16,20},{18,... | collective-permute-start | bytes 491528 | tf_op jit(solution)/shard_map/ppermute | solution.py:261
  216.4 16.8 %collective-permute-start.15 = (bf16[40,2048]{1,0:T(8,128)(2,1)S(1)}, bf16[40,2048]{1,0:T(8,128)(2,1)S(1)}, u32[]{:S(2)}, u32[]{:S(2)}) collective-permute-start(bf16[40,2048]{1,0:T(8,128)(2,1)S(1)} %get-tuple-element.66), channel_id=1, source_target_pairs={{0,16},{2,18},{4,20},{6,22},{8,24},{10,26},{12,28},{14,30},{16,0},... | collective-permute-start | bytes 491528 | tf_op jit(solution)/shard_map/ppermute | solution.py:261
  217.2 21.4 %collective-permute-start.16 = (bf16[40,2048]{1,0:T(8,128)(2,1)}, bf16[40,2048]{1,0:T(8,128)(2,1)S(1)}, u32[]{:S(2)}, u32[]{:S(2)}) collective-permute-start(bf16[40,2048]{1,0:T(8,128)(2,1)} %get-tuple-element.65), channel_id=1, source_target_pairs={{0,20},{2,22},{4,16},{6,18},{8,28},{10,30},{12,24},{14,26},{16,4},... | collective-permute-start | bytes 491528 | tf_op jit(solution)/shard_map/ppermute | solution.py:261
  220.6 17.9 %collective-permute-start.17 = (bf16[40,2048]{1,0:T(8,128)(2,1)S(1)}, bf16[40,2048]{1,0:T(8,128)(2,1)S(1)}, u32[]{:S(2)}, u32[]{:S(2)}) collective-permute-start(bf16[40,2048]{1,0:T(8,128)(2,1)S(1)} %get-tuple-element.64), channel_id=1, source_target_pairs={{0,24},{2,26},{4,28},{6,30},{8,16},{10,18},{12,20},{14,22},{16,8},... | collective-permute-start | bytes 491528 | tf_op jit(solution)/shard_map/ppermute | solution.py:261
  226.9 11.7 %collective-permute-start.18 = (bf16[40,2048]{1,0:T(8,128)(2,1)S(1)}, bf16[40,2048]{1,0:T(8,128)(2,1)S(1)}, u32[]{:S(2)}, u32[]{:S(2)}) collective-permute-start(bf16[40,2048]{1,0:T(8,128)(2,1)S(1)} %get-tuple-element.59), channel_id=1, source_target_pairs={{0,28},{2,30},{4,24},{6,26},{8,20},{10,22},{12,16},{14,18},{16,12}... | collective-permute-start | bytes 491528 | tf_op jit(solution)/shard_map/ppermute | solution.py:261
  229.6 15.9 %collective-permute-start.23 = (bf16[160,2048]{1,0:T(8,128)(2,1)S(1)}, bf16[160,2048]{1,0:T(8,128)(2,1)}, u32[]{:S(2)}, u32[]{:S(2)}) collective-permute-start(bf16[160,2048]{1,0:T(8,128)(2,1)S(1)} %get-tuple-element.75), channel_id=1, source_target_pairs={{0,1},{1,0},{2,3},{3,2},{4,5},{5,4},{6,7},{7,6},{8,9},{9,8},{10,11... | collective-permute-start | bytes 1966088 | tf_op jit(solution)/shard_map/ppermute | solution.py:30
  238.6 15.7 %collective-permute-start.19 = (bf16[160,2048]{1,0:T(8,128)(2,1)S(1)}, bf16[160,2048]{1,0:T(8,128)(2,1)}, u32[]{:S(2)}, u32[]{:S(2)}) collective-permute-start(bf16[160,2048]{1,0:T(8,128)(2,1)S(1)} %constant_dynamic-update-slice_fusion.12), channel_id=1, source_target_pairs={{0,1},{1,0},{2,3},{3,2},{4,5},{5,4},{6,7},{7,6},{8,9},{9,8},{10,11... | collective-permute-start | bytes 1966088 | tf_op jit(solution)/shard_map/ppermute | solution.py:30
  246.6 9.0 %collective-permute-start.25 = (bf16[160,4096]{1,0:T(8,128)(2,1)S(1)}, bf16[160,4096]{1,0:T(8,128)(2,1)S(1)}, u32[]{:S(2)}, u32[]{:S(2)}) collective-permute-start(bf16[160,4096]{1,0:T(8,128)(2,1)S(1)} %constant_dynamic-update-slice_fusion.20), channel_id=1, source_target_pairs={{0,2},{2,0},{4,6},{6,4},{8,10},{10,8},{12,14},{14,12},{16,18},{18,... | collective-permute-start | bytes 3932168 | tf_op jit(solution)/shard_map/ppermute | solution.py:439
  323.8 16.8 %collective-permute-start.27 = (bf16[160,2048]{1,0:T(8,128)(2,1)S(1)}, bf16[160,2048]{1,0:T(8,128)(2,1)S(1)}, u32[]{:S(2)}, u32[]{:S(2)}) collective-permute-start(bf16[160,2048]{1,0:T(8,128)(2,1)S(1)} %get-tuple-element.58), channel_id=1, source_target_pairs={{0,1},{1,0},{2,3},{3,2},{4,5},{5,4},{6,7},{7,6},{8,9},{9,8},{10,11... | collective-permute-start | bytes 1966088 | tf_op jit(solution)/shard_map/ppermute | solution.py:30
  340.6 37.4 %collective-permute-start.29 = (bf16[160,2048]{1,0:T(8,128)(2,1)S(1)}, bf16[160,2048]{1,0:T(8,128)(2,1)S(1)}, u32[]{:S(2)}, u32[]{:S(2)}) collective-permute-start(bf16[160,2048]{1,0:T(8,128)(2,1)S(1)} %get-tuple-element.47), channel_id=1, source_target_pairs={{0,1},{1,0},{2,3},{3,2},{4,5},{5,4},{6,7},{7,6},{8,9},{9,8},{10,11... | collective-permute-start | bytes 1966088 | tf_op jit(solution)/shard_map/ppermute | solution.py:30
  344.4 9.9 %collective-permute-start.33 = (bf16[40,2048]{1,0:T(8,128)(2,1)S(1)}, bf16[40,2048]{1,0:T(8,128)(2,1)S(1)}, u32[]{:S(2)}, u32[]{:S(2)}) collective-permute-start(bf16[40,2048]{1,0:T(8,128)(2,1)S(1)} %get-tuple-element.72), channel_id=1, source_target_pairs={{0,28},{2,30},{4,24},{6,26},{8,20},{10,22},{12,16},{14,18},{16,12}... | collective-permute-start | bytes 491528 | tf_op jit(solution)/shard_map/ppermute | solution.py:261
  344.6 13.2 %collective-permute-start.32 = (bf16[40,2048]{1,0:T(8,128)(2,1)S(1)}, bf16[40,2048]{1,0:T(8,128)(2,1)S(1)}, u32[]{:S(2)}, u32[]{:S(2)}) collective-permute-start(bf16[40,2048]{1,0:T(8,128)(2,1)S(1)} %get-tuple-element.73), channel_id=1, source_target_pairs={{0,24},{2,26},{4,28},{6,30},{8,16},{10,18},{12,20},{14,22},{16,8},... | collective-permute-start | bytes 491528 | tf_op jit(solution)/shard_map/ppermute | solution.py:261
  349.1 25.4 %collective-permute-start.31 = (bf16[40,2048]{1,0:T(8,128)(2,1)S(1)}, bf16[40,2048]{1,0:T(8,128)(2,1)S(1)}, u32[]{:S(2)}, u32[]{:S(2)}) collective-permute-start(bf16[40,2048]{1,0:T(8,128)(2,1)S(1)} %get-tuple-element.74), channel_id=1, source_target_pairs={{0,20},{2,22},{4,16},{6,18},{8,28},{10,30},{12,24},{14,26},{16,4},... | collective-permute-start | bytes 491528 | tf_op jit(solution)/shard_map/ppermute | solution.py:261
  350.9 27.1 %collective-permute-start.30 = (bf16[40,2048]{1,0:T(8,128)(2,1)S(1)}, bf16[40,2048]{1,0:T(8,128)(2,1)S(1)}, u32[]{:S(2)}, u32[]{:S(2)}) collective-permute-start(bf16[40,2048]{1,0:T(8,128)(2,1)S(1)} %get-tuple-element.71), channel_id=1, source_target_pairs={{0,16},{2,18},{4,20},{6,22},{8,24},{10,26},{12,28},{14,30},{16,0},... | collective-permute-start | bytes 491528 | tf_op jit(solution)/shard_map/ppermute | solution.py:261
  378.2 6.3 %collective-permute-start.34 = (bf16[40,2048]{1,0:T(8,128)(2,1)S(1)}, bf16[40,2048]{1,0:T(8,128)(2,1)S(1)}, u32[]{:S(2)}, u32[]{:S(2)}) collective-permute-start(bf16[40,2048]{1,0:T(8,128)(2,1)S(1)} %get-tuple-element.69), channel_id=1, source_target_pairs={{0,4},{2,6},{4,0},{6,2},{8,12},{10,14},{12,8},{14,10},{16,20},{18,... | collective-permute-start | bytes 491528 | tf_op jit(solution)/shard_map/ppermute | solution.py:261
  378.9 7.1 %collective-permute-start.35 = (bf16[40,2048]{1,0:T(8,128)(2,1)S(1)}, bf16[40,2048]{1,0:T(8,128)(2,1)S(1)}, u32[]{:S(2)}, u32[]{:S(2)}) collective-permute-start(bf16[40,2048]{1,0:T(8,128)(2,1)S(1)} %get-tuple-element.68), channel_id=1, source_target_pairs={{0,8},{2,10},{4,12},{6,14},{8,0},{10,2},{12,4},{14,6},{16,24},{18,... | collective-permute-start | bytes 491528 | tf_op jit(solution)/shard_map/ppermute | solution.py:261
  378.9 10.3 %collective-permute-start.36 = (bf16[40,2048]{1,0:T(8,128)(2,1)S(1)}, bf16[40,2048]{1,0:T(8,128)(2,1)S(1)}, u32[]{:S(2)}, u32[]{:S(2)}) collective-permute-start(bf16[40,2048]{1,0:T(8,128)(2,1)S(1)} %get-tuple-element.67), channel_id=1, source_target_pairs={{0,12},{2,14},{4,8},{6,10},{8,4},{10,6},{12,0},{14,2},{16,28},{18,... | collective-permute-start | bytes 491528 | tf_op jit(solution)/shard_map/ppermute | solution.py:261
  (35 other events, 224.1 us)

commit v4 on v3

--- a/solution.py
+++ b/solution.py
@@ -13,10 +13,12 @@
 TOPK = 2
 CAP = 40
 LANES = 128
+EIGHTHS = 8
 SUBLANES = 8
 RESET = 1e30
 LOG2E = math.log2(math.e)
 VMEM = 40 * 1024 * 1024
+SMALL_VMEM = 16 * 1024 * 1024
 
 
 def shifted(x, axis, by):
@@ -141,7 +143,7 @@
             pltpu.VMEM((tokens // SUBLANES, SUBLANES, width), jnp.float32),
             pltpu.VMEM((tokens // SUBLANES, SUBLANES, width), jnp.float32),
         ],
-        compiler_params=pltpu.CompilerParams(vmem_limit_bytes=VMEM),
+        compiler_params=pltpu.CompilerParams(vmem_limit_bytes=SMALL_VMEM),
         cost_estimate=pl.CostEstimate(
             flops=5 * tokens * NSTATE * channels,
             bytes_accessed=8 * tokens * channels,
@@ -160,12 +162,10 @@
     )(ends, decay_rate)
 
 
-def scan_gated(step, decay_rate, conved, gain, kept, carry, pick, skip_gain, gate_in, half):
-    tokens, channels = conved.shape[0], conved.shape[1] // 2
-    width = min(512, channels)
+def scan_gated(step, decay_rate, conved, gain, kept, carry, pick, skip_gain, gate_in, first, steps):
+    tokens, width = conved.shape[0], conved.shape[1] // EIGHTHS
+    channels = steps * width
     chunk = carry.shape[2]
-    steps = channels // width
-    first = half * steps
     part = lambda rows: pl.BlockSpec((rows, width), lambda i: (0, first + i))
     return pl.pallas_call(
         scan_kernel,
@@ -183,7 +183,7 @@
             pltpu.VMEM((tokens * NSTATE, width), jnp.bfloat16),
         ],
         out_shape=jax.ShapeDtypeStruct((tokens, channels), jnp.bfloat16),
-        compiler_params=pltpu.CompilerParams(vmem_limit_bytes=VMEM),
+        compiler_params=pltpu.CompilerParams(vmem_limit_bytes=SMALL_VMEM),
         cost_estimate=pl.CostEstimate(
             flops=7 * tokens * NSTATE * channels,
             bytes_accessed=12 * tokens * channels,
@@ -191,6 +191,43 @@
         ),
         name="scan_gated",
     )(step, decay_rate, conved, gain, kept, carry, pick, skip_gain[None, :], gate_in)
+
+
+def raise_kernel(*refs):
+    pieces, (gate_ref, up_ref, hidden_ref, rows_ref) = refs[:-4], refs[-4:]
+
+    @pl.when(pl.program_id(0) == 0)
+    def _():
+        for k, piece_ref in enumerate(pieces):
+            rows = piece_ref.shape[0]
+            rows_ref[k * rows : (k + 1) * rows] = piece_ref[...]
+
+    rows = rows_ref[...]
+    gate = jnp.dot(rows, gate_ref[0], preferred_element_type=jnp.float32)
+    up = jnp.dot(rows, up_ref[0], preferred_element_type=jnp.float32)
+    hidden_ref[...] = (jax.nn.silu(gate) * up).astype(hidden_ref.dtype)
+
+
+def raised(pieces, gate_weight, up_weight):
+    rows, depth = sum(piece.shape[0] for piece in pieces), pieces[0].shape[1]
+    width = gate_weight.shape[2]
+    tile = min(512, width)
+    weight = pl.BlockSpec((1, depth, tile), lambda i: (0, 0, i))
+    return pl.pallas_call(
+        raise_kernel,
+        grid=(width // tile,),
+        in_specs=[whole(piece.shape) for piece in pieces] + [weight, weight],
+        out_specs=pl.BlockSpec((rows, tile), lambda i: (0, i)),
+        out_shape=jax.ShapeDtypeStruct((rows, width), jnp.bfloat16),
+        scratch_shapes=[pltpu.VMEM((rows, depth), jnp.bfloat16)],
+        compiler_params=pltpu.CompilerParams(vmem_limit_bytes=56 * 1024 * 1024),
+        cost_estimate=pl.CostEstimate(
+            flops=4 * rows * depth * width,
+            bytes_accessed=4 * depth * width,
+            transcendentals=rows * width,
+        ),
+        name="raised",
+    )(*pieces, gate_weight, up_weight)
 
 
 def lower_kernel(shard_ref, hidden_ref, weight_ref, *out_refs):
@@ -290,7 +327,7 @@
                 (gather_matrix.shape[0], residual_in.shape[1]), jnp.bfloat16
             ),
         ],
-        compiler_params=pltpu.CompilerParams(vmem_limit_bytes=VMEM),
+        compiler_params=pltpu.CompilerParams(vmem_limit_bytes=SMALL_VMEM),
         name="hidden_and_packed",
     )(low, gather_matrix, residual_in, *pieces)
 
@@ -322,7 +359,9 @@
     shard = lax.axis_index("tp")
     shards = lax.axis_size("tp")
     low = groups // shards
-    columns = [out_proj] + [across(out_proj, low * high) for high in range(1, shards)]
+    first_steps = 3
+    first_rows = channels // EIGHTHS * first_steps
+    far_first = [across(out_proj[:first_rows], low * high) for high in range(1, shards)]
     conv_taps = conv_weight.shape[0]
     rim_rows = shifted(mixer_in[tokens - (conv_taps - 1) :], "loop", 1)
     extended = jnp.concatenate([rim_rows, mixer_in], axis=0)
@@ -360,20 +399,24 @@
     step_size, end_state = scan_end(
         low_rank, step_proj, step_bias, decay_rate, conved, gain, kept, groups
     )
+    end_state, far_first = lax.optimization_barrier((end_state, far_first))
     ends = lax.all_to_all(end_state, "loop", 0, 0, tiled=True)
     chunk = channels // groups
     own_rates = lax.dynamic_slice_in_dim(decay_rate, position * chunk, chunk, 1)
     carry = lax.all_to_all(carries(ends, own_rates), "loop", 0, 0, tiled=True)
+    later_rows, carry = lax.optimization_barrier((out_proj[first_rows:], carry))
+    far_later = [across(later_rows, low * high) for high in range(1, shards)]
     own_low, own_high = position % low, position // low
     tokens_of = []
-    for half in range(2):
+    for first, steps in ((0, first_steps), (first_steps, EIGHTHS - first_steps)):
         gated = scan_gated(
-            step_size, decay_rate, conved, gain, kept, carry, pick, skip_gain, gate_in, half
+            step_size, decay_rate, conved, gain, kept, carry, pick, skip_gain, gate_in, first,
+            steps,
         )
         tokens_of.append(
             {m: gated if m == 0 else across(gated, m) for m in (0, 2, 4) if m < low}
         )
-    columns[1:], tokens_of = lax.optimization_barrier((columns[1:], tokens_of))
+    far_later, tokens_of = lax.optimization_barrier((far_later, tokens_of))
     for half, got in enumerate(tokens_of):
         for m in range(6, low, 2):
             one = m & -m
@@ -385,14 +428,14 @@
     all_tokens = [
         jnp.concatenate([got[m] for m in range(0, low, 2)], axis=0) for got in tokens_of
     ]
-    depth = channels // 2
+    blocks = [(out_proj[:first_rows], out_proj[first_rows:])] + list(zip(far_first, far_later))
     mixes = []
-    for block in columns:
-        pair = jnp.concatenate([block, across(block, 1)], axis=1)
-        mixes.append(
-            jnp.dot(all_tokens[0], pair[:depth], preferred_element_type=jnp.float32)
-            + jnp.dot(all_tokens[1], pair[depth:], preferred_element_type=jnp.float32)
-        )
+    for block in blocks:
+        mix = 0.0
+        for some_tokens, part in zip(all_tokens, block):
+            pair = jnp.concatenate([part, across(part, 1)], axis=1)
+            mix = mix + jnp.dot(some_tokens, pair, preferred_element_type=jnp.float32)
+        mixes.append(mix)
 
     def for_shard(t):
         mix = mixes[0]
@@ -442,12 +485,8 @@
         gathered(teams_swapped(packed[first : first + near], first, members), "tp", shard, 1)
         for first in (near, 0)
     ]
-    slot_rows = jnp.concatenate(
-        parts + [from_member(by)(part) for by in range(1, members) for part in parts], axis=0
-    )
-    gate_value = jnp.dot(slot_rows, gate_weight[0], preferred_element_type=jnp.float32)
-    up_value = jnp.dot(slot_rows, up_weight[0], preferred_element_type=jnp.float32)
-    hidden = (jax.nn.silu(gate_value) * up_value).astype(jnp.bfloat16)
+    pieces = parts + [from_member(by)(part) for by in range(1, members) for part in parts]
+    hidden = raised(pieces, gate_weight, up_weight)
 
     def member_sum(outs):
         total = outs[0].astype(jnp.float32)

time: 392 us -> 364 us (0.929)
  matrix products: 57.5 us -> 12.5 us
  Pallas kernels: 49.6 us -> 90.1 us
  waiting for transfers between devices: 184 us -> 149 us
  starting transfers between devices: 51 us -> 67.5 us
    all_to_all x1, waiting for transfers between devices: 71 us -> 9.44 us  [per_device(): ends = lax.all_to_all(end_state, 'loop', 0, 0, tiled=True)]
    dot_general x6 -> x4, matrix products: 52.8 us -> 8.62 us  [per_device(): mix = mix + jnp.dot(some_tokens, pair, preferred_element_type=jnp.float32)]
    ppermute x12 -> x15, waiting for transfers between devices: 19.6 us -> 62.1 us  [across(): lax.ppermute(x, 'loop', [(i, i ^ mask) for i in range(lax.axis_size('loop...]
    pallas_call x0 -> x1, Pallas kernels: none -> 39.7 us  [raised(): pl.pallas_call(raise_kernel, grid=(width // tile,), in_specs=[whole(piece...]
    ppermute x14, starting transfers between devices: 18.4 us -> 31.7 us  [teams_swapped(): out.append(lax.ppermute(x[k], 'loop', pairs))]
    ppermute x14, waiting for transfers between devices: 49 us -> 38.9 us  [teams_swapped(): out.append(lax.ppermute(x[k], 'loop', pairs))]
    slice x1 -> x4, local copies, waits for them, and re-layouts: 0.21 us -> 5.67 us  [the longest x1 2.56 us: per_device(): later_rows, carry = lax.optimization_barrier((out_proj[first_rows:], carry))]
    unnamed x71 -> x79, local copies, waits for them, and re-layouts: 25 us -> 19.7 us
  transfers between devices with their start and end apart: 39 -> 42, of which waited for: 27 -> 25; matrix products, arithmetic and copies ran while one was open for 6% -> 8% of each run, Pallas kernels for 10% -> 10%
where the time goes in v4:
time: 364 us; the launch traced here: 363 us
  waiting for transfers between devices  149 us (41%)
  Pallas kernels  90.1 us (25%)
  starting transfers between devices  67.5 us (19%)
  local copies, waits for them, and re-layouts  33.3 us (9%)
  matrix products  12.5 us (3%)
  other arithmetic  8.76 us (2%)
    ppermute x15, waiting for transfers between devices, across(): lax.ppermute(x, 'loop', [(i, i ^ mask) for i in range(lax.axis_size('loop...  62.1 us
    pallas_call x1, Pallas kernels, raised(): pl.pallas_call(raise_kernel, grid=(width // tile,), in_specs=[whole(piece...  39.7 us
    ppermute x14, waiting for transfers between devices, teams_swapped(): out.append(lax.ppermute(x[k], 'loop', pairs))  38.9 us
    ppermute x14, starting transfers between devices, teams_swapped(): out.append(lax.ppermute(x[k], 'loop', pairs))  31.7 us
    ppermute x6, waiting for transfers between devices, rotated(): return lax.ppermute(x, axis, [(i, (i + by) % size) for i in range(size)])  26.1 us
    pallas_call x2, Pallas kernels, lowered(): pl.pallas_call(lower_kernel, grid_spec=pltpu.PrefetchScalarGridSpec(num_s...  22.8 us
    unnamed x79, local copies, waits for them, and re-layouts  19.7 us
    pallas_call x2, Pallas kernels, scan_gated(): pl.pallas_call(scan_kernel, grid=(steps,), in_specs=[part(tokens), part(N...  14.1 us
  transfers between devices with their start and end apart: 42, of which 25 were waited for; matrix products, arithmetic and copies ran while one was open for 8% of the time, Pallas kernels for 10%

profile of v4, /device:TPU:0, one launch (start us, length us, event | category | flops | bytes accessed | tf_op | source)
XLA Modules:
  0.0 362.6 jit_solution(3462702310296489677)
XLA Ops:
  5.6 3.6 collective-permute-start.2
  17.7 2.6 collective-permute-done.1
  23.2 11.2 %scan_end.1 = (f32[128,4096]{1,0:T(8,128)S(1)}, bf16[16,32,256]{2,1,0:T(8,128)(2,1)}) custom-call(bf16[128,256]{1,0:T(8,128)(2,1)S(1)} %slice.204.low_ref, bf16[256,4096]{1,0:T(8,128)(2,1)S(1)} %copy-done.14, f32[1,4096]{1,0:T(1,128)S(1)} %bitcast.32, f32[16,4096]{1,0:T(8,128)S(1)} %copy-done.10, bf16[128,4096]{1,0:T(8,128)(2,1)S(1)} %multiply_convert_fusion.conved_ref, ...), custom_call_target="tpu_custom_call" | custom-call | flops 41943040 | bytes 4194304 | tf_op jit(solution)/shard_map/scan_end/pallas_call | solution.py:127
  35.7 8.1 %collective-permute-done.2 = bf16[1536,256]{1,0:T(8,128)(2,1)} collective-permute-done((bf16[1536,256]{1,0:T(8,128)(2,1)}, bf16[1536,256]{1,0:T(8,128)(2,1)}, u32[]{:S(2)}, u32[]{:S(2)}) %collective-permute-start.2) | collective-permute-done | bytes 786464 | tf_op jit(solution)/shard_map/ppermute | solution.py:286
  43.8 6.1 %all-to-all-start = ((bf16[16,32,256]{2,1,0:T(8,128)(2,1)}), bf16[16,32,256]{2,1,0:T(8,128)(2,1)S(1)}, u32[]{:S(2)}, u32[]{:S(2)}) async-start(bf16[16,32,256]{2,1,0:T(8,128)(2,1)} %get-tuple-element.33), calls=%async_computation | async-start | bytes 524288 | tf_op jit(solution)/shard_map/all_to_all | solution.py:403
  50.6 9.4 %all-to-all-done.ends_ref = bf16[16,32,256]{2,1,0:T(8,128)(2,1)S(1)} async-done(((bf16[16,32,256]{2,1,0:T(8,128)(2,1)}), bf16[16,32,256]{2,1,0:T(8,128)(2,1)S(1)}, u32[]{:S(2)}, u32[]{:S(2)}) %all-to-all-start) | async-done | bytes 262176 | tf_op jit(solution)/shard_map/all_to_all | solution.py:403
  62.4 3.7 %all-to-all-start.1 = ((bf16[16,16,256]{2,1,0:T(8,128)(2,1)}), bf16[16,16,256]{2,1,0:T(8,128)(2,1)S(1)}, u32[]{:S(2)}, u32[]{:S(2)}) async-start(bf16[16,16,256]{2,1,0:T(8,128)(2,1)} %carries.1), calls=%async_computation.1 | async-start | bytes 262144 | tf_op jit(solution)/shard_map/all_to_all | solution.py:406
  66.1 2.6 slice.160
  68.7 5.1 %all-to-all-done.1.carry_ref = bf16[16,16,256]{2,1,0:T(8,128)(2,1)S(1)} async-done(((bf16[16,16,256]{2,1,0:T(8,128)(2,1)}), bf16[16,16,256]{2,1,0:T(8,128)(2,1)S(1)}, u32[]{:S(2)}, u32[]{:S(2)}) %all-to-all-start.1) | async-done | bytes 131104 | tf_op jit(solution)/shard_map/all_to_all | solution.py:406
  77.2 9.1 %scan_gated.3 = bf16[128,2560]{1,0:T(8,128)(2,1)} custom-call(f32[128,4096]{1,0:T(8,128)S(1)} %copy-done.3, f32[16,4096]{1,0:T(8,128)S(1)} %copy-done.11, bf16[128,4096]{1,0:T(8,128)(2,1)S(1)} %multiply_convert_fusion.conved_ref, f32[128,16,128]{2,1,0:T(8,128)S(1)} %broadcast_in_dim.48.gain_ref, f32[128,1]{1,0:T(8,128)S(1)} %copy.51.kept_ref, ...), custom_call_target="tpu_custom_call" | custom-call | flops 36700160 | bytes 3932160 | tf_op jit(solution)/shard_map/scan_gated/pallas_call | solution.py:170
  93.2 5.0 %scan_gated.2 = bf16[128,1536]{1,0:T(8,128)(2,1)S(1)} custom-call(f32[128,4096]{1,0:T(8,128)S(1)} %copy-done.4, f32[16,4096]{1,0:T(8,128)S(1)} %copy-done.12, bf16[128,4096]{1,0:T(8,128)(2,1)S(1)} %multiply_convert_fusion.conved_ref, f32[128,16,128]{2,1,0:T(8,128)S(1)} %broadcast_in_dim.48.gain_ref, f32[128,1]{1,0:T(8,128)S(1)} %copy.51.kept_ref, ...), custom_call_target="tpu_custom_call" | custom-call | flops 22020096 | bytes 2359296 | tf_op jit(solution)/shard_map/scan_gated/pallas_call | solution.py:170
  101.6 9.8 %collective-permute-done.4 = bf16[128,1536]{1,0:T(8,128)(2,1)S(1)} collective-permute-done((bf16[128,1536]{1,0:T(8,128)(2,1)S(1)}, bf16[128,1536]{1,0:T(8,128)(2,1)S(1)}, u32[]{:S(2)}, u32[]{:S(2)}) %collective-permute-start.4) | collective-permute-done | bytes 393248 | tf_op jit(solution)/shard_map/ppermute | solution.py:286
  111.4 28.1 %collective-permute-done.5 = bf16[128,1536]{1,0:T(8,128)(2,1)S(1)} collective-permute-done((bf16[128,1536]{1,0:T(8,128)(2,1)S(1)}, bf16[128,1536]{1,0:T(8,128)(2,1)S(1)}, u32[]{:S(2)}, u32[]{:S(2)}) %collective-permute-start.5) | collective-permute-done | bytes 393248 | tf_op jit(solution)/shard_map/ppermute | solution.py:286
  145.2 8.3 %collective-permute-done.8 = bf16[128,1536]{1,0:T(8,128)(2,1)S(1)} collective-permute-done((bf16[128,1536]{1,0:T(8,128)(2,1)S(1)}, bf16[128,1536]{1,0:T(8,128)(2,1)S(1)}, u32[]{:S(2)}, u32[]{:S(2)}) %collective-permute-start.8) | collective-permute-done | bytes 393248 | tf_op jit(solution)/shard_map/ppermute | solution.py:286
  153.5 4.5 %collective-permute-done.10 = bf16[128,2560]{1,0:T(8,128)(2,1)S(1)} collective-permute-done((bf16[128,2560]{1,0:T(8,128)(2,1)}, bf16[128,2560]{1,0:T(8,128)(2,1)S(1)}, u32[]{:S(2)}, u32[]{:S(2)}) %collective-permute-start.10) | collective-permute-done | bytes 655392 | tf_op jit(solution)/shard_map/ppermute | solution.py:286
  161.8 2.9 fusion
  168.6 11.2 %collective-permute-done.14 = bf16[512,512]{1,0:T(8,128)(2,1)S(1)} collective-permute-done((bf16[512,512]{1,0:T(8,128)(2,1)S(1)}, bf16[512,512]{1,0:T(8,128)(2,1)S(1)}, u32[]{:S(2)}, u32[]{:S(2)}) %collective-permute-start.14) | collective-permute-done | bytes 524320 | tf_op jit(solution)/shard_map/ppermute | solution.py:32
  207.6 7.7 %collective-permute-done.18 = bf16[40,2048]{1,0:T(8,128)(2,1)S(1)} collective-permute-done((bf16[40,2048]{1,0:T(8,128)(2,1)S(1)}, bf16[40,2048]{1,0:T(8,128)(2,1)S(1)}, u32[]{:S(2)}, u32[]{:S(2)}) %collective-permute-start.18) | collective-permute-done | bytes 163872 | tf_op jit(solution)/shard_map/ppermute | solution.py:298
  215.4 4.6 %collective-permute-done.19 = bf16[40,2048]{1,0:T(8,128)(2,1)S(1)} collective-permute-done((bf16[40,2048]{1,0:T(8,128)(2,1)}, bf16[40,2048]{1,0:T(8,128)(2,1)S(1)}, u32[]{:S(2)}, u32[]{:S(2)}) %collective-permute-start.19) | collective-permute-done | bytes 163872 | tf_op jit(solution)/shard_map/ppermute | solution.py:298
  223.2 8.5 %collective-permute-done.22 = bf16[160,2048]{1,0:T(8,128)(2,1)} collective-permute-done((bf16[160,2048]{1,0:T(8,128)(2,1)S(1)}, bf16[160,2048]{1,0:T(8,128)(2,1)}, u32[]{:S(2)}, u32[]{:S(2)}) %collective-permute-start.22) | collective-permute-done | bytes 655392 | tf_op jit(solution)/shard_map/ppermute | solution.py:32
  232.9 3.0 collective-permute-done.27.refs_2_
  237.1 39.7 %raised.1.hidden_ref = bf16[640,3072]{1,0:T(8,128)(2,1)} custom-call(bf16[160,4096]{1,0:T(8,128)(2,1)} %copy-done.19, bf16[160,4096]{1,0:T(8,128)(2,1)} %copy-done.18, bf16[160,4096]{1,0:T(8,128)(2,1)} %copy-done.31, bf16[160,4096]{1,0:T(8,128)(2,1)} %copy-done.30, bf16[1,4096,3072]{2,1,0:T(8,128)(2,1)} %refs_4_.1, bf16[1,4096,3072]{2,1,0:T(8,128)(2,1)} %refs_5_.1), custom_call_target="tpu_custom_call" | custom-call | flops 32212254720 | bytes 50331648 | tf_op jit(solution)/shard_map/raised/pallas_call | solution.py:216
  278.9 11.4 %lowered.2 = (bf16[320,2048]{1,0:T(8,128)(2,1)S(1)}, bf16[320,2048]{1,0:T(8,128)(2,1)S(1)}) custom-call(s32[1]{0:T(128)} %bitcast.12.shard_ref, bf16[640,3072]{1,0:T(8,128)(2,1)S(1)} %copy-done.16, bf16[1,3072,4096]{2,1,0:T(8,128)(2,1)} %weight_ref.3), custom_call_target="tpu_custom_call" | custom-call | flops 8053063680 | bytes 12582912 | tf_op jit(solution)/shard_map/lowered/pallas_call | solution.py:245
  290.5 2.9 collective-permute-done.29
  295.7 11.4 %lowered.3 = (bf16[320,2048]{1,0:T(8,128)(2,1)S(1)}, bf16[320,2048]{1,0:T(8,128)(2,1)S(1)}) custom-call(s32[1]{0:T(128)} %bitcast.13.shard_ref, bf16[640,3072]{1,0:T(8,128)(2,1)S(1)} %copy-done.16, bf16[1,3072,4096]{2,1,0:T(8,128)(2,1)} %weight_ref.3), custom_call_target="tpu_custom_call" | custom-call | flops 8053063680 | bytes 12582912 | tf_op jit(solution)/shard_map/lowered/pallas_call | solution.py:245
  307.1 3.8 %collective-permute-done.30 = bf16[160,2048]{1,0:T(8,128)(2,1)S(1)} collective-permute-done((bf16[160,2048]{1,0:T(8,128)(2,1)S(1)}, bf16[160,2048]{1,0:T(8,128)(2,1)S(1)}, u32[]{:S(2)}, u32[]{:S(2)}) %collective-permute-start.30) | collective-permute-done | bytes 655392 | tf_op jit(solution)/shard_map/ppermute | solution.py:32
  314.7 7.3 %collective-permute-start.33 = (bf16[40,2048]{1,0:T(8,128)(2,1)S(1)}, bf16[40,2048]{1,0:T(8,128)(2,1)S(1)}, u32[]{:S(2)}, u32[]{:S(2)}) collective-permute-start(bf16[40,2048]{1,0:T(8,128)(2,1)S(1)} %get-tuple-element.79), channel_id=1, source_target_pairs={{0,16},{2,18},{4,20},{6,22},{8,24},{10,26},{12,28},{14,30},{16,0},... | collective-permute-start | bytes 491528 | tf_op jit(solution)/shard_map/ppermute | solution.py:298
  324.0 2.8 collective-permute-start.36
  326.8 14.2 %collective-permute-done.33 = bf16[40,2048]{1,0:T(8,128)(2,1)S(1)} collective-permute-done((bf16[40,2048]{1,0:T(8,128)(2,1)S(1)}, bf16[40,2048]{1,0:T(8,128)(2,1)S(1)}, u32[]{:S(2)}, u32[]{:S(2)}) %collective-permute-start.33) | collective-permute-done | bytes 163872 | tf_op jit(solution)/shard_map/ppermute | solution.py:298
  341.0 3.5 collective-permute-done.34
  346.4 7.1 %collective-permute-start.38 = (bf16[40,2048]{1,0:T(8,128)(2,1)S(1)}, bf16[40,2048]{1,0:T(8,128)(2,1)S(1)}, u32[]{:S(2)}, u32[]{:S(2)}) collective-permute-start(bf16[40,2048]{1,0:T(8,128)(2,1)S(1)} %get-tuple-element.76), channel_id=1, source_target_pairs={{0,8},{2,10},{4,12},{6,14},{8,0},{10,2},{12,4},{14,6},{16,24},{18,... | collective-permute-start | bytes 491528 | tf_op jit(solution)/shard_map/ppermute | solution.py:298
  353.5 5.1 %collective-permute-done.38 = bf16[40,2048]{1,0:T(8,128)(2,1)S(1)} collective-permute-done((bf16[40,2048]{1,0:T(8,128)(2,1)S(1)}, bf16[40,2048]{1,0:T(8,128)(2,1)S(1)}, u32[]{:S(2)}, u32[]{:S(2)}) %collective-permute-start.38) | collective-permute-done | bytes 163872 | tf_op jit(solution)/shard_map/ppermute | solution.py:298
  (201 shorter events, 97.0 us)
Async XLA Ops:
  5.6 38.2 %collective-permute-start.2 = (bf16[1536,256]{1,0:T(8,128)(2,1)}, bf16[1536,256]{1,0:T(8,128)(2,1)}, u32[]{:S(2)}, u32[]{:S(2)}) collective-permute-start(bf16[1536,256]{1,0:T(8,128)(2,1)} %slice.173), channel_id=1, source_target_pairs={{0,16},{2,18},{4,20},{6,22},{8,24},{10,26},{12,28},{14,30},{16,0},... | collective-permute-start | bytes 2359304 | tf_op jit(solution)/shard_map/ppermute | solution.py:286
  43.8 16.1 %all-to-all-start = ((bf16[16,32,256]{2,1,0:T(8,128)(2,1)}), bf16[16,32,256]{2,1,0:T(8,128)(2,1)S(1)}, u32[]{:S(2)}, u32[]{:S(2)}) async-start(bf16[16,32,256]{2,1,0:T(8,128)(2,1)} %get-tuple-element.33), calls=%async_computation | async-start | bytes 524288 | tf_op jit(solution)/shard_map/all_to_all | solution.py:403
  62.4 11.4 %all-to-all-start.1 = ((bf16[16,16,256]{2,1,0:T(8,128)(2,1)}), bf16[16,16,256]{2,1,0:T(8,128)(2,1)S(1)}, u32[]{:S(2)}, u32[]{:S(2)}) async-start(bf16[16,16,256]{2,1,0:T(8,128)(2,1)} %carries.1), calls=%async_computation.1 | async-start | bytes 262144 | tf_op jit(solution)/shard_map/all_to_all | solution.py:406
  73.8 66.2 %collective-permute-start.3 = (bf16[2560,256]{1,0:T(8,128)(2,1)}, bf16[2560,256]{1,0:T(8,128)(2,1)}, u32[]{:S(2)}, u32[]{:S(2)}) collective-permute-start(bf16[2560,256]{1,0:T(8,128)(2,1)} %slice.160), channel_id=1, source_target_pairs={{0,16},{2,18},{4,20},{6,22},{8,24},{10,26},{12,28},{14,30},{16,0},... | collective-permute-start | bytes 3932168 | tf_op jit(solution)/shard_map/ppermute | solution.py:286
  86.3 53.2 %collective-permute-start.6 = (bf16[128,2560]{1,0:T(8,128)(2,1)}, bf16[128,2560]{1,0:T(8,128)(2,1)}, u32[]{:S(2)}, u32[]{:S(2)}) collective-permute-start(bf16[128,2560]{1,0:T(8,128)(2,1)} %scan_gated.3), channel_id=1, source_target_pairs={{0,4},{2,6},{4,0},{6,2},{8,12},{10,14},{12,8},{14,10},{16,20},{18,... | collective-permute-start | bytes 1966088 | tf_op jit(solution)/shard_map/ppermute | solution.py:286
  86.6 53.4 %collective-permute-start.7 = (bf16[128,2560]{1,0:T(8,128)(2,1)}, bf16[128,2560]{1,0:T(8,128)(2,1)}, u32[]{:S(2)}, u32[]{:S(2)}) collective-permute-start(bf16[128,2560]{1,0:T(8,128)(2,1)} %scan_gated.3), channel_id=1, source_target_pairs={{0,8},{2,10},{4,12},{6,14},{8,0},{10,2},{12,4},{14,6},{16,24},{18,... | collective-permute-start | bytes 1966088 | tf_op jit(solution)/shard_map/ppermute | solution.py:286
  98.2 13.1 %collective-permute-start.4 = (bf16[128,1536]{1,0:T(8,128)(2,1)S(1)}, bf16[128,1536]{1,0:T(8,128)(2,1)S(1)}, u32[]{:S(2)}, u32[]{:S(2)}) collective-permute-start(bf16[128,1536]{1,0:T(8,128)(2,1)S(1)} %scan_gated.2), channel_id=1, source_target_pairs={{0,4},{2,6},{4,0},{6,2},{8,12},{10,14},{12,8},{14,10},{16,20},{18,... | collective-permute-start | bytes 1179656 | tf_op jit(solution)/shard_map/ppermute | solution.py:286
  99.5 39.9 %collective-permute-start.5 = (bf16[128,1536]{1,0:T(8,128)(2,1)S(1)}, bf16[128,1536]{1,0:T(8,128)(2,1)S(1)}, u32[]{:S(2)}, u32[]{:S(2)}) collective-permute-start(bf16[128,1536]{1,0:T(8,128)(2,1)S(1)} %scan_gated.2), channel_id=1, source_target_pairs={{0,8},{2,10},{4,12},{6,14},{8,0},{10,2},{12,4},{14,6},{16,24},{18,... | collective-permute-start | bytes 1179656 | tf_op jit(solution)/shard_map/ppermute | solution.py:286
  111.4 46.7 %collective-permute-start.13 = (bf16[2560,256]{1,0:T(8,128)(2,1)}, bf16[2560,256]{1,0:T(8,128)(2,1)S(1)}, u32[]{:S(2)}, u32[]{:S(2)}) collective-permute-start(bf16[2560,256]{1,0:T(8,128)(2,1)} %slice.160), channel_id=1, source_target_pairs={{0,2},{2,0},{4,6},{6,4},{8,10},{10,8},{12,14},{14,12},{16,18},{18,... | collective-permute-start | bytes 3932168 | tf_op jit(solution)/shard_map/ppermute | solution.py:286
  139.5 20.2 %collective-permute-start.12 = (bf16[1536,256]{1,0:T(8,128)(2,1)}, bf16[1536,256]{1,0:T(8,128)(2,1)S(1)}, u32[]{:S(2)}, u32[]{:S(2)}) collective-permute-start(bf16[1536,256]{1,0:T(8,128)(2,1)} %slice.173), channel_id=1, source_target_pairs={{0,2},{2,0},{4,6},{6,4},{8,10},{10,8},{12,14},{14,12},{16,18},{18,... | collective-permute-start | bytes 2359304 | tf_op jit(solution)/shard_map/ppermute | solution.py:286
  139.5 25.2 %collective-permute-start.9 = (bf16[1536,256]{1,0:T(8,128)(2,1)}, bf16[1536,256]{1,0:T(8,128)(2,1)S(1)}, u32[]{:S(2)}, u32[]{:S(2)}) collective-permute-start(bf16[1536,256]{1,0:T(8,128)(2,1)} %collective-permute-done.2), channel_id=1, source_target_pairs={{0,2},{2,0},{4,6},{6,4},{8,10},{10,8},{12,14},{14,12},{16,18},{18,... | collective-permute-start | bytes 2359304 | tf_op jit(solution)/shard_map/ppermute | solution.py:286
  141.1 16.9 %collective-permute-start.10 = (bf16[128,2560]{1,0:T(8,128)(2,1)}, bf16[128,2560]{1,0:T(8,128)(2,1)S(1)}, u32[]{:S(2)}, u32[]{:S(2)}) collective-permute-start(bf16[128,2560]{1,0:T(8,128)(2,1)} %collective-permute-done.7), channel_id=1, source_target_pairs={{0,4},{2,6},{4,0},{6,2},{8,12},{10,14},{12,8},{14,10},{16,20},{18,... | collective-permute-start | bytes 1966088 | tf_op jit(solution)/shard_map/ppermute | solution.py:286
  142.7 10.8 %collective-permute-start.8 = (bf16[128,1536]{1,0:T(8,128)(2,1)S(1)}, bf16[128,1536]{1,0:T(8,128)(2,1)S(1)}, u32[]{:S(2)}, u32[]{:S(2)}) collective-permute-start(bf16[128,1536]{1,0:T(8,128)(2,1)S(1)} %collective-permute-done.4), channel_id=1, source_target_pairs={{0,8},{2,10},{4,12},{6,14},{8,0},{10,2},{12,4},{14,6},{16,24},{18,... | collective-permute-start | bytes 1179656 | tf_op jit(solution)/shard_map/ppermute | solution.py:286
  153.5 8.3 %collective-permute-start.11 = (bf16[2560,256]{1,0:T(8,128)(2,1)}, bf16[2560,256]{1,0:T(8,128)(2,1)S(1)}, u32[]{:S(2)}, u32[]{:S(2)}) collective-permute-start(bf16[2560,256]{1,0:T(8,128)(2,1)} %collective-permute-done.3), channel_id=1, source_target_pairs={{0,2},{2,0},{4,6},{6,4},{8,10},{10,8},{12,14},{14,12},{16,18},{18,... | collective-permute-start | bytes 3932168 | tf_op jit(solution)/shard_map/ppermute | solution.py:286
  166.8 13.1 %collective-permute-start.14 = (bf16[512,512]{1,0:T(8,128)(2,1)S(1)}, bf16[512,512]{1,0:T(8,128)(2,1)S(1)}, u32[]{:S(2)}, u32[]{:S(2)}) collective-permute-start(bf16[512,512]{1,0:T(8,128)(2,1)S(1)} %get-tuple-element.92), channel_id=1, source_target_pairs={{0,1},{1,0},{2,3},{3,2},{4,5},{5,4},{6,7},{7,6},{8,9},{9,8},{10,11... | collective-permute-start | bytes 1572872 | tf_op jit(solution)/shard_map/ppermute | solution.py:32
  192.9 8.4 %collective-permute-start.24 = (bf16[40,2048]{1,0:T(8,128)(2,1)S(1)}, bf16[40,2048]{1,0:T(8,128)(2,1)S(1)}, u32[]{:S(2)}, u32[]{:S(2)}) collective-permute-start(bf16[40,2048]{1,0:T(8,128)(2,1)S(1)} %get-tuple-element.69), channel_id=1, source_target_pairs={{0,8},{2,10},{4,12},{6,14},{8,0},{10,2},{12,4},{14,6},{16,24},{18,... | collective-permute-start | bytes 491528 | tf_op jit(solution)/shard_map/ppermute | solution.py:298
  193.5 10.6 %collective-permute-start.25 = (bf16[40,2048]{1,0:T(8,128)(2,1)S(1)}, bf16[40,2048]{1,0:T(8,128)(2,1)S(1)}, u32[]{:S(2)}, u32[]{:S(2)}) collective-permute-start(bf16[40,2048]{1,0:T(8,128)(2,1)S(1)} %get-tuple-element.68), channel_id=1, source_target_pairs={{0,12},{2,14},{4,8},{6,10},{8,4},{10,6},{12,0},{14,2},{16,28},{18,... | collective-permute-start | bytes 491528 | tf_op jit(solution)/shard_map/ppermute | solution.py:298
  194.9 20.5 %collective-permute-start.18 = (bf16[40,2048]{1,0:T(8,128)(2,1)S(1)}, bf16[40,2048]{1,0:T(8,128)(2,1)S(1)}, u32[]{:S(2)}, u32[]{:S(2)}) collective-permute-start(bf16[40,2048]{1,0:T(8,128)(2,1)S(1)} %get-tuple-element.74), channel_id=1, source_target_pairs={{0,16},{2,18},{4,20},{6,22},{8,24},{10,26},{12,28},{14,30},{16,0},... | collective-permute-start | bytes 491528 | tf_op jit(solution)/shard_map/ppermute | solution.py:298
  196.9 23.2 %collective-permute-start.19 = (bf16[40,2048]{1,0:T(8,128)(2,1)}, bf16[40,2048]{1,0:T(8,128)(2,1)S(1)}, u32[]{:S(2)}, u32[]{:S(2)}) collective-permute-start(bf16[40,2048]{1,0:T(8,128)(2,1)} %get-tuple-element.73), channel_id=1, source_target_pairs={{0,20},{2,22},{4,16},{6,18},{8,28},{10,30},{12,24},{14,26},{16,4},... | collective-permute-start | bytes 491528 | tf_op jit(solution)/shard_map/ppermute | solution.py:298
  198.7 21.3 %collective-permute-start.20 = (bf16[40,2048]{1,0:T(8,128)(2,1)S(1)}, bf16[40,2048]{1,0:T(8,128)(2,1)S(1)}, u32[]{:S(2)}, u32[]{:S(2)}) collective-permute-start(bf16[40,2048]{1,0:T(8,128)(2,1)S(1)} %get-tuple-element.72), channel_id=1, source_target_pairs={{0,24},{2,26},{4,28},{6,30},{8,16},{10,18},{12,20},{14,22},{16,8},... | collective-permute-start | bytes 491528 | tf_op jit(solution)/shard_map/ppermute | solution.py:298
  201.3 18.8 %collective-permute-start.21 = (bf16[40,2048]{1,0:T(8,128)(2,1)S(1)}, bf16[40,2048]{1,0:T(8,128)(2,1)S(1)}, u32[]{:S(2)}, u32[]{:S(2)}) collective-permute-start(bf16[40,2048]{1,0:T(8,128)(2,1)S(1)} %get-tuple-element.71), channel_id=1, source_target_pairs={{0,28},{2,30},{4,24},{6,26},{8,20},{10,22},{12,16},{14,18},{16,12}... | collective-permute-start | bytes 491528 | tf_op jit(solution)/shard_map/ppermute | solution.py:298
  206.0 15.9 %collective-permute-start.26 = (bf16[160,2048]{1,0:T(8,128)(2,1)S(1)}, bf16[160,2048]{1,0:T(8,128)(2,1)}, u32[]{:S(2)}, u32[]{:S(2)}) collective-permute-start(bf16[160,2048]{1,0:T(8,128)(2,1)S(1)} %get-tuple-element.83), channel_id=1, source_target_pairs={{0,1},{1,0},{2,3},{3,2},{4,5},{5,4},{6,7},{7,6},{8,9},{9,8},{10,11... | collective-permute-start | bytes 1966088 | tf_op jit(solution)/shard_map/ppermute | solution.py:32
  220.1 11.5 %collective-permute-start.22 = (bf16[160,2048]{1,0:T(8,128)(2,1)S(1)}, bf16[160,2048]{1,0:T(8,128)(2,1)}, u32[]{:S(2)}, u32[]{:S(2)}) collective-permute-start(bf16[160,2048]{1,0:T(8,128)(2,1)S(1)} %constant_dynamic-update-slice_fusion.8), channel_id=1, source_target_pairs={{0,1},{1,0},{2,3},{3,2},{4,5},{5,4},{6,7},{7,6},{8,9},{9,8},{10,11... | collective-permute-start | bytes 1966088 | tf_op jit(solution)/shard_map/ppermute | solution.py:32
  223.1 9.8 %collective-permute-start.28 = (bf16[160,4096]{1,0:T(8,128)(2,1)S(1)}, bf16[160,4096]{1,0:T(8,128)(2,1)S(1)}, u32[]{:S(2)}, u32[]{:S(2)}) collective-permute-start(bf16[160,4096]{1,0:T(8,128)(2,1)S(1)} %constant_dynamic-update-slice_fusion.16.refs_1_), channel_id=1, source_target_pairs={{0,2},{2,0},{4,6},{6,4},{8,10},{10,8},{12,14},{14,12},{16,18},{18,... | collective-permute-start | bytes 3932168 | tf_op jit(solution)/shard_map/ppermute | solution.py:482
  294.1 16.8 %collective-permute-start.30 = (bf16[160,2048]{1,0:T(8,128)(2,1)S(1)}, bf16[160,2048]{1,0:T(8,128)(2,1)S(1)}, u32[]{:S(2)}, u32[]{:S(2)}) collective-permute-start(bf16[160,2048]{1,0:T(8,128)(2,1)S(1)} %get-tuple-element.66), channel_id=1, source_target_pairs={{0,1},{1,0},{2,3},{3,2},{4,5},{5,4},{6,7},{7,6},{8,9},{9,8},{10,11... | collective-permute-start | bytes 1966088 | tf_op jit(solution)/shard_map/ppermute | solution.py:32
  310.9 33.7 %collective-permute-start.32 = (bf16[160,2048]{1,0:T(8,128)(2,1)S(1)}, bf16[160,2048]{1,0:T(8,128)(2,1)S(1)}, u32[]{:S(2)}, u32[]{:S(2)}) collective-permute-start(bf16[160,2048]{1,0:T(8,128)(2,1)S(1)} %get-tuple-element.55), channel_id=1, source_target_pairs={{0,1},{1,0},{2,3},{3,2},{4,5},{5,4},{6,7},{7,6},{8,9},{9,8},{10,11... | collective-permute-start | bytes 1966088 | tf_op jit(solution)/shard_map/ppermute | solution.py:32
  314.7 26.3 %collective-permute-start.33 = (bf16[40,2048]{1,0:T(8,128)(2,1)S(1)}, bf16[40,2048]{1,0:T(8,128)(2,1)S(1)}, u32[]{:S(2)}, u32[]{:S(2)}) collective-permute-start(bf16[40,2048]{1,0:T(8,128)(2,1)S(1)} %get-tuple-element.79), channel_id=1, source_target_pairs={{0,16},{2,18},{4,20},{6,22},{8,24},{10,26},{12,28},{14,30},{16,0},... | collective-permute-start | bytes 491528 | tf_op jit(solution)/shard_map/ppermute | solution.py:298
  322.0 22.6 %collective-permute-start.34 = (bf16[40,2048]{1,0:T(8,128)(2,1)S(1)}, bf16[40,2048]{1,0:T(8,128)(2,1)S(1)}, u32[]{:S(2)}, u32[]{:S(2)}) collective-permute-start(bf16[40,2048]{1,0:T(8,128)(2,1)S(1)} %get-tuple-element.82), channel_id=1, source_target_pairs={{0,20},{2,22},{4,16},{6,18},{8,28},{10,30},{12,24},{14,26},{16,4},... | collective-permute-start | bytes 491528 | tf_op jit(solution)/shard_map/ppermute | solution.py:298
  322.1 22.5 %collective-permute-start.35 = (bf16[40,2048]{1,0:T(8,128)(2,1)S(1)}, bf16[40,2048]{1,0:T(8,128)(2,1)S(1)}, u32[]{:S(2)}, u32[]{:S(2)}) collective-permute-start(bf16[40,2048]{1,0:T(8,128)(2,1)S(1)} %get-tuple-element.81), channel_id=1, source_target_pairs={{0,24},{2,26},{4,28},{6,30},{8,16},{10,18},{12,20},{14,22},{16,8},... | collective-permute-start | bytes 491528 | tf_op jit(solution)/shard_map/ppermute | solution.py:298
  324.0 20.5 %collective-permute-start.36 = (bf16[40,2048]{1,0:T(8,128)(2,1)S(1)}, bf16[40,2048]{1,0:T(8,128)(2,1)S(1)}, u32[]{:S(2)}, u32[]{:S(2)}) collective-permute-start(bf16[40,2048]{1,0:T(8,128)(2,1)S(1)} %get-tuple-element.80), channel_id=1, source_target_pairs={{0,28},{2,30},{4,24},{6,26},{8,20},{10,22},{12,16},{14,18},{16,12}... | collective-permute-start | bytes 491528 | tf_op jit(solution)/shard_map/ppermute | solution.py:298
  344.9 8.6 %collective-permute-start.37 = (bf16[40,2048]{1,0:T(8,128)(2,1)S(1)}, bf16[40,2048]{1,0:T(8,128)(2,1)S(1)}, u32[]{:S(2)}, u32[]{:S(2)}) collective-permute-start(bf16[40,2048]{1,0:T(8,128)(2,1)S(1)} %get-tuple-element.77), channel_id=1, source_target_pairs={{0,4},{2,6},{4,0},{6,2},{8,12},{10,14},{12,8},{14,10},{16,20},{18,... | collective-permute-start | bytes 491528 | tf_op jit(solution)/shard_map/ppermute | solution.py:298
  346.4 12.2 %collective-permute-start.38 = (bf16[40,2048]{1,0:T(8,128)(2,1)S(1)}, bf16[40,2048]{1,0:T(8,128)(2,1)S(1)}, u32[]{:S(2)}, u32[]{:S(2)}) collective-permute-start(bf16[40,2048]{1,0:T(8,128)(2,1)S(1)} %get-tuple-element.76), channel_id=1, source_target_pairs={{0,8},{2,10},{4,12},{6,14},{8,0},{10,2},{12,4},{14,6},{16,24},{18,... | collective-permute-start | bytes 491528 | tf_op jit(solution)/shard_map/ppermute | solution.py:298
  (43 other events, 240.2 us)

commit v5 on v4

--- a/solution.py
+++ b/solution.py
@@ -1,3 +1,4 @@
+import functools
 import math
 
 import jax
@@ -193,41 +194,74 @@
     )(step, decay_rate, conved, gain, kept, carry, pick, skip_gain[None, :], gate_in)
 
 
-def raise_kernel(*refs):
-    pieces, (gate_ref, up_ref, hidden_ref, rows_ref) = refs[:-4], refs[-4:]
-
-    @pl.when(pl.program_id(0) == 0)
+def raise_kernel(shard_ref, *refs, pieces, members, steps):
+    piece_refs, (gate_ref, up_ref, down_ref, hidden_ref) = refs[:pieces], refs[pieces : pieces + 4]
+    out_refs, (rows_ref, all_ref) = refs[pieces + 4 : -2], refs[-2:]
+    step = pl.program_id(0)
+
+    @pl.when(step == 0)
     def _():
-        for k, piece_ref in enumerate(pieces):
+        for k, piece_ref in enumerate(piece_refs):
             rows = piece_ref.shape[0]
             rows_ref[k * rows : (k + 1) * rows] = piece_ref[...]
 
-    rows = rows_ref[...]
-    gate = jnp.dot(rows, gate_ref[0], preferred_element_type=jnp.float32)
-    up = jnp.dot(rows, up_ref[0], preferred_element_type=jnp.float32)
-    hidden_ref[...] = (jax.nn.silu(gate) * up).astype(hidden_ref.dtype)
-
-
-def raised(pieces, gate_weight, up_weight):
+    @pl.when(step < steps)
+    def _():
+        rows = rows_ref[...]
+        tile = hidden_ref.shape[1]
+        gate = jnp.dot(rows, gate_ref[0], preferred_element_type=jnp.float32)
+        up = jnp.dot(rows, up_ref[0], preferred_element_type=jnp.float32)
+        hidden = (jax.nn.silu(gate) * up).astype(hidden_ref.dtype)
+        hidden_ref[...] = hidden
+        all_ref[:, pl.ds(pl.multiple_of(step * tile, tile), tile)] = hidden
+
+    @pl.when(step >= steps)
+    def _():
+        out = jnp.dot(all_ref[...], down_ref[0], preferred_element_type=jnp.float32)
+        for k, out_ref in enumerate(out_refs):
+            rows = out_ref.shape[0]
+            out_ref[...] = out[k * rows : (k + 1) * rows].astype(out_ref.dtype)
+
+
+def raised(pieces, gate_weight, up_weight, down_weight, shard, features, members):
     rows, depth = sum(piece.shape[0] for piece in pieces), pieces[0].shape[1]
     width = gate_weight.shape[2]
-    tile = min(512, width)
-    weight = pl.BlockSpec((1, depth, tile), lambda i: (0, 0, i))
-    return pl.pallas_call(
-        raise_kernel,
-        grid=(width // tile,),
-        in_specs=[whole(piece.shape) for piece in pieces] + [weight, weight],
-        out_specs=pl.BlockSpec((rows, tile), lambda i: (0, i)),
-        out_shape=jax.ShapeDtypeStruct((rows, width), jnp.bfloat16),
-        scratch_shapes=[pltpu.VMEM((rows, depth), jnp.bfloat16)],
-        compiler_params=pltpu.CompilerParams(vmem_limit_bytes=56 * 1024 * 1024),
+    tile, out_tile = min(512, width), min(512, features)
+    steps, out_steps = width // tile, features // out_tile
+    up_at = lambda i: jnp.minimum(i, steps - 1)
+    down_at = lambda i: jnp.maximum(i - steps, 0)
+    weight = pl.BlockSpec((1, depth, tile), lambda i, t: (0, 0, up_at(i)))
+    outs = pl.pallas_call(
+        functools.partial(raise_kernel, pieces=len(pieces), members=members, steps=steps),
+        grid_spec=pltpu.PrefetchScalarGridSpec(
+            num_scalar_prefetch=1,
+            grid=(steps + out_steps,),
+            in_specs=[pl.BlockSpec(piece.shape, lambda i, t: (0, 0)) for piece in pieces]
+            + [
+                weight,
+                weight,
+                pl.BlockSpec(
+                    (1, width, out_tile), lambda i, t: (0, 0, t[0] * out_steps + down_at(i))
+                ),
+            ],
+            out_specs=[pl.BlockSpec((rows, tile), lambda i, t: (0, up_at(i)))]
+            + [pl.BlockSpec((rows // members, out_tile), lambda i, t: (0, down_at(i)))] * members,
+            scratch_shapes=[
+                pltpu.VMEM((rows, depth), jnp.bfloat16),
+                pltpu.VMEM((rows, width), jnp.bfloat16),
+            ],
+        ),
+        out_shape=[jax.ShapeDtypeStruct((rows, width), jnp.bfloat16)]
+        + [jax.ShapeDtypeStruct((rows // members, features), jnp.bfloat16)] * members,
+        compiler_params=pltpu.CompilerParams(vmem_limit_bytes=60 * 1024 * 1024),
         cost_estimate=pl.CostEstimate(
-            flops=4 * rows * depth * width,
-            bytes_accessed=4 * depth * width,
+            flops=2 * rows * width * (2 * depth + features),
+            bytes_accessed=2 * width * (2 * depth + features),
             transcendentals=rows * width,
         ),
         name="raised",
-    )(*pieces, gate_weight, up_weight)
+    )(shard.astype(jnp.int32)[None], *pieces, gate_weight, up_weight, down_weight)
+    return outs[0], outs[1:]
 
 
 def lower_kernel(shard_ref, hidden_ref, weight_ref, *out_refs):
@@ -239,7 +273,7 @@
 
 def lowered(hidden, down_weight, shard, width, members):
     rows, depth = hidden.shape
-    tile = min(1024, width)
+    tile = min(512, width)
     steps = width // tile
     out = jax.ShapeDtypeStruct((rows // members, width), jnp.bfloat16)
     return pl.pallas_call(
@@ -405,7 +439,10 @@
     own_rates = lax.dynamic_slice_in_dim(decay_rate, position * chunk, chunk, 1)
     carry = lax.all_to_all(carries(ends, own_rates), "loop", 0, 0, tiled=True)
     later_rows, carry = lax.optimization_barrier((out_proj[first_rows:], carry))
-    far_later = [across(later_rows, low * high) for high in range(1, shards)]
+    middle_rows = channels // EIGHTHS * 2
+    far_middle = [across(later_rows[:middle_rows], low * high) for high in range(1, shards)]
+    last_rows, far_middle = lax.optimization_barrier((later_rows[middle_rows:], far_middle))
+    far_last = [across(last_rows, low * high) for high in range(1, shards)]
     own_low, own_high = position % low, position // low
     tokens_of = []
     for first, steps in ((0, first_steps), (first_steps, EIGHTHS - first_steps)):
@@ -416,15 +453,13 @@
         tokens_of.append(
             {m: gated if m == 0 else across(gated, m) for m in (0, 2, 4) if m < low}
         )
-    far_later, tokens_of = lax.optimization_barrier((far_later, tokens_of))
-    for half, got in enumerate(tokens_of):
+    tokens_of = lax.optimization_barrier(tokens_of)
+    for got in tokens_of:
         for m in range(6, low, 2):
             one = m & -m
-            if one == m:
-                got[m] = across(got[0], m)
-            else:
-                via = one if half == 0 else m ^ one
-                got[m] = across(got[via], m ^ via)
+            got[m] = across(got[m ^ one], one) if m != one else across(got[0], m)
+    far_last, tokens_of = lax.optimization_barrier((far_last, tokens_of))
+    far_later = [jnp.concatenate(parts, axis=0) for parts in zip(far_middle, far_last)]
     all_tokens = [
         jnp.concatenate([got[m] for m in range(0, low, 2)], axis=0) for got in tokens_of
     ]
@@ -486,7 +521,9 @@
         for first in (near, 0)
     ]
     pieces = parts + [from_member(by)(part) for by in range(1, members) for part in parts]
-    hidden = raised(pieces, gate_weight, up_weight)
+    hidden, outs = raised(
+        pieces, gate_weight, up_weight, down_weight, (shard + 1) % shards, width, members
+    )
 
     def member_sum(outs):
         total = outs[0].astype(jnp.float32)
@@ -497,9 +534,9 @@
     def for_shard_of(hidden, t):
         return lowered(hidden, down_weight, t, width, members)
 
-    sent = [
+    sent = [member_sum(outs).astype(jnp.bfloat16)] + [
         member_sum(for_shard_of(hidden, (shard + by) % shards)).astype(jnp.bfloat16)
-        for by in range(1, shards)
+        for by in range(2, shards)
     ]
     hidden, sent = lax.optimization_barrier((hidden, sent))
     far_sums = [rotated(part[:rows], "tp", by) for by, part in enumerate(sent, 1)]
@@ -510,16 +547,22 @@
     near_sums = [rotated(part, "tp", by) for by, part in enumerate(near_sent, 1)]
     own_sum = member_sum(own_outs)
 
-    def given_back(first, own, sums):
+    def shared(own, sums):
         share = own
         for part in sums:
             share = share + part.astype(jnp.float32)
-        share = share.astype(jnp.bfloat16).reshape(near, CAP, width)
-        return teams_swapped(share, first, members)
-
-    far_back = given_back(near, own_sum[:rows], far_sums)
-    near_sums, far_back = lax.optimization_barrier((near_sums, far_back))
-    back = [given_back(0, own_sum[rows:], near_sums), far_back]
+        return share.astype(jnp.bfloat16).reshape(near, CAP, width)
+
+    ahead = near // 2
+    far_share = shared(own_sum[:rows], far_sums)
+    far_ahead = teams_swapped(far_share[:ahead], near, members)
+    near_sums, far_ahead = lax.optimization_barrier((near_sums, far_ahead))
+    near_share = shared(own_sum[rows:], near_sums)
+    back = [
+        teams_swapped(near_share, 0, members),
+        far_ahead,
+        teams_swapped(far_share[ahead:], near + ahead, members),
+    ]
     returned = jnp.concatenate(back, axis=0).reshape(EXPERTS * CAP, width)
     expert_sum = jnp.dot(
         weighted.T,

time: 364 us -> 386 us (1.060)
  waiting for transfers between devices: 149 us -> 180 us
  starting transfers between devices: 67.5 us -> 61.2 us
  local copies, waits for them, and re-layouts: 33.3 us -> 29.1 us
    ppermute x6, waiting for transfers between devices: 26.1 us -> 40.3 us  [rotated(): return lax.ppermute(x, axis, [(i, (i + by) % size) for i in range(size)])]
    ppermute x15 -> x16, waiting for transfers between devices: 62.1 us -> 75 us  [across(): lax.ppermute(x, 'loop', [(i, i ^ mask) for i in range(lax.axis_size('loop...]
    pallas_call x1, Pallas kernels: 39.7 us -> 51.8 us  [raised(): pl.pallas_call(functools.partial(raise_kernel, pieces=len(pieces), member...]
    pallas_call x2 -> x1, Pallas kernels: 22.8 us -> 10.8 us  [lowered(): pl.pallas_call(lower_kernel, grid_spec=pltpu.PrefetchScalarGridSpec(num_s...]
    unnamed x79 -> x80, local copies, waits for them, and re-layouts: 19.7 us -> 11.9 us
    ppermute x14, starting transfers between devices: 31.7 us -> 24.4 us  [teams_swapped(): out.append(lax.ppermute(x[k], 'loop', pairs))]
    ppermute x14, waiting for transfers between devices: 38.9 us -> 43.7 us  [teams_swapped(): out.append(lax.ppermute(x[k], 'loop', pairs))]
    ppermute x15 -> x16, starting transfers between devices: 13.7 us -> 14.9 us  [across(): lax.ppermute(x, 'loop', [(i, i ^ mask) for i in range(lax.axis_size('loop...]
  transfers between devices with their start and end apart: 42 -> 43, of which waited for: 25 -> 26; matrix products, arithmetic and copies ran while one was open for 8% -> 9% of each run, Pallas kernels for 10% -> 9%
where the time goes in v5:
time: 386 us; the launch traced here: 385 us
  waiting for transfers between devices  180 us (47%)
  Pallas kernels  89.4 us (23%)
  starting transfers between devices  61.2 us (16%)
  local copies, waits for them, and re-layouts  29.1 us (8%)
  matrix products  13.9 us (4%)
  other arithmetic  9.4 us (2%)
    ppermute x16, waiting for transfers between devices, across(): lax.ppermute(x, 'loop', [(i, i ^ mask) for i in range(lax.axis_size('loop...  75 us
    pallas_call x1, Pallas kernels, raised(): pl.pallas_call(functools.partial(raise_kernel, pieces=len(pieces), member...  51.8 us
    ppermute x14, waiting for transfers between devices, teams_swapped(): out.append(lax.ppermute(x[k], 'loop', pairs))  43.7 us
    ppermute x6, waiting for transfers between devices, rotated(): return lax.ppermute(x, axis, [(i, (i + by) % size) for i in range(size)])  40.3 us
    ppermute x14, starting transfers between devices, teams_swapped(): out.append(lax.ppermute(x[k], 'loop', pairs))  24.4 us
    ppermute x16, starting transfers between devices, across(): lax.ppermute(x, 'loop', [(i, i ^ mask) for i in range(lax.axis_size('loop...  14.9 us
    pallas_call x2, Pallas kernels, scan_gated(): pl.pallas_call(scan_kernel, grid=(steps,), in_specs=[part(tokens), part(N...  13.3 us
    unnamed x80, local copies, waits for them, and re-layouts  11.9 us
  transfers between devices with their start and end apart: 43, of which 26 were waited for; matrix products, arithmetic and copies ran while one was open for 9% of the time, Pallas kernels for 9%

profile of v5, /device:TPU:0, one launch (start us, length us, event | category | flops | bytes accessed | tf_op | source)
XLA Modules:
  0.0 384.6 jit_solution(14553713301967472712)
XLA Ops:
  5.7 3.6 collective-permute-start.2
  17.7 2.7 collective-permute-done.1
  23.3 11.2 %scan_end.1 = (f32[128,4096]{1,0:T(8,128)S(1)}, bf16[16,32,256]{2,1,0:T(8,128)(2,1)}) custom-call(bf16[128,256]{1,0:T(8,128)(2,1)S(1)} %slice.220.low_ref, bf16[256,4096]{1,0:T(8,128)(2,1)S(1)} %copy-done.13, f32[1,4096]{1,0:T(1,128)S(1)} %bitcast.32, f32[16,4096]{1,0:T(8,128)S(1)} %copy-done.10, bf16[128,4096]{1,0:T(8,128)(2,1)S(1)} %multiply_convert_fusion.conved_ref, ...), custom_call_target="tpu_custom_call" | custom-call | flops 41943040 | bytes 4194304 | tf_op jit(solution)/shard_map/scan_end/pallas_call | solution.py:128
  35.9 8.0 %collective-permute-done.2 = bf16[1536,256]{1,0:T(8,128)(2,1)} collective-permute-done((bf16[1536,256]{1,0:T(8,128)(2,1)}, bf16[1536,256]{1,0:T(8,128)(2,1)}, u32[]{:S(2)}, u32[]{:S(2)}) %collective-permute-start.2) | collective-permute-done | bytes 786464 | tf_op jit(solution)/shard_map/ppermute | solution.py:320
  43.9 6.1 %all-to-all-start = ((bf16[16,32,256]{2,1,0:T(8,128)(2,1)}), bf16[16,32,256]{2,1,0:T(8,128)(2,1)S(1)}, u32[]{:S(2)}, u32[]{:S(2)}) async-start(bf16[16,32,256]{2,1,0:T(8,128)(2,1)} %get-tuple-element.44), calls=%async_computation | async-start | bytes 524288 | tf_op jit(solution)/shard_map/all_to_all | solution.py:437
  50.6 9.4 %all-to-all-done.ends_ref = bf16[16,32,256]{2,1,0:T(8,128)(2,1)S(1)} async-done(((bf16[16,32,256]{2,1,0:T(8,128)(2,1)}), bf16[16,32,256]{2,1,0:T(8,128)(2,1)S(1)}, u32[]{:S(2)}, u32[]{:S(2)}) %all-to-all-start) | async-done | bytes 262176 | tf_op jit(solution)/shard_map/all_to_all | solution.py:437
  62.4 3.7 all-to-all-start.1
  69.7 4.1 %all-to-all-done.1.carry_ref = bf16[16,16,256]{2,1,0:T(8,128)(2,1)S(1)} async-done(((bf16[16,16,256]{2,1,0:T(8,128)(2,1)}), bf16[16,16,256]{2,1,0:T(8,128)(2,1)S(1)}, u32[]{:S(2)}, u32[]{:S(2)}) %all-to-all-start.1) | async-done | bytes 131104 | tf_op jit(solution)/shard_map/all_to_all | solution.py:440
  78.9 8.3 %scan_gated.3 = bf16[128,2560]{1,0:T(8,128)(2,1)S(1)} custom-call(f32[128,4096]{1,0:T(8,128)S(1)} %copy-done.3, f32[16,4096]{1,0:T(8,128)S(1)} %copy-done.11, bf16[128,4096]{1,0:T(8,128)(2,1)S(1)} %multiply_convert_fusion.conved_ref, f32[128,16,128]{2,1,0:T(8,128)S(1)} %broadcast_in_dim.48.gain_ref, f32[128,1]{1,0:T(8,128)S(1)} %copy.51.kept_ref, ...), custom_call_target="tpu_custom_call" | custom-call | flops 36700160 | bytes 3932160 | tf_op jit(solution)/shard_map/scan_gated/pallas_call | solution.py:171
  89.0 5.0 %scan_gated.2 = bf16[128,1536]{1,0:T(8,128)(2,1)S(1)} custom-call(f32[128,4096]{1,0:T(8,128)S(1)} %copy-done.3, f32[16,4096]{1,0:T(8,128)S(1)} %copy-done.11, bf16[128,4096]{1,0:T(8,128)(2,1)S(1)} %multiply_convert_fusion.conved_ref, f32[128,16,128]{2,1,0:T(8,128)S(1)} %broadcast_in_dim.48.gain_ref, f32[128,1]{1,0:T(8,128)S(1)} %copy.51.kept_ref, ...), custom_call_target="tpu_custom_call" | custom-call | flops 22020096 | bytes 2359296 | tf_op jit(solution)/shard_map/scan_gated/pallas_call | solution.py:171
  97.6 2.8 collective-permute-done.3
  100.4 11.8 %collective-permute-done.5 = bf16[128,1536]{1,0:T(8,128)(2,1)S(1)} collective-permute-done((bf16[128,1536]{1,0:T(8,128)(2,1)S(1)}, bf16[128,1536]{1,0:T(8,128)(2,1)S(1)}, u32[]{:S(2)}, u32[]{:S(2)}) %collective-permute-start.5) | collective-permute-done | bytes 393248 | tf_op jit(solution)/shard_map/ppermute | solution.py:320
  112.2 27.4 %collective-permute-done.6 = bf16[128,1536]{1,0:T(8,128)(2,1)S(1)} collective-permute-done((bf16[128,1536]{1,0:T(8,128)(2,1)S(1)}, bf16[128,1536]{1,0:T(8,128)(2,1)S(1)}, u32[]{:S(2)}, u32[]{:S(2)}) %collective-permute-start.6) | collective-permute-done | bytes 393248 | tf_op jit(solution)/shard_map/ppermute | solution.py:320
  145.6 20.3 %collective-permute-done.9 = bf16[128,1536]{1,0:T(8,128)(2,1)} collective-permute-done((bf16[128,1536]{1,0:T(8,128)(2,1)}, bf16[128,1536]{1,0:T(8,128)(2,1)}, u32[]{:S(2)}, u32[]{:S(2)}) %collective-permute-start.9) | collective-permute-done | bytes 393248 | tf_op jit(solution)/shard_map/ppermute | solution.py:320
  169.1 3.2 fusion.4
  181.3 12.2 %collective-permute-done.15 = bf16[512,512]{1,0:T(8,128)(2,1)} collective-permute-done((bf16[512,512]{1,0:T(8,128)(2,1)S(1)}, bf16[512,512]{1,0:T(8,128)(2,1)}, u32[]{:S(2)}, u32[]{:S(2)}) %collective-permute-start.15) | collective-permute-done | bytes 524320 | tf_op jit(solution)/shard_map/ppermute | solution.py:33
  195.6 2.8 collective-permute-start.18
  209.0 3.0 collective-permute-start.22
  212.0 11.7 %collective-permute-done.19 = bf16[40,2048]{1,0:T(8,128)(2,1)S(1)} collective-permute-done((bf16[40,2048]{1,0:T(8,128)(2,1)S(1)}, bf16[40,2048]{1,0:T(8,128)(2,1)S(1)}, u32[]{:S(2)}, u32[]{:S(2)}) %collective-permute-start.19) | collective-permute-done | bytes 163872 | tf_op jit(solution)/shard_map/ppermute | solution.py:332
  223.8 4.0 %collective-permute-done.20 = bf16[40,2048]{1,0:T(8,128)(2,1)S(1)} collective-permute-done((bf16[40,2048]{1,0:T(8,128)(2,1)S(1)}, bf16[40,2048]{1,0:T(8,128)(2,1)S(1)}, u32[]{:S(2)}, u32[]{:S(2)}) %collective-permute-start.20) | collective-permute-done | bytes 163872 | tf_op jit(solution)/shard_map/ppermute | solution.py:332
  236.0 10.6 %collective-permute-done.23 = bf16[160,2048]{1,0:T(8,128)(2,1)} collective-permute-done((bf16[160,2048]{1,0:T(8,128)(2,1)S(1)}, bf16[160,2048]{1,0:T(8,128)(2,1)}, u32[]{:S(2)}, u32[]{:S(2)}) %collective-permute-start.23) | collective-permute-done | bytes 655392 | tf_op jit(solution)/shard_map/ppermute | solution.py:33
  247.8 10.5 %collective-permute-done.27 = bf16[160,2048]{1,0:T(8,128)(2,1)} collective-permute-done((bf16[160,2048]{1,0:T(8,128)(2,1)}, bf16[160,2048]{1,0:T(8,128)(2,1)}, u32[]{:S(2)}, u32[]{:S(2)}) %collective-permute-start.27) | collective-permute-done | bytes 655392 | tf_op jit(solution)/shard_map/ppermute | solution.py:33
  259.5 3.0 collective-permute-done.29.refs_3_
  263.6 51.8 %raised.1 = (bf16[640,3072]{1,0:T(8,128)(2,1)}, bf16[320,2048]{1,0:T(8,128)(2,1)}, bf16[320,2048]{1,0:T(8,128)(2,1)}) custom-call(s32[1]{0:T(128)} %bitcast.12.shard_ref, bf16[160,4096]{1,0:T(8,128)(2,1)} %copy-done.17, bf16[160,4096]{1,0:T(8,128)(2,1)} %copy-done.16, bf16[160,4096]{1,0:T(8,128)(2,1)} %copy-done.29, bf16[160,4096]{1,0:T(8,128)(2,1)} %copy-done.30, ...), custom_call_target="tpu_custom_call" | custom-call | flops 40265318400 | bytes 62914560 | tf_op jit(solution)/shard_map/raised/pallas_call | solution.py:234
  315.5 3.1 collective-permute-done.30
  322.4 10.8 %lowered.1 = (bf16[320,2048]{1,0:T(8,128)(2,1)S(1)}, bf16[320,2048]{1,0:T(8,128)(2,1)S(1)}) custom-call(s32[1]{0:T(128)} %bitcast.13.shard_ref, bf16[640,3072]{1,0:T(8,128)(2,1)S(1)} %copy-done.15, bf16[1,3072,4096]{2,1,0:T(8,128)(2,1)} %weight_ref.1), custom_call_target="tpu_custom_call" | custom-call | flops 8053063680 | bytes 12582912 | tf_op jit(solution)/shard_map/lowered/pallas_call | solution.py:279
  333.3 4.4 %collective-permute-done.31 = bf16[160,2048]{1,0:T(8,128)(2,1)S(1)} collective-permute-done((bf16[160,2048]{1,0:T(8,128)(2,1)S(1)}, bf16[160,2048]{1,0:T(8,128)(2,1)S(1)}, u32[]{:S(2)}, u32[]{:S(2)}) %collective-permute-start.31) | collective-permute-done | bytes 655392 | tf_op jit(solution)/shard_map/ppermute | solution.py:33
  341.4 7.3 %collective-permute-start.35 = (bf16[40,2048]{1,0:T(8,128)(2,1)S(1)}, bf16[40,2048]{1,0:T(8,128)(2,1)S(1)}, u32[]{:S(2)}, u32[]{:S(2)}) collective-permute-start(bf16[40,2048]{1,0:T(8,128)(2,1)S(1)} %get-tuple-element.99), channel_id=1, source_target_pairs={{0,20},{2,22},{4,16},{6,18},{8,28},{10,30},{12,24},{14,26},{16,4},... | collective-permute-start | bytes 491528 | tf_op jit(solution)/shard_map/ppermute | solution.py:332
  348.7 12.0 %collective-permute-done.35 = bf16[40,2048]{1,0:T(8,128)(2,1)S(1)} collective-permute-done((bf16[40,2048]{1,0:T(8,128)(2,1)S(1)}, bf16[40,2048]{1,0:T(8,128)(2,1)S(1)}, u32[]{:S(2)}, u32[]{:S(2)}) %collective-permute-start.35) | collective-permute-done | bytes 163872 | tf_op jit(solution)/shard_map/ppermute | solution.py:332
  368.2 3.1 collective-permute-start.38
  371.4 7.7 %collective-permute-done.37 = bf16[40,2048]{1,0:T(8,128)(2,1)S(1)} collective-permute-done((bf16[40,2048]{1,0:T(8,128)(2,1)S(1)}, bf16[40,2048]{1,0:T(8,128)(2,1)S(1)}, u32[]{:S(2)}, u32[]{:S(2)}) %collective-permute-start.37) | collective-permute-done | bytes 163872 | tf_op jit(solution)/shard_map/ppermute | solution.py:332
  379.1 3.6 collective-permute-done.38
  (206 shorter events, 94.0 us)
Async XLA Ops:
  5.7 38.2 %collective-permute-start.2 = (bf16[1536,256]{1,0:T(8,128)(2,1)}, bf16[1536,256]{1,0:T(8,128)(2,1)}, u32[]{:S(2)}, u32[]{:S(2)}) collective-permute-start(bf16[1536,256]{1,0:T(8,128)(2,1)} %slice.187), channel_id=1, source_target_pairs={{0,16},{2,18},{4,20},{6,22},{8,24},{10,26},{12,28},{14,30},{16,0},... | collective-permute-start | bytes 2359304 | tf_op jit(solution)/shard_map/ppermute | solution.py:320
  43.9 16.1 %all-to-all-start = ((bf16[16,32,256]{2,1,0:T(8,128)(2,1)}), bf16[16,32,256]{2,1,0:T(8,128)(2,1)S(1)}, u32[]{:S(2)}, u32[]{:S(2)}) async-start(bf16[16,32,256]{2,1,0:T(8,128)(2,1)} %get-tuple-element.44), calls=%async_computation | async-start | bytes 524288 | tf_op jit(solution)/shard_map/all_to_all | solution.py:437
  62.4 11.4 %all-to-all-start.1 = ((bf16[16,16,256]{2,1,0:T(8,128)(2,1)}), bf16[16,16,256]{2,1,0:T(8,128)(2,1)S(1)}, u32[]{:S(2)}, u32[]{:S(2)}) async-start(bf16[16,16,256]{2,1,0:T(8,128)(2,1)} %carries.1), calls=%async_computation.1 | async-start | bytes 262144 | tf_op jit(solution)/shard_map/all_to_all | solution.py:440
  74.9 25.5 %collective-permute-start.3 = (bf16[1024,256]{1,0:T(8,128)(2,1)S(1)}, bf16[1024,256]{1,0:T(8,128)(2,1)S(1)}, u32[]{:S(2)}, u32[]{:S(2)}) collective-permute-start(bf16[1024,256]{1,0:T(8,128)(2,1)S(1)} %slice.189), channel_id=1, source_target_pairs={{0,16},{2,18},{4,20},{6,22},{8,24},{10,26},{12,28},{14,30},{16,0},... | collective-permute-start | bytes 1572872 | tf_op jit(solution)/shard_map/ppermute | solution.py:320
  87.2 52.4 %collective-permute-start.7 = (bf16[128,2560]{1,0:T(8,128)(2,1)S(1)}, bf16[128,2560]{1,0:T(8,128)(2,1)S(1)}, u32[]{:S(2)}, u32[]{:S(2)}) collective-permute-start(bf16[128,2560]{1,0:T(8,128)(2,1)S(1)} %scan_gated.3), channel_id=1, source_target_pairs={{0,4},{2,6},{4,0},{6,2},{8,12},{10,14},{12,8},{14,10},{16,20},{18,... | collective-permute-start | bytes 1966088 | tf_op jit(solution)/shard_map/ppermute | solution.py:320
  87.6 52.0 %collective-permute-start.8 = (bf16[128,2560]{1,0:T(8,128)(2,1)S(1)}, bf16[128,2560]{1,0:T(8,128)(2,1)}, u32[]{:S(2)}, u32[]{:S(2)}) collective-permute-start(bf16[128,2560]{1,0:T(8,128)(2,1)S(1)} %scan_gated.3), channel_id=1, source_target_pairs={{0,8},{2,10},{4,12},{6,14},{8,0},{10,2},{12,4},{14,6},{16,24},{18,... | collective-permute-start | bytes 1966088 | tf_op jit(solution)/shard_map/ppermute | solution.py:320
  94.0 18.1 %collective-permute-start.5 = (bf16[128,1536]{1,0:T(8,128)(2,1)S(1)}, bf16[128,1536]{1,0:T(8,128)(2,1)S(1)}, u32[]{:S(2)}, u32[]{:S(2)}) collective-permute-start(bf16[128,1536]{1,0:T(8,128)(2,1)S(1)} %scan_gated.2), channel_id=1, source_target_pairs={{0,4},{2,6},{4,0},{6,2},{8,12},{10,14},{12,8},{14,10},{16,20},{18,... | collective-permute-start | bytes 1179656 | tf_op jit(solution)/shard_map/ppermute | solution.py:320
  95.3 44.3 %collective-permute-start.6 = (bf16[128,1536]{1,0:T(8,128)(2,1)S(1)}, bf16[128,1536]{1,0:T(8,128)(2,1)S(1)}, u32[]{:S(2)}, u32[]{:S(2)}) collective-permute-start(bf16[128,1536]{1,0:T(8,128)(2,1)S(1)} %scan_gated.2), channel_id=1, source_target_pairs={{0,8},{2,10},{4,12},{6,14},{8,0},{10,2},{12,4},{14,6},{16,24},{18,... | collective-permute-start | bytes 1179656 | tf_op jit(solution)/shard_map/ppermute | solution.py:320
  100.4 65.5 %collective-permute-start.4 = (bf16[1536,256]{1,0:T(8,128)(2,1)S(1)}, bf16[1536,256]{1,0:T(8,128)(2,1)S(1)}, u32[]{:S(2)}, u32[]{:S(2)}) collective-permute-start(bf16[1536,256]{1,0:T(8,128)(2,1)S(1)} %slice.188), channel_id=1, source_target_pairs={{0,16},{2,18},{4,20},{6,22},{8,24},{10,26},{12,28},{14,30},{16,0},... | collective-permute-start | bytes 2359304 | tf_op jit(solution)/shard_map/ppermute | solution.py:320
  140.5 25.4 %collective-permute-start.10 = (bf16[128,2560]{1,0:T(8,128)(2,1)}, bf16[128,2560]{1,0:T(8,128)(2,1)}, u32[]{:S(2)}, u32[]{:S(2)}) collective-permute-start(bf16[128,2560]{1,0:T(8,128)(2,1)} %collective-permute-done.8), channel_id=1, source_target_pairs={{0,4},{2,6},{4,0},{6,2},{8,12},{10,14},{12,8},{14,10},{16,20},{18,... | collective-permute-start | bytes 1966088 | tf_op jit(solution)/shard_map/ppermute | solution.py:320
  141.2 27.9 %collective-permute-start.14 = (bf16[2560,256]{1,0:T(8,128)(2,1)}, bf16[2560,256]{1,0:T(8,128)(2,1)}, u32[]{:S(2)}, u32[]{:S(2)}) collective-permute-start(bf16[2560,256]{1,0:T(8,128)(2,1)} %slice.174), channel_id=1, source_target_pairs={{0,2},{2,0},{4,6},{6,4},{8,10},{10,8},{12,14},{14,12},{16,18},{18,... | collective-permute-start | bytes 3932168 | tf_op jit(solution)/shard_map/ppermute | solution.py:320
  141.2 32.2 %collective-permute-start.13 = (bf16[1536,256]{1,0:T(8,128)(2,1)}, bf16[1536,256]{1,0:T(8,128)(2,1)}, u32[]{:S(2)}, u32[]{:S(2)}) collective-permute-start(bf16[1536,256]{1,0:T(8,128)(2,1)} %slice.187), channel_id=1, source_target_pairs={{0,2},{2,0},{4,6},{6,4},{8,10},{10,8},{12,14},{14,12},{16,18},{18,... | collective-permute-start | bytes 2359304 | tf_op jit(solution)/shard_map/ppermute | solution.py:320
  142.0 23.9 %collective-permute-start.9 = (bf16[128,1536]{1,0:T(8,128)(2,1)}, bf16[128,1536]{1,0:T(8,128)(2,1)}, u32[]{:S(2)}, u32[]{:S(2)}) collective-permute-start(bf16[128,1536]{1,0:T(8,128)(2,1)} %copy-done.23), channel_id=1, source_target_pairs={{0,4},{2,6},{4,0},{6,2},{8,12},{10,14},{12,8},{14,10},{16,20},{18,... | collective-permute-start | bytes 1179656 | tf_op jit(solution)/shard_map/ppermute | solution.py:320
  165.9 11.4 %collective-permute-start.11 = (bf16[1536,256]{1,0:T(8,128)(2,1)}, bf16[1536,256]{1,0:T(8,128)(2,1)S(1)}, u32[]{:S(2)}, u32[]{:S(2)}) collective-permute-start(bf16[1536,256]{1,0:T(8,128)(2,1)} %collective-permute-done.2), channel_id=1, source_target_pairs={{0,2},{2,0},{4,6},{6,4},{8,10},{10,8},{12,14},{14,12},{16,18},{18,... | collective-permute-start | bytes 2359304 | tf_op jit(solution)/shard_map/ppermute | solution.py:320
  166.0 9.7 %collective-permute-start.12 = (bf16[2560,256]{1,0:T(8,128)(2,1)S(1)}, bf16[2560,256]{1,0:T(8,128)(2,1)S(1)}, u32[]{:S(2)}, u32[]{:S(2)}) collective-permute-start(bf16[2560,256]{1,0:T(8,128)(2,1)S(1)} %constant_dynamic-update-slice_fusion.8), channel_id=1, source_target_pairs={{0,2},{2,0},{4,6},{6,4},{8,10},{10,8},{12,14},{14,12},{16,18},{18,... | collective-permute-start | bytes 3932168 | tf_op jit(solution)/shard_map/ppermute | solution.py:320
  179.4 14.0 %collective-permute-start.15 = (bf16[512,512]{1,0:T(8,128)(2,1)S(1)}, bf16[512,512]{1,0:T(8,128)(2,1)}, u32[]{:S(2)}, u32[]{:S(2)}) collective-permute-start(bf16[512,512]{1,0:T(8,128)(2,1)S(1)} %get-tuple-element.114), channel_id=1, source_target_pairs={{0,1},{1,0},{2,3},{3,2},{4,5},{5,4},{6,7},{7,6},{8,9},{9,8},{10,11... | collective-permute-start | bytes 1572872 | tf_op jit(solution)/shard_map/ppermute | solution.py:33
  204.3 19.5 %collective-permute-start.19 = (bf16[40,2048]{1,0:T(8,128)(2,1)S(1)}, bf16[40,2048]{1,0:T(8,128)(2,1)S(1)}, u32[]{:S(2)}, u32[]{:S(2)}) collective-permute-start(bf16[40,2048]{1,0:T(8,128)(2,1)S(1)} %get-tuple-element.96), channel_id=1, source_target_pairs={{0,16},{2,18},{4,20},{6,22},{8,24},{10,26},{12,28},{14,30},{16,0},... | collective-permute-start | bytes 491528 | tf_op jit(solution)/shard_map/ppermute | solution.py:332
  204.9 22.8 %collective-permute-start.20 = (bf16[40,2048]{1,0:T(8,128)(2,1)S(1)}, bf16[40,2048]{1,0:T(8,128)(2,1)S(1)}, u32[]{:S(2)}, u32[]{:S(2)}) collective-permute-start(bf16[40,2048]{1,0:T(8,128)(2,1)S(1)} %get-tuple-element.95), channel_id=1, source_target_pairs={{0,20},{2,22},{4,16},{6,18},{8,28},{10,30},{12,24},{14,26},{16,4},... | collective-permute-start | bytes 491528 | tf_op jit(solution)/shard_map/ppermute | solution.py:332
  207.4 21.3 %collective-permute-start.21 = (bf16[40,2048]{1,0:T(8,128)(2,1)S(1)}, bf16[40,2048]{1,0:T(8,128)(2,1)S(1)}, u32[]{:S(2)}, u32[]{:S(2)}) collective-permute-start(bf16[40,2048]{1,0:T(8,128)(2,1)S(1)} %get-tuple-element.94), channel_id=1, source_target_pairs={{0,24},{2,26},{4,28},{6,30},{8,16},{10,18},{12,20},{14,22},{16,8},... | collective-permute-start | bytes 491528 | tf_op jit(solution)/shard_map/ppermute | solution.py:332
  209.0 19.7 %collective-permute-start.22 = (bf16[40,2048]{1,0:T(8,128)(2,1)S(1)}, bf16[40,2048]{1,0:T(8,128)(2,1)S(1)}, u32[]{:S(2)}, u32[]{:S(2)}) collective-permute-start(bf16[40,2048]{1,0:T(8,128)(2,1)S(1)} %get-tuple-element.93), channel_id=1, source_target_pairs={{0,28},{2,30},{4,24},{6,26},{8,20},{10,22},{12,16},{14,18},{16,12}... | collective-permute-start | bytes 491528 | tf_op jit(solution)/shard_map/ppermute | solution.py:332
  212.0 18.3 %collective-permute-start.26 = (bf16[40,2048]{1,0:T(8,128)(2,1)S(1)}, bf16[40,2048]{1,0:T(8,128)(2,1)S(1)}, u32[]{:S(2)}, u32[]{:S(2)}) collective-permute-start(bf16[40,2048]{1,0:T(8,128)(2,1)S(1)} %get-tuple-element.90), channel_id=1, source_target_pairs={{0,12},{2,14},{4,8},{6,10},{8,4},{10,6},{12,0},{14,2},{16,28},{18,... | collective-permute-start | bytes 491528 | tf_op jit(solution)/shard_map/ppermute | solution.py:332
  228.7 17.8 %collective-permute-start.23 = (bf16[160,2048]{1,0:T(8,128)(2,1)S(1)}, bf16[160,2048]{1,0:T(8,128)(2,1)}, u32[]{:S(2)}, u32[]{:S(2)}) collective-permute-start(bf16[160,2048]{1,0:T(8,128)(2,1)S(1)} %constant_dynamic-update-slice_fusion.10), channel_id=1, source_target_pairs={{0,1},{1,0},{2,3},{3,2},{4,5},{5,4},{6,7},{7,6},{8,9},{9,8},{10,11... | collective-permute-start | bytes 1966088 | tf_op jit(solution)/shard_map/ppermute | solution.py:33
  234.2 24.0 %collective-permute-start.27 = (bf16[160,2048]{1,0:T(8,128)(2,1)}, bf16[160,2048]{1,0:T(8,128)(2,1)}, u32[]{:S(2)}, u32[]{:S(2)}) collective-permute-start(bf16[160,2048]{1,0:T(8,128)(2,1)} %get-tuple-element.105), channel_id=1, source_target_pairs={{0,1},{1,0},{2,3},{3,2},{4,5},{5,4},{6,7},{7,6},{8,9},{9,8},{10,11... | collective-permute-start | bytes 1966088 | tf_op jit(solution)/shard_map/ppermute | solution.py:33
  247.7 11.8 %collective-permute-start.28 = (bf16[160,4096]{1,0:T(8,128)(2,1)S(1)}, bf16[160,4096]{1,0:T(8,128)(2,1)S(1)}, u32[]{:S(2)}, u32[]{:S(2)}) collective-permute-start(bf16[160,4096]{1,0:T(8,128)(2,1)S(1)} %constant_dynamic-update-slice_fusion.22.refs_0_), channel_id=1, source_target_pairs={{0,2},{2,0},{4,6},{6,4},{8,10},{10,8},{12,14},{14,12},{16,18},{18,... | collective-permute-start | bytes 3932168 | tf_op jit(solution)/shard_map/ppermute | solution.py:517
  320.8 16.8 %collective-permute-start.31 = (bf16[160,2048]{1,0:T(8,128)(2,1)S(1)}, bf16[160,2048]{1,0:T(8,128)(2,1)S(1)}, u32[]{:S(2)}, u32[]{:S(2)}) collective-permute-start(bf16[160,2048]{1,0:T(8,128)(2,1)S(1)} %get-tuple-element.88), channel_id=1, source_target_pairs={{0,1},{1,0},{2,3},{3,2},{4,5},{5,4},{6,7},{7,6},{8,9},{9,8},{10,11... | collective-permute-start | bytes 1966088 | tf_op jit(solution)/shard_map/ppermute | solution.py:33
  337.7 25.0 %collective-permute-start.33 = (bf16[160,2048]{1,0:T(8,128)(2,1)S(1)}, bf16[160,2048]{1,0:T(8,128)(2,1)S(1)}, u32[]{:S(2)}, u32[]{:S(2)}) collective-permute-start(bf16[160,2048]{1,0:T(8,128)(2,1)S(1)} %get-tuple-element.77), channel_id=1, source_target_pairs={{0,1},{1,0},{2,3},{3,2},{4,5},{5,4},{6,7},{7,6},{8,9},{9,8},{10,11... | collective-permute-start | bytes 1966088 | tf_op jit(solution)/shard_map/ppermute | solution.py:33
  341.4 19.3 %collective-permute-start.35 = (bf16[40,2048]{1,0:T(8,128)(2,1)S(1)}, bf16[40,2048]{1,0:T(8,128)(2,1)S(1)}, u32[]{:S(2)}, u32[]{:S(2)}) collective-permute-start(bf16[40,2048]{1,0:T(8,128)(2,1)S(1)} %get-tuple-element.99), channel_id=1, source_target_pairs={{0,20},{2,22},{4,16},{6,18},{8,28},{10,30},{12,24},{14,26},{16,4},... | collective-permute-start | bytes 491528 | tf_op jit(solution)/shard_map/ppermute | solution.py:332
  348.7 14.0 %collective-permute-start.34 = (bf16[40,2048]{1,0:T(8,128)(2,1)S(1)}, bf16[40,2048]{1,0:T(8,128)(2,1)S(1)}, u32[]{:S(2)}, u32[]{:S(2)}) collective-permute-start(bf16[40,2048]{1,0:T(8,128)(2,1)S(1)} %get-tuple-element.100), channel_id=1, source_target_pairs={{0,16},{2,18},{4,20},{6,22},{8,24},{10,26},{12,28},{14,30},{16,0},... | collective-permute-start | bytes 491528 | tf_op jit(solution)/shard_map/ppermute | solution.py:332
  364.6 18.1 %collective-permute-start.39 = (bf16[40,2048]{1,0:T(8,128)(2,1)S(1)}, bf16[40,2048]{1,0:T(8,128)(2,1)S(1)}, u32[]{:S(2)}, u32[]{:S(2)}) collective-permute-start(bf16[40,2048]{1,0:T(8,128)(2,1)S(1)} %get-tuple-element.98), channel_id=1, source_target_pairs={{0,24},{2,26},{4,28},{6,30},{8,16},{10,18},{12,20},{14,22},{16,8},... | collective-permute-start | bytes 491528 | tf_op jit(solution)/shard_map/ppermute | solution.py:332
  367.0 15.7 %collective-permute-start.40 = (bf16[40,2048]{1,0:T(8,128)(2,1)S(1)}, bf16[40,2048]{1,0:T(8,128)(2,1)S(1)}, u32[]{:S(2)}, u32[]{:S(2)}) collective-permute-start(bf16[40,2048]{1,0:T(8,128)(2,1)S(1)} %get-tuple-element.97), channel_id=1, source_target_pairs={{0,28},{2,30},{4,24},{6,26},{8,20},{10,22},{12,16},{14,18},{16,12}... | collective-permute-start | bytes 491528 | tf_op jit(solution)/shard_map/ppermute | solution.py:332
  368.2 10.8 %collective-permute-start.37 = (bf16[40,2048]{1,0:T(8,128)(2,1)S(1)}, bf16[40,2048]{1,0:T(8,128)(2,1)S(1)}, u32[]{:S(2)}, u32[]{:S(2)}) collective-permute-start(bf16[40,2048]{1,0:T(8,128)(2,1)S(1)} %get-tuple-element.102), channel_id=1, source_target_pairs={{0,8},{2,10},{4,12},{6,14},{8,0},{10,2},{12,4},{14,6},{16,24},{18,... | collective-permute-start | bytes 491528 | tf_op jit(solution)/shard_map/ppermute | solution.py:332
  368.2 14.4 %collective-permute-start.38 = (bf16[40,2048]{1,0:T(8,128)(2,1)S(1)}, bf16[40,2048]{1,0:T(8,128)(2,1)S(1)}, u32[]{:S(2)}, u32[]{:S(2)}) collective-permute-start(bf16[40,2048]{1,0:T(8,128)(2,1)S(1)} %get-tuple-element.101), channel_id=1, source_target_pairs={{0,12},{2,14},{4,8},{6,10},{8,4},{10,6},{12,0},{14,2},{16,28},{18,... | collective-permute-start | bytes 491528 | tf_op jit(solution)/shard_map/ppermute | solution.py:332
  (43 other events, 393.4 us)

commit v6 on v5

--- a/solution.py
+++ b/solution.py
@@ -450,16 +450,25 @@
             step_size, decay_rate, conved, gain, kept, carry, pick, skip_gain, gate_in, first,
             steps,
         )
-        tokens_of.append(
-            {m: gated if m == 0 else across(gated, m) for m in (0, 2, 4) if m < low}
-        )
-    tokens_of = lax.optimization_barrier(tokens_of)
-    for got in tokens_of:
+        tokens_of.append({0: gated})
+    def joined(got, more):
         for m in range(6, low, 2):
             one = m & -m
-            got[m] = across(got[m ^ one], one) if m != one else across(got[0], m)
-    far_last, tokens_of = lax.optimization_barrier((far_last, tokens_of))
+            more[m] = across(got[m ^ one], one) if m != one else across(got[0], m)
+
+    first, later = tokens_of
+    for m in (2, 4):
+        if m < low:
+            later[m] = across(later[0], m)
+    later, first = lax.optimization_barrier((later, first))
+    for m in (2, 4):
+        if m < low:
+            first[m] = across(first[0], m)
+    joined(later, later)
+    far_last, later, first = lax.optimization_barrier((far_last, later, first))
     far_later = [jnp.concatenate(parts, axis=0) for parts in zip(far_middle, far_last)]
+    joined(first, first)
+    tokens_of = [first, later]
     all_tokens = [
         jnp.concatenate([got[m] for m in range(0, low, 2)], axis=0) for got in tokens_of
     ]
@@ -518,7 +527,7 @@
 
     parts = [
         gathered(teams_swapped(packed[first : first + near], first, members), "tp", shard, 1)
-        for first in (near, 0)
+        for first in (0, near)
     ]
     pieces = parts + [from_member(by)(part) for by in range(1, members) for part in parts]
     hidden, outs = raised(
@@ -539,10 +548,10 @@
         for by in range(2, shards)
     ]
     hidden, sent = lax.optimization_barrier((hidden, sent))
-    far_sums = [rotated(part[:rows], "tp", by) for by, part in enumerate(sent, 1)]
+    far_sums = [rotated(part[rows:], "tp", by) for by, part in enumerate(sent, 1)]
     own_outs = for_shard_of(hidden, shard)
     far_sums, own_outs, near_sent = lax.optimization_barrier(
-        (far_sums, own_outs, [part[rows:] for part in sent])
+        (far_sums, own_outs, [part[:rows] for part in sent])
     )
     near_sums = [rotated(part, "tp", by) for by, part in enumerate(near_sent, 1)]
     own_sum = member_sum(own_outs)
@@ -554,10 +563,10 @@
         return share.astype(jnp.bfloat16).reshape(near, CAP, width)
 
     ahead = near // 2
-    far_share = shared(own_sum[:rows], far_sums)
+    far_share = shared(own_sum[rows:], far_sums)
     far_ahead = teams_swapped(far_share[:ahead], near, members)
     near_sums, far_ahead = lax.optimization_barrier((near_sums, far_ahead))
-    near_share = shared(own_sum[rows:], near_sums)
+    near_share = shared(own_sum[:rows], near_sums)
     back = [
         teams_swapped(near_share, 0, members),
         far_ahead,

time: 386 us -> 354 us (0.917)
  waiting for transfers between devices: 180 us -> 151 us
    ppermute x16, waiting for transfers between devices: 75 us -> 62.3 us  [across(): lax.ppermute(x, 'loop', [(i, i ^ mask) for i in range(lax.axis_size('loop...]
    ppermute x6, waiting for transfers between devices: 40.3 us -> 29.6 us  [rotated(): return lax.ppermute(x, axis, [(i, (i + by) % size) for i in range(size)])]
    ppermute x14, waiting for transfers between devices: 43.7 us -> 38.6 us  [teams_swapped(): out.append(lax.ppermute(x[k], 'loop', pairs))]
    unnamed x80 -> x78, local copies, waits for them, and re-layouts: 11.9 us -> 11.5 us
  transfers between devices with their start and end apart: 43 -> 43, of which waited for: 26 -> 26; matrix products, arithmetic and copies ran while one was open for 9% -> 9% of each run, Pallas kernels for 9% -> 10%
where the time goes in v6:
time: 354 us; the launch traced here: 353 us
  waiting for transfers between devices  151 us (43%)
  Pallas kernels  89.5 us (25%)
  starting transfers between devices  59.3 us (17%)
  local copies, waits for them, and re-layouts  28.6 us (8%)
  matrix products  13.7 us (4%)
  other arithmetic  10.3 us (3%)
    ppermute x16, waiting for transfers between devices, across(): lax.ppermute(x, 'loop', [(i, i ^ mask) for i in range(lax.axis_size('loop...  62.3 us
    pallas_call x1, Pallas kernels, raised(): pl.pallas_call(functools.partial(raise_kernel, pieces=len(pieces), member...  51.8 us
    ppermute x14, waiting for transfers between devices, teams_swapped(): out.append(lax.ppermute(x[k], 'loop', pairs))  38.6 us
    ppermute x6, waiting for transfers between devices, rotated(): return lax.ppermute(x, axis, [(i, (i + by) % size) for i in range(size)])  29.6 us
    ppermute x14, starting transfers between devices, teams_swapped(): out.append(lax.ppermute(x[k], 'loop', pairs))  24.8 us
    pallas_call x2, Pallas kernels, scan_gated(): pl.pallas_call(scan_kernel, grid=(steps,), in_specs=[part(tokens), part(N...  13.3 us
    ppermute x16, starting transfers between devices, across(): lax.ppermute(x, 'loop', [(i, i ^ mask) for i in range(lax.axis_size('loop...  12.5 us
    unnamed x78, local copies, waits for them, and re-layouts  11.5 us
  transfers between devices with their start and end apart: 43, of which 26 were waited for; matrix products, arithmetic and copies ran while one was open for 9% of the time, Pallas kernels for 10%

profile of v6, /device:TPU:0, one launch (start us, length us, event | category | flops | bytes accessed | tf_op | source)
XLA Modules:
  0.0 353.3 jit_solution(16986473204359647371)
XLA Ops:
  5.6 3.6 %collective-permute-start.2 = (bf16[1536,256]{1,0:T(8,128)(2,1)}, bf16[1536,256]{1,0:T(8,128)(2,1)}, u32[]{:S(2)}, u32[]{:S(2)}) collective-permute-start(bf16[1536,256]{1,0:T(8,128)(2,1)} %slice.187), channel_id=1, source_target_pairs={{0,16},{2,18},{4,20},{6,22},{8,24},{10,26},{12,28},{14,30},{16,0},... | collective-permute-start | bytes 2359304 | tf_op jit(solution)/shard_map/ppermute | solution.py:320
  17.7 2.7 collective-permute-done.1
  23.3 11.2 %scan_end.1 = (f32[128,4096]{1,0:T(8,128)S(1)}, bf16[16,32,256]{2,1,0:T(8,128)(2,1)}) custom-call(bf16[128,256]{1,0:T(8,128)(2,1)S(1)} %slice.220.low_ref, bf16[256,4096]{1,0:T(8,128)(2,1)S(1)} %copy-done.13, f32[1,4096]{1,0:T(1,128)S(1)} %bitcast.32, f32[16,4096]{1,0:T(8,128)S(1)} %copy-done.10, bf16[128,4096]{1,0:T(8,128)(2,1)S(1)} %multiply_convert_fusion.conved_ref, ...), custom_call_target="tpu_custom_call" | custom-call | flops 41943040 | bytes 4194304 | tf_op jit(solution)/shard_map/scan_end/pallas_call | solution.py:128
  35.8 8.0 %collective-permute-done.2 = bf16[1536,256]{1,0:T(8,128)(2,1)} collective-permute-done((bf16[1536,256]{1,0:T(8,128)(2,1)}, bf16[1536,256]{1,0:T(8,128)(2,1)}, u32[]{:S(2)}, u32[]{:S(2)}) %collective-permute-start.2) | collective-permute-done | bytes 786464 | tf_op jit(solution)/shard_map/ppermute | solution.py:320
  43.8 6.1 %all-to-all-start = ((bf16[16,32,256]{2,1,0:T(8,128)(2,1)}), bf16[16,32,256]{2,1,0:T(8,128)(2,1)S(1)}, u32[]{:S(2)}, u32[]{:S(2)}) async-start(bf16[16,32,256]{2,1,0:T(8,128)(2,1)} %get-tuple-element.41), calls=%async_computation | async-start | bytes 524288 | tf_op jit(solution)/shard_map/all_to_all | solution.py:437
  50.5 9.4 %all-to-all-done.ends_ref = bf16[16,32,256]{2,1,0:T(8,128)(2,1)S(1)} async-done(((bf16[16,32,256]{2,1,0:T(8,128)(2,1)}), bf16[16,32,256]{2,1,0:T(8,128)(2,1)S(1)}, u32[]{:S(2)}, u32[]{:S(2)}) %all-to-all-start) | async-done | bytes 262176 | tf_op jit(solution)/shard_map/all_to_all | solution.py:437
  62.3 3.7 %all-to-all-start.1 = ((bf16[16,16,256]{2,1,0:T(8,128)(2,1)}), bf16[16,16,256]{2,1,0:T(8,128)(2,1)S(1)}, u32[]{:S(2)}, u32[]{:S(2)}) async-start(bf16[16,16,256]{2,1,0:T(8,128)(2,1)} %carries.1), calls=%async_computation.1 | async-start | bytes 262144 | tf_op jit(solution)/shard_map/all_to_all | solution.py:440
  69.7 4.1 %all-to-all-done.1.carry_ref = bf16[16,16,256]{2,1,0:T(8,128)(2,1)S(1)} async-done(((bf16[16,16,256]{2,1,0:T(8,128)(2,1)}), bf16[16,16,256]{2,1,0:T(8,128)(2,1)S(1)}, u32[]{:S(2)}, u32[]{:S(2)}) %all-to-all-start.1) | async-done | bytes 131104 | tf_op jit(solution)/shard_map/all_to_all | solution.py:440
  78.8 8.3 %scan_gated.2 = bf16[128,2560]{1,0:T(8,128)(2,1)S(1)} custom-call(f32[128,4096]{1,0:T(8,128)S(1)} %copy-done.3, f32[16,4096]{1,0:T(8,128)S(1)} %copy-done.11, bf16[128,4096]{1,0:T(8,128)(2,1)S(1)} %multiply_convert_fusion.conved_ref, f32[128,16,128]{2,1,0:T(8,128)S(1)} %broadcast_in_dim.48.gain_ref, f32[128,1]{1,0:T(8,128)S(1)} %copy.51.kept_ref, ...), custom_call_target="tpu_custom_call" | custom-call | flops 36700160 | bytes 3932160 | tf_op jit(solution)/shard_map/scan_gated/pallas_call | solution.py:171
  91.0 9.3 %collective-permute-done.3 = bf16[1024,256]{1,0:T(8,128)(2,1)S(1)} collective-permute-done((bf16[1024,256]{1,0:T(8,128)(2,1)S(1)}, bf16[1024,256]{1,0:T(8,128)(2,1)S(1)}, u32[]{:S(2)}, u32[]{:S(2)}) %collective-permute-start.3) | collective-permute-done | bytes 524320 | tf_op jit(solution)/shard_map/ppermute | solution.py:320
  100.3 5.0 %scan_gated.3 = bf16[128,1536]{1,0:T(8,128)(2,1)S(1)} custom-call(f32[128,4096]{1,0:T(8,128)S(1)} %copy-done.3, f32[16,4096]{1,0:T(8,128)S(1)} %copy-done.11, bf16[128,4096]{1,0:T(8,128)(2,1)S(1)} %multiply_convert_fusion.conved_ref, f32[128,16,128]{2,1,0:T(8,128)S(1)} %broadcast_in_dim.48.gain_ref, f32[128,1]{1,0:T(8,128)S(1)} %copy.51.kept_ref, ...), custom_call_target="tpu_custom_call" | custom-call | flops 22020096 | bytes 2359296 | tf_op jit(solution)/shard_map/scan_gated/pallas_call | solution.py:171
  105.4 10.5 %collective-permute-done.6 = bf16[128,2560]{1,0:T(8,128)(2,1)S(1)} collective-permute-done((bf16[128,2560]{1,0:T(8,128)(2,1)S(1)}, bf16[128,2560]{1,0:T(8,128)(2,1)S(1)}, u32[]{:S(2)}, u32[]{:S(2)}) %collective-permute-start.6) | collective-permute-done | bytes 655392 | tf_op jit(solution)/shard_map/ppermute | solution.py:320
  120.5 20.6 %collective-permute-done.8 = bf16[128,1536]{1,0:T(8,128)(2,1)S(1)} collective-permute-done((bf16[128,1536]{1,0:T(8,128)(2,1)S(1)}, bf16[128,1536]{1,0:T(8,128)(2,1)S(1)}, u32[]{:S(2)}, u32[]{:S(2)}) %collective-permute-start.8) | collective-permute-done | bytes 393248 | tf_op jit(solution)/shard_map/ppermute | solution.py:320
  141.1 3.6 %collective-permute-done.9 = bf16[128,1536]{1,0:T(8,128)(2,1)S(1)} collective-permute-done((bf16[128,1536]{1,0:T(8,128)(2,1)S(1)}, bf16[128,1536]{1,0:T(8,128)(2,1)S(1)}, u32[]{:S(2)}, u32[]{:S(2)}) %collective-permute-start.9) | collective-permute-done | bytes 393248 | tf_op jit(solution)/shard_map/ppermute | solution.py:320
  147.3 3.2 fusion.4
  150.5 5.9 %collective-permute-done.10 = bf16[128,1536]{1,0:T(8,128)(2,1)S(1)} collective-permute-done((bf16[128,1536]{1,0:T(8,128)(2,1)S(1)}, bf16[128,1536]{1,0:T(8,128)(2,1)S(1)}, u32[]{:S(2)}, u32[]{:S(2)}) %collective-permute-start.10) | collective-permute-done | bytes 393248 | tf_op jit(solution)/shard_map/ppermute | solution.py:320
  164.1 11.9 %collective-permute-done.15 = bf16[512,512]{1,0:T(8,128)(2,1)} collective-permute-done((bf16[512,512]{1,0:T(8,128)(2,1)S(1)}, bf16[512,512]{1,0:T(8,128)(2,1)}, u32[]{:S(2)}, u32[]{:S(2)}) %collective-permute-start.15) | collective-permute-done | bytes 524320 | tf_op jit(solution)/shard_map/ppermute | solution.py:33
  178.1 2.8 collective-permute-start.18
  193.1 3.3 collective-permute-done.21
  204.8 6.7 %collective-permute-done.23 = bf16[40,2048]{1,0:T(8,128)(2,1)S(1)} collective-permute-done((bf16[40,2048]{1,0:T(8,128)(2,1)S(1)}, bf16[40,2048]{1,0:T(8,128)(2,1)S(1)}, u32[]{:S(2)}, u32[]{:S(2)}) %collective-permute-start.23) | collective-permute-done | bytes 163872 | tf_op jit(solution)/shard_map/ppermute | solution.py:332
  211.5 2.9 collective-permute-done.24
  216.3 3.3 collective-permute-done.22
  220.8 7.4 %collective-permute-done.27 = bf16[160,2048]{1,0:T(8,128)(2,1)} collective-permute-done((bf16[160,2048]{1,0:T(8,128)(2,1)S(1)}, bf16[160,2048]{1,0:T(8,128)(2,1)}, u32[]{:S(2)}, u32[]{:S(2)}) %collective-permute-start.27) | collective-permute-done | bytes 655392 | tf_op jit(solution)/shard_map/ppermute | solution.py:33
  233.6 51.8 %raised.1 = (bf16[640,3072]{1,0:T(8,128)(2,1)}, bf16[320,2048]{1,0:T(8,128)(2,1)}, bf16[320,2048]{1,0:T(8,128)(2,1)}) custom-call(s32[1]{0:T(128)} %bitcast.12.shard_ref, bf16[160,4096]{1,0:T(8,128)(2,1)} %copy-done.16, bf16[160,4096]{1,0:T(8,128)(2,1)} %copy-done.17, bf16[160,4096]{1,0:T(8,128)(2,1)} %copy-done.28, bf16[160,4096]{1,0:T(8,128)(2,1)} %copy-done.29, ...), custom_call_target="tpu_custom_call" | custom-call | flops 40265318400 | bytes 62914560 | tf_op jit(solution)/shard_map/raised/pallas_call | solution.py:234
  285.5 3.1 collective-permute-done.30
  292.4 10.8 %lowered.1 = (bf16[320,2048]{1,0:T(8,128)(2,1)S(1)}, bf16[320,2048]{1,0:T(8,128)(2,1)S(1)}) custom-call(s32[1]{0:T(128)} %bitcast.13.shard_ref, bf16[640,3072]{1,0:T(8,128)(2,1)S(1)} %copy-done.15, bf16[1,3072,4096]{2,1,0:T(8,128)(2,1)} %weight_ref.1), custom_call_target="tpu_custom_call" | custom-call | flops 8053063680 | bytes 12582912 | tf_op jit(solution)/shard_map/lowered/pallas_call | solution.py:279
  303.3 4.3 %collective-permute-done.31 = bf16[160,2048]{1,0:T(8,128)(2,1)S(1)} collective-permute-done((bf16[160,2048]{1,0:T(8,128)(2,1)S(1)}, bf16[160,2048]{1,0:T(8,128)(2,1)S(1)}, u32[]{:S(2)}, u32[]{:S(2)}) %collective-permute-start.31) | collective-permute-done | bytes 655392 | tf_op jit(solution)/shard_map/ppermute | solution.py:33
  311.4 6.1 %collective-permute-start.35 = (bf16[40,2048]{1,0:T(8,128)(2,1)S(1)}, bf16[40,2048]{1,0:T(8,128)(2,1)S(1)}, u32[]{:S(2)}, u32[]{:S(2)}) collective-permute-start(bf16[40,2048]{1,0:T(8,128)(2,1)S(1)} %get-tuple-element.93), channel_id=1, source_target_pairs={{0,20},{2,22},{4,16},{6,18},{8,28},{10,30},{12,24},{14,26},{16,4},... | collective-permute-start | bytes 491528 | tf_op jit(solution)/shard_map/ppermute | solution.py:332
  317.5 12.0 %collective-permute-done.35 = bf16[40,2048]{1,0:T(8,128)(2,1)S(1)} collective-permute-done((bf16[40,2048]{1,0:T(8,128)(2,1)S(1)}, bf16[40,2048]{1,0:T(8,128)(2,1)S(1)}, u32[]{:S(2)}, u32[]{:S(2)}) %collective-permute-start.35) | collective-permute-done | bytes 163872 | tf_op jit(solution)/shard_map/ppermute | solution.py:332
  337.3 2.8 collective-permute-start.38
  340.2 7.7 %collective-permute-done.37 = bf16[40,2048]{1,0:T(8,128)(2,1)S(1)} collective-permute-done((bf16[40,2048]{1,0:T(8,128)(2,1)S(1)}, bf16[40,2048]{1,0:T(8,128)(2,1)S(1)}, u32[]{:S(2)}, u32[]{:S(2)}) %collective-permute-start.37) | collective-permute-done | bytes 163872 | tf_op jit(solution)/shard_map/ppermute | solution.py:332
  347.9 3.5 collective-permute-done.38
  (204 shorter events, 96.2 us)
Async XLA Ops:
  5.6 38.2 %collective-permute-start.2 = (bf16[1536,256]{1,0:T(8,128)(2,1)}, bf16[1536,256]{1,0:T(8,128)(2,1)}, u32[]{:S(2)}, u32[]{:S(2)}) collective-permute-start(bf16[1536,256]{1,0:T(8,128)(2,1)} %slice.187), channel_id=1, source_target_pairs={{0,16},{2,18},{4,20},{6,22},{8,24},{10,26},{12,28},{14,30},{16,0},... | collective-permute-start | bytes 2359304 | tf_op jit(solution)/shard_map/ppermute | solution.py:320
  43.8 16.1 %all-to-all-start = ((bf16[16,32,256]{2,1,0:T(8,128)(2,1)}), bf16[16,32,256]{2,1,0:T(8,128)(2,1)S(1)}, u32[]{:S(2)}, u32[]{:S(2)}) async-start(bf16[16,32,256]{2,1,0:T(8,128)(2,1)} %get-tuple-element.41), calls=%async_computation | async-start | bytes 524288 | tf_op jit(solution)/shard_map/all_to_all | solution.py:437
  62.3 11.4 %all-to-all-start.1 = ((bf16[16,16,256]{2,1,0:T(8,128)(2,1)}), bf16[16,16,256]{2,1,0:T(8,128)(2,1)S(1)}, u32[]{:S(2)}, u32[]{:S(2)}) async-start(bf16[16,16,256]{2,1,0:T(8,128)(2,1)} %carries.1), calls=%async_computation.1 | async-start | bytes 262144 | tf_op jit(solution)/shard_map/all_to_all | solution.py:440
  74.8 25.5 %collective-permute-start.3 = (bf16[1024,256]{1,0:T(8,128)(2,1)S(1)}, bf16[1024,256]{1,0:T(8,128)(2,1)S(1)}, u32[]{:S(2)}, u32[]{:S(2)}) collective-permute-start(bf16[1024,256]{1,0:T(8,128)(2,1)S(1)} %slice.189), channel_id=1, source_target_pairs={{0,16},{2,18},{4,20},{6,22},{8,24},{10,26},{12,28},{14,30},{16,0},... | collective-permute-start | bytes 1572872 | tf_op jit(solution)/shard_map/ppermute | solution.py:320
  87.2 18.2 %collective-permute-start.5 = (bf16[128,2560]{1,0:T(8,128)(2,1)S(1)}, bf16[128,2560]{1,0:T(8,128)(2,1)S(1)}, u32[]{:S(2)}, u32[]{:S(2)}) collective-permute-start(bf16[128,2560]{1,0:T(8,128)(2,1)S(1)} %scan_gated.2), channel_id=1, source_target_pairs={{0,4},{2,6},{4,0},{6,2},{8,12},{10,14},{12,8},{14,10},{16,20},{18,... | collective-permute-start | bytes 1966088 | tf_op jit(solution)/shard_map/ppermute | solution.py:320
  87.6 28.4 %collective-permute-start.6 = (bf16[128,2560]{1,0:T(8,128)(2,1)S(1)}, bf16[128,2560]{1,0:T(8,128)(2,1)S(1)}, u32[]{:S(2)}, u32[]{:S(2)}) collective-permute-start(bf16[128,2560]{1,0:T(8,128)(2,1)S(1)} %scan_gated.2), channel_id=1, source_target_pairs={{0,8},{2,10},{4,12},{6,14},{8,0},{10,2},{12,4},{14,6},{16,24},{18,... | collective-permute-start | bytes 1966088 | tf_op jit(solution)/shard_map/ppermute | solution.py:320
  100.3 44.4 %collective-permute-start.4 = (bf16[1536,256]{1,0:T(8,128)(2,1)}, bf16[1536,256]{1,0:T(8,128)(2,1)}, u32[]{:S(2)}, u32[]{:S(2)}) collective-permute-start(bf16[1536,256]{1,0:T(8,128)(2,1)} %slice.188), channel_id=1, source_target_pairs={{0,16},{2,18},{4,20},{6,22},{8,24},{10,26},{12,28},{14,30},{16,0},... | collective-permute-start | bytes 2359304 | tf_op jit(solution)/shard_map/ppermute | solution.py:320
  116.0 28.8 %collective-permute-start.7 = (bf16[128,2560]{1,0:T(8,128)(2,1)S(1)}, bf16[128,2560]{1,0:T(8,128)(2,1)S(1)}, u32[]{:S(2)}, u32[]{:S(2)}) collective-permute-start(bf16[128,2560]{1,0:T(8,128)(2,1)S(1)} %collective-permute-done.6), channel_id=1, source_target_pairs={{0,4},{2,6},{4,0},{6,2},{8,12},{10,14},{12,8},{14,10},{16,20},{18,... | collective-permute-start | bytes 1966088 | tf_op jit(solution)/shard_map/ppermute | solution.py:320
  117.3 30.0 %collective-permute-start.14 = (bf16[2560,256]{1,0:T(8,128)(2,1)}, bf16[2560,256]{1,0:T(8,128)(2,1)}, u32[]{:S(2)}, u32[]{:S(2)}) collective-permute-start(bf16[2560,256]{1,0:T(8,128)(2,1)} %slice.174), channel_id=1, source_target_pairs={{0,2},{2,0},{4,6},{6,4},{8,10},{10,8},{12,14},{14,12},{16,18},{18,... | collective-permute-start | bytes 3932168 | tf_op jit(solution)/shard_map/ppermute | solution.py:320
  117.6 23.6 %collective-permute-start.8 = (bf16[128,1536]{1,0:T(8,128)(2,1)S(1)}, bf16[128,1536]{1,0:T(8,128)(2,1)S(1)}, u32[]{:S(2)}, u32[]{:S(2)}) collective-permute-start(bf16[128,1536]{1,0:T(8,128)(2,1)S(1)} %scan_gated.3), channel_id=1, source_target_pairs={{0,4},{2,6},{4,0},{6,2},{8,12},{10,14},{12,8},{14,10},{16,20},{18,... | collective-permute-start | bytes 1179656 | tf_op jit(solution)/shard_map/ppermute | solution.py:320
  118.3 26.4 %collective-permute-start.9 = (bf16[128,1536]{1,0:T(8,128)(2,1)S(1)}, bf16[128,1536]{1,0:T(8,128)(2,1)S(1)}, u32[]{:S(2)}, u32[]{:S(2)}) collective-permute-start(bf16[128,1536]{1,0:T(8,128)(2,1)S(1)} %scan_gated.3), channel_id=1, source_target_pairs={{0,8},{2,10},{4,12},{6,14},{8,0},{10,2},{12,4},{14,6},{16,24},{18,... | collective-permute-start | bytes 1179656 | tf_op jit(solution)/shard_map/ppermute | solution.py:320
  141.1 15.3 %collective-permute-start.13 = (bf16[1536,256]{1,0:T(8,128)(2,1)}, bf16[1536,256]{1,0:T(8,128)(2,1)S(1)}, u32[]{:S(2)}, u32[]{:S(2)}) collective-permute-start(bf16[1536,256]{1,0:T(8,128)(2,1)} %slice.187), channel_id=1, source_target_pairs={{0,2},{2,0},{4,6},{6,4},{8,10},{10,8},{12,14},{14,12},{16,18},{18,... | collective-permute-start | bytes 2359304 | tf_op jit(solution)/shard_map/ppermute | solution.py:320
  144.7 15.4 %collective-permute-start.11 = (bf16[1536,256]{1,0:T(8,128)(2,1)}, bf16[1536,256]{1,0:T(8,128)(2,1)S(1)}, u32[]{:S(2)}, u32[]{:S(2)}) collective-permute-start(bf16[1536,256]{1,0:T(8,128)(2,1)} %collective-permute-done.2), channel_id=1, source_target_pairs={{0,2},{2,0},{4,6},{6,4},{8,10},{10,8},{12,14},{14,12},{16,18},{18,... | collective-permute-start | bytes 2359304 | tf_op jit(solution)/shard_map/ppermute | solution.py:320
  144.8 11.6 %collective-permute-start.10 = (bf16[128,1536]{1,0:T(8,128)(2,1)S(1)}, bf16[128,1536]{1,0:T(8,128)(2,1)S(1)}, u32[]{:S(2)}, u32[]{:S(2)}) collective-permute-start(bf16[128,1536]{1,0:T(8,128)(2,1)S(1)} %collective-permute-done.9), channel_id=1, source_target_pairs={{0,4},{2,6},{4,0},{6,2},{8,12},{10,14},{12,8},{14,10},{16,20},{18,... | collective-permute-start | bytes 1179656 | tf_op jit(solution)/shard_map/ppermute | solution.py:320
  146.7 11.8 %collective-permute-start.12 = (bf16[2560,256]{1,0:T(8,128)(2,1)S(1)}, bf16[2560,256]{1,0:T(8,128)(2,1)S(1)}, u32[]{:S(2)}, u32[]{:S(2)}) collective-permute-start(bf16[2560,256]{1,0:T(8,128)(2,1)S(1)} %constant_dynamic-update-slice_fusion.8), channel_id=1, source_target_pairs={{0,2},{2,0},{4,6},{6,4},{8,10},{10,8},{12,14},{14,12},{16,18},{18,... | collective-permute-start | bytes 3932168 | tf_op jit(solution)/shard_map/ppermute | solution.py:320
  162.3 13.7 %collective-permute-start.15 = (bf16[512,512]{1,0:T(8,128)(2,1)S(1)}, bf16[512,512]{1,0:T(8,128)(2,1)}, u32[]{:S(2)}, u32[]{:S(2)}) collective-permute-start(bf16[512,512]{1,0:T(8,128)(2,1)S(1)} %get-tuple-element.108), channel_id=1, source_target_pairs={{0,1},{1,0},{2,3},{3,2},{4,5},{5,4},{6,7},{7,6},{8,9},{9,8},{10,11... | collective-permute-start | bytes 1572872 | tf_op jit(solution)/shard_map/ppermute | solution.py:33
  187.7 10.4 %collective-permute-start.20 = (bf16[40,2048]{1,0:T(8,128)(2,1)S(1)}, bf16[40,2048]{1,0:T(8,128)(2,1)S(1)}, u32[]{:S(2)}, u32[]{:S(2)}) collective-permute-start(bf16[40,2048]{1,0:T(8,128)(2,1)S(1)} %get-tuple-element.88), channel_id=1, source_target_pairs={{0,8},{2,10},{4,12},{6,14},{8,0},{10,2},{12,4},{14,6},{16,24},{18,... | collective-permute-start | bytes 491528 | tf_op jit(solution)/shard_map/ppermute | solution.py:332
  188.7 11.9 %collective-permute-start.19 = (bf16[40,2048]{1,0:T(8,128)(2,1)S(1)}, bf16[40,2048]{1,0:T(8,128)(2,1)S(1)}, u32[]{:S(2)}, u32[]{:S(2)}) collective-permute-start(bf16[40,2048]{1,0:T(8,128)(2,1)S(1)} %get-tuple-element.89), channel_id=1, source_target_pairs={{0,4},{2,6},{4,0},{6,2},{8,12},{10,14},{12,8},{14,10},{16,20},{18,... | collective-permute-start | bytes 491528 | tf_op jit(solution)/shard_map/ppermute | solution.py:332
  190.0 21.5 %collective-permute-start.23 = (bf16[40,2048]{1,0:T(8,128)(2,1)S(1)}, bf16[40,2048]{1,0:T(8,128)(2,1)S(1)}, u32[]{:S(2)}, u32[]{:S(2)}) collective-permute-start(bf16[40,2048]{1,0:T(8,128)(2,1)S(1)} %get-tuple-element.86), channel_id=1, source_target_pairs={{0,16},{2,18},{4,20},{6,22},{8,24},{10,26},{12,28},{14,30},{16,0},... | collective-permute-start | bytes 491528 | tf_op jit(solution)/shard_map/ppermute | solution.py:332
  190.6 23.9 %collective-permute-start.24 = (bf16[40,2048]{1,0:T(8,128)(2,1)S(1)}, bf16[40,2048]{1,0:T(8,128)(2,1)S(1)}, u32[]{:S(2)}, u32[]{:S(2)}) collective-permute-start(bf16[40,2048]{1,0:T(8,128)(2,1)S(1)} %get-tuple-element.85), channel_id=1, source_target_pairs={{0,20},{2,22},{4,16},{6,18},{8,28},{10,30},{12,24},{14,26},{16,4},... | collective-permute-start | bytes 491528 | tf_op jit(solution)/shard_map/ppermute | solution.py:332
  196.4 18.1 %collective-permute-start.25 = (bf16[40,2048]{1,0:T(8,128)(2,1)S(1)}, bf16[40,2048]{1,0:T(8,128)(2,1)S(1)}, u32[]{:S(2)}, u32[]{:S(2)}) collective-permute-start(bf16[40,2048]{1,0:T(8,128)(2,1)S(1)} %get-tuple-element.84), channel_id=1, source_target_pairs={{0,24},{2,26},{4,28},{6,30},{8,16},{10,18},{12,20},{14,22},{16,8},... | collective-permute-start | bytes 491528 | tf_op jit(solution)/shard_map/ppermute | solution.py:332
  198.1 16.4 %collective-permute-start.26 = (bf16[40,2048]{1,0:T(8,128)(2,1)S(1)}, bf16[40,2048]{1,0:T(8,128)(2,1)S(1)}, u32[]{:S(2)}, u32[]{:S(2)}) collective-permute-start(bf16[40,2048]{1,0:T(8,128)(2,1)S(1)} %get-tuple-element.83), channel_id=1, source_target_pairs={{0,28},{2,30},{4,24},{6,26},{8,20},{10,22},{12,16},{14,18},{16,12}... | collective-permute-start | bytes 491528 | tf_op jit(solution)/shard_map/ppermute | solution.py:332
  203.3 16.3 %collective-permute-start.22 = (bf16[160,2048]{1,0:T(8,128)(2,1)}, bf16[160,2048]{1,0:T(8,128)(2,1)}, u32[]{:S(2)}, u32[]{:S(2)}) collective-permute-start(bf16[160,2048]{1,0:T(8,128)(2,1)} %get-tuple-element.99), channel_id=1, source_target_pairs={{0,1},{1,0},{2,3},{3,2},{4,5},{5,4},{6,7},{7,6},{8,9},{9,8},{10,11... | collective-permute-start | bytes 1966088 | tf_op jit(solution)/shard_map/ppermute | solution.py:33
  214.5 13.7 %collective-permute-start.27 = (bf16[160,2048]{1,0:T(8,128)(2,1)S(1)}, bf16[160,2048]{1,0:T(8,128)(2,1)}, u32[]{:S(2)}, u32[]{:S(2)}) collective-permute-start(bf16[160,2048]{1,0:T(8,128)(2,1)S(1)} %constant_dynamic-update-slice_fusion.10), channel_id=1, source_target_pairs={{0,1},{1,0},{2,3},{3,2},{4,5},{5,4},{6,7},{7,6},{8,9},{9,8},{10,11... | collective-permute-start | bytes 1966088 | tf_op jit(solution)/shard_map/ppermute | solution.py:33
  290.8 16.8 %collective-permute-start.31 = (bf16[160,2048]{1,0:T(8,128)(2,1)S(1)}, bf16[160,2048]{1,0:T(8,128)(2,1)S(1)}, u32[]{:S(2)}, u32[]{:S(2)}) collective-permute-start(bf16[160,2048]{1,0:T(8,128)(2,1)S(1)} %get-tuple-element.82), channel_id=1, source_target_pairs={{0,1},{1,0},{2,3},{3,2},{4,5},{5,4},{6,7},{7,6},{8,9},{9,8},{10,11... | collective-permute-start | bytes 1966088 | tf_op jit(solution)/shard_map/ppermute | solution.py:33
  307.6 24.1 %collective-permute-start.33 = (bf16[160,2048]{1,0:T(8,128)(2,1)S(1)}, bf16[160,2048]{1,0:T(8,128)(2,1)S(1)}, u32[]{:S(2)}, u32[]{:S(2)}) collective-permute-start(bf16[160,2048]{1,0:T(8,128)(2,1)S(1)} %get-tuple-element.71), channel_id=1, source_target_pairs={{0,1},{1,0},{2,3},{3,2},{4,5},{5,4},{6,7},{7,6},{8,9},{9,8},{10,11... | collective-permute-start | bytes 1966088 | tf_op jit(solution)/shard_map/ppermute | solution.py:33
  311.4 18.1 %collective-permute-start.35 = (bf16[40,2048]{1,0:T(8,128)(2,1)S(1)}, bf16[40,2048]{1,0:T(8,128)(2,1)S(1)}, u32[]{:S(2)}, u32[]{:S(2)}) collective-permute-start(bf16[40,2048]{1,0:T(8,128)(2,1)S(1)} %get-tuple-element.93), channel_id=1, source_target_pairs={{0,20},{2,22},{4,16},{6,18},{8,28},{10,30},{12,24},{14,26},{16,4},... | collective-permute-start | bytes 491528 | tf_op jit(solution)/shard_map/ppermute | solution.py:332
  317.5 14.2 %collective-permute-start.34 = (bf16[40,2048]{1,0:T(8,128)(2,1)S(1)}, bf16[40,2048]{1,0:T(8,128)(2,1)S(1)}, u32[]{:S(2)}, u32[]{:S(2)}) collective-permute-start(bf16[40,2048]{1,0:T(8,128)(2,1)S(1)} %get-tuple-element.94), channel_id=1, source_target_pairs={{0,16},{2,18},{4,20},{6,22},{8,24},{10,26},{12,28},{14,30},{16,0},... | collective-permute-start | bytes 491528 | tf_op jit(solution)/shard_map/ppermute | solution.py:332
  333.4 18.0 %collective-permute-start.39 = (bf16[40,2048]{1,0:T(8,128)(2,1)S(1)}, bf16[40,2048]{1,0:T(8,128)(2,1)S(1)}, u32[]{:S(2)}, u32[]{:S(2)}) collective-permute-start(bf16[40,2048]{1,0:T(8,128)(2,1)S(1)} %get-tuple-element.92), channel_id=1, source_target_pairs={{0,24},{2,26},{4,28},{6,30},{8,16},{10,18},{12,20},{14,22},{16,8},... | collective-permute-start | bytes 491528 | tf_op jit(solution)/shard_map/ppermute | solution.py:332
  334.9 16.5 %collective-permute-start.40 = (bf16[40,2048]{1,0:T(8,128)(2,1)S(1)}, bf16[40,2048]{1,0:T(8,128)(2,1)S(1)}, u32[]{:S(2)}, u32[]{:S(2)}) collective-permute-start(bf16[40,2048]{1,0:T(8,128)(2,1)S(1)} %get-tuple-element.91), channel_id=1, source_target_pairs={{0,28},{2,30},{4,24},{6,26},{8,20},{10,22},{12,16},{14,18},{16,12}... | collective-permute-start | bytes 491528 | tf_op jit(solution)/shard_map/ppermute | solution.py:332
  337.3 10.6 %collective-permute-start.37 = (bf16[40,2048]{1,0:T(8,128)(2,1)S(1)}, bf16[40,2048]{1,0:T(8,128)(2,1)S(1)}, u32[]{:S(2)}, u32[]{:S(2)}) collective-permute-start(bf16[40,2048]{1,0:T(8,128)(2,1)S(1)} %get-tuple-element.96), channel_id=1, source_target_pairs={{0,8},{2,10},{4,12},{6,14},{8,0},{10,2},{12,4},{14,6},{16,24},{18,... | collective-permute-start | bytes 491528 | tf_op jit(solution)/shard_map/ppermute | solution.py:332
  337.3 14.1 %collective-permute-start.38 = (bf16[40,2048]{1,0:T(8,128)(2,1)S(1)}, bf16[40,2048]{1,0:T(8,128)(2,1)S(1)}, u32[]{:S(2)}, u32[]{:S(2)}) collective-permute-start(bf16[40,2048]{1,0:T(8,128)(2,1)S(1)} %get-tuple-element.95), channel_id=1, source_target_pairs={{0,12},{2,14},{4,8},{6,10},{8,4},{10,6},{12,0},{14,2},{16,28},{18,... | collective-permute-start | bytes 491528 | tf_op jit(solution)/shard_map/ppermute | solution.py:332
  (42 other events, 329.3 us)

commit v7 on v6

--- a/solution.py
+++ b/solution.py
@@ -393,7 +393,7 @@
     shard = lax.axis_index("tp")
     shards = lax.axis_size("tp")
     low = groups // shards
-    first_steps = 3
+    first_steps = 2
     first_rows = channels // EIGHTHS * first_steps
     far_first = [across(out_proj[:first_rows], low * high) for high in range(1, shards)]
     conv_taps = conv_weight.shape[0]
@@ -460,10 +460,11 @@
     for m in (2, 4):
         if m < low:
             later[m] = across(later[0], m)
+    if low > 2:
+        first[2] = across(first[0], 2)
     later, first = lax.optimization_barrier((later, first))
-    for m in (2, 4):
-        if m < low:
-            first[m] = across(first[0], m)
+    if low > 4:
+        first[4] = across(first[0], 4)
     joined(later, later)
     far_last, later, first = lax.optimization_barrier((far_last, later, first))
     far_later = [jnp.concatenate(parts, axis=0) for parts in zip(far_middle, far_last)]

time: 354 us -> 350 us (0.989)
  waiting for transfers between devices: 151 us -> 141 us
    ppermute x16, waiting for transfers between devices: 62.3 us -> 54.3 us  [across(): lax.ppermute(x, 'loop', [(i, i ^ mask) for i in range(lax.axis_size('loop...]
    unnamed x78 -> x74, local copies, waits for them, and re-layouts: 11.5 us -> 13.6 us
  transfers between devices with their start and end apart: 43 -> 43, of which waited for: 26 -> 24; matrix products, arithmetic and copies ran while one was open for 9% -> 11% of each run, Pallas kernels for 10% -> 10%
where the time goes in v7:
time: 350 us; the launch traced here: 349 us
  waiting for transfers between devices  141 us (40%)
  Pallas kernels  89.5 us (26%)
  starting transfers between devices  59.1 us (17%)
  local copies, waits for them, and re-layouts  31.9 us (9%)
  matrix products  14.7 us (4%)
  other arithmetic  11.6 us (3%)
    ppermute x16, waiting for transfers between devices, across(): lax.ppermute(x, 'loop', [(i, i ^ mask) for i in range(lax.axis_size('loop...  54.3 us
    pallas_call x1, Pallas kernels, raised(): pl.pallas_call(functools.partial(raise_kernel, pieces=len(pieces), member...  51.8 us
    ppermute x14, waiting for transfers between devices, teams_swapped(): out.append(lax.ppermute(x[k], 'loop', pairs))  40.2 us
    ppermute x6, waiting for transfers between devices, rotated(): return lax.ppermute(x, axis, [(i, (i + by) % size) for i in range(size)])  27.2 us
    ppermute x14, starting transfers between devices, teams_swapped(): out.append(lax.ppermute(x[k], 'loop', pairs))  26.5 us
    unnamed x74, local copies, waits for them, and re-layouts  13.6 us
    pallas_call x2, Pallas kernels, scan_gated(): pl.pallas_call(scan_kernel, grid=(steps,), in_specs=[part(tokens), part(N...  13.3 us
    ppermute x16, starting transfers between devices, across(): lax.ppermute(x, 'loop', [(i, i ^ mask) for i in range(lax.axis_size('loop...  13.1 us
  transfers between devices with their start and end apart: 43, of which 24 were waited for; matrix products, arithmetic and copies ran while one was open for 11% of the time, Pallas kernels for 10%

profile of v7, /device:TPU:0, one launch (start us, length us, event | category | flops | bytes accessed | tf_op | source)
XLA Modules:
  0.0 349.0 jit_solution(3436253608758625825)
XLA Ops:
  5.3 3.6 %collective-permute-start.2 = (bf16[1024,256]{1,0:T(8,128)(2,1)}, bf16[1024,256]{1,0:T(8,128)(2,1)}, u32[]{:S(2)}, u32[]{:S(2)}) collective-permute-start(bf16[1024,256]{1,0:T(8,128)(2,1)} %slice.187), channel_id=1, source_target_pairs={{0,16},{2,18},{4,20},{6,22},{8,24},{10,26},{12,28},{14,30},{16,0},... | collective-permute-start | bytes 1572872 | tf_op jit(solution)/shard_map/ppermute | solution.py:320
  10.0 3.9 %multiply_convert_fusion.conved_ref = bf16[128,4096]{1,0:T(8,128)(2,1)S(1)} fusion(bf16[128,4096]{1,0:T(8,128)(2,1)} %param.18, bf16[3,4096]{1,0:T(4,128)(2,1)S(1)} %collective-permute-done, f32[4096]{0:T(1024)S(1)} %bitcast.35, f32[4096]{0:T(1024)S(1)} %bitcast.36, f32[4096]{0:T(1024)S(1)} %bitcast.34, f32[4096]{0:T(1024)S(1)} %bitcast.33, f32[4096]{0:T(1024)} %param.22), kind=kLoop, calls=%fused_computation.12 | loop fusion | flops 13631488 | bytes 2203648 | tf_op jit(solution)/shard_map/convert_element_type | solution.py:407
  20.7 2.5 collective-permute-done.1
  26.2 11.2 %scan_end.1 = (f32[128,4096]{1,0:T(8,128)S(1)}, bf16[16,32,256]{2,1,0:T(8,128)(2,1)}) custom-call(bf16[128,256]{1,0:T(8,128)(2,1)S(1)} %slice.220.low_ref, bf16[256,4096]{1,0:T(8,128)(2,1)S(1)} %copy-done.14, f32[1,4096]{1,0:T(1,128)S(1)} %bitcast.32, f32[16,4096]{1,0:T(8,128)S(1)} %copy-done.9, bf16[128,4096]{1,0:T(8,128)(2,1)S(1)} %multiply_convert_fusion.conved_ref, ...), custom_call_target="tpu_custom_call" | custom-call | flops 41943040 | bytes 4194304 | tf_op jit(solution)/shard_map/scan_end/pallas_call | solution.py:128
  38.7 3.7 %all-to-all-start = ((bf16[16,32,256]{2,1,0:T(8,128)(2,1)}), bf16[16,32,256]{2,1,0:T(8,128)(2,1)S(1)}, u32[]{:S(2)}, u32[]{:S(2)}) async-start(bf16[16,32,256]{2,1,0:T(8,128)(2,1)} %get-tuple-element.42), calls=%async_computation | async-start | bytes 524288 | tf_op jit(solution)/shard_map/all_to_all | solution.py:437
  43.0 9.4 %all-to-all-done.ends_ref = bf16[16,32,256]{2,1,0:T(8,128)(2,1)S(1)} async-done(((bf16[16,32,256]{2,1,0:T(8,128)(2,1)}), bf16[16,32,256]{2,1,0:T(8,128)(2,1)S(1)}, u32[]{:S(2)}, u32[]{:S(2)}) %all-to-all-start) | async-done | bytes 262176 | tf_op jit(solution)/shard_map/all_to_all | solution.py:437
  54.8 3.7 %all-to-all-start.1 = ((bf16[16,16,256]{2,1,0:T(8,128)(2,1)}), bf16[16,16,256]{2,1,0:T(8,128)(2,1)S(1)}, u32[]{:S(2)}, u32[]{:S(2)}) async-start(bf16[16,16,256]{2,1,0:T(8,128)(2,1)} %carries.1), calls=%async_computation.1 | async-start | bytes 262144 | tf_op jit(solution)/shard_map/all_to_all | solution.py:440
  58.6 2.8 slice.174
  63.2 3.0 all-to-all-done.1.carry_ref
  71.2 10.0 %scan_gated.2 = bf16[128,3072]{1,0:T(8,128)(2,1)S(1)} custom-call(f32[128,4096]{1,0:T(8,128)S(1)} %copy-done.3, f32[16,4096]{1,0:T(8,128)S(1)} %copy-done.9, bf16[128,4096]{1,0:T(8,128)(2,1)S(1)} %multiply_convert_fusion.conved_ref, f32[128,16,128]{2,1,0:T(8,128)S(1)} %broadcast_in_dim.48.gain_ref, f32[128,1]{1,0:T(8,128)S(1)} %copy-done.12, ...), custom_call_target="tpu_custom_call" | custom-call | flops 44040192 | bytes 4718592 | tf_op jit(solution)/shard_map/scan_gated/pallas_call | solution.py:171
  85.8 3.3 scan_gated.3
  90.0 2.9 collective-permute-done.3
  92.8 13.4 %collective-permute-done.7 = bf16[128,1024]{1,0:T(8,128)(2,1)S(1)} collective-permute-done((bf16[128,1024]{1,0:T(8,128)(2,1)S(1)}, bf16[128,1024]{1,0:T(8,128)(2,1)S(1)}, u32[]{:S(2)}, u32[]{:S(2)}) %collective-permute-start.7) | collective-permute-done | bytes 262176 | tf_op jit(solution)/shard_map/ppermute | solution.py:320
  106.2 9.4 %collective-permute-done.6 = bf16[128,3072]{1,0:T(8,128)(2,1)} collective-permute-done((bf16[128,3072]{1,0:T(8,128)(2,1)S(1)}, bf16[128,3072]{1,0:T(8,128)(2,1)}, u32[]{:S(2)}, u32[]{:S(2)}) %collective-permute-start.6) | collective-permute-done | bytes 786464 | tf_op jit(solution)/shard_map/ppermute | solution.py:320
  120.8 23.2 %collective-permute-done.9 = bf16[128,1024]{1,0:T(8,128)(2,1)} collective-permute-done((bf16[128,1024]{1,0:T(8,128)(2,1)S(1)}, bf16[128,1024]{1,0:T(8,128)(2,1)}, u32[]{:S(2)}, u32[]{:S(2)}) %collective-permute-start.9) | collective-permute-done | bytes 262176 | tf_op jit(solution)/shard_map/ppermute | solution.py:320
  146.0 3.7 %fusion.4 = f32[512,512]{1,0:T(8,128)S(1)} fusion(bf16[512,3072]{1,0:T(8,128)(2,1)S(1)} %constant_dynamic-update-slice_fusion.4, bf16[3072,256]{1,0:T(8,128)(2,1)} %collective-permute-done.14, bf16[3072,256]{1,0:T(8,128)(2,1)} %slice.174), kind=kOutput, calls=%fused_computation.4 | convolution fusion | flops 1616904192 | bytes 7340032 | tf_op jit(solution)/shard_map/dot_general | solution.py:482
  160.3 11.7 %collective-permute-done.15 = bf16[512,512]{1,0:T(8,128)(2,1)S(1)} collective-permute-done((bf16[512,512]{1,0:T(8,128)(2,1)S(1)}, bf16[512,512]{1,0:T(8,128)(2,1)S(1)}, u32[]{:S(2)}, u32[]{:S(2)}) %collective-permute-start.15) | collective-permute-done | bytes 524320 | tf_op jit(solution)/shard_map/ppermute | solution.py:33
  174.0 3.0 collective-permute-start.18
  189.1 3.2 collective-permute-done.21
  199.2 7.5 %collective-permute-done.23 = bf16[40,2048]{1,0:T(8,128)(2,1)S(1)} collective-permute-done((bf16[40,2048]{1,0:T(8,128)(2,1)S(1)}, bf16[40,2048]{1,0:T(8,128)(2,1)S(1)}, u32[]{:S(2)}, u32[]{:S(2)}) %collective-permute-start.23) | collective-permute-done | bytes 163872 | tf_op jit(solution)/shard_map/ppermute | solution.py:332
  206.7 4.3 %collective-permute-done.24 = bf16[40,2048]{1,0:T(8,128)(2,1)S(1)} collective-permute-done((bf16[40,2048]{1,0:T(8,128)(2,1)S(1)}, bf16[40,2048]{1,0:T(8,128)(2,1)S(1)}, u32[]{:S(2)}, u32[]{:S(2)}) %collective-permute-start.24) | collective-permute-done | bytes 163872 | tf_op jit(solution)/shard_map/ppermute | solution.py:332
  214.1 8.6 %collective-permute-done.27 = bf16[160,2048]{1,0:T(8,128)(2,1)} collective-permute-done((bf16[160,2048]{1,0:T(8,128)(2,1)S(1)}, bf16[160,2048]{1,0:T(8,128)(2,1)}, u32[]{:S(2)}, u32[]{:S(2)}) %collective-permute-start.27) | collective-permute-done | bytes 655392 | tf_op jit(solution)/shard_map/ppermute | solution.py:33
  228.1 51.8 %raised.1 = (bf16[640,3072]{1,0:T(8,128)(2,1)}, bf16[320,2048]{1,0:T(8,128)(2,1)}, bf16[320,2048]{1,0:T(8,128)(2,1)}) custom-call(s32[1]{0:T(128)} %bitcast.12.shard_ref, bf16[160,4096]{1,0:T(8,128)(2,1)} %copy-done.17, bf16[160,4096]{1,0:T(8,128)(2,1)} %copy-done.18, bf16[160,4096]{1,0:T(8,128)(2,1)} %copy-done.26, bf16[160,4096]{1,0:T(8,128)(2,1)} %copy-done.27, ...), custom_call_target="tpu_custom_call" | custom-call | flops 40265318400 | bytes 62914560 | tf_op jit(solution)/shard_map/raised/pallas_call | solution.py:234
  280.0 3.1 collective-permute-done.30
  286.9 10.8 %lowered.1 = (bf16[320,2048]{1,0:T(8,128)(2,1)S(1)}, bf16[320,2048]{1,0:T(8,128)(2,1)S(1)}) custom-call(s32[1]{0:T(128)} %bitcast.13.shard_ref, bf16[640,3072]{1,0:T(8,128)(2,1)S(1)} %copy-done.16, bf16[1,3072,4096]{2,1,0:T(8,128)(2,1)} %weight_ref.1), custom_call_target="tpu_custom_call" | custom-call | flops 8053063680 | bytes 12582912 | tf_op jit(solution)/shard_map/lowered/pallas_call | solution.py:279
  297.8 4.3 %collective-permute-done.31 = bf16[160,2048]{1,0:T(8,128)(2,1)S(1)} collective-permute-done((bf16[160,2048]{1,0:T(8,128)(2,1)S(1)}, bf16[160,2048]{1,0:T(8,128)(2,1)S(1)}, u32[]{:S(2)}, u32[]{:S(2)}) %collective-permute-start.31) | collective-permute-done | bytes 655392 | tf_op jit(solution)/shard_map/ppermute | solution.py:33
  305.9 7.4 %collective-permute-start.35 = (bf16[40,2048]{1,0:T(8,128)(2,1)S(1)}, bf16[40,2048]{1,0:T(8,128)(2,1)S(1)}, u32[]{:S(2)}, u32[]{:S(2)}) collective-permute-start(bf16[40,2048]{1,0:T(8,128)(2,1)S(1)} %get-tuple-element.95), channel_id=1, source_target_pairs={{0,20},{2,22},{4,16},{6,18},{8,28},{10,30},{12,24},{14,26},{16,4},... | collective-permute-start | bytes 491528 | tf_op jit(solution)/shard_map/ppermute | solution.py:332
  313.3 12.0 %collective-permute-done.35 = bf16[40,2048]{1,0:T(8,128)(2,1)S(1)} collective-permute-done((bf16[40,2048]{1,0:T(8,128)(2,1)S(1)}, bf16[40,2048]{1,0:T(8,128)(2,1)S(1)}, u32[]{:S(2)}, u32[]{:S(2)}) %collective-permute-start.35) | collective-permute-done | bytes 163872 | tf_op jit(solution)/shard_map/ppermute | solution.py:332
  330.5 2.5 collective-permute-start.40
  333.0 3.0 collective-permute-start.38
  336.0 7.7 %collective-permute-done.37 = bf16[40,2048]{1,0:T(8,128)(2,1)S(1)} collective-permute-done((bf16[40,2048]{1,0:T(8,128)(2,1)S(1)}, bf16[40,2048]{1,0:T(8,128)(2,1)S(1)}, u32[]{:S(2)}, u32[]{:S(2)}) %collective-permute-start.37) | collective-permute-done | bytes 163872 | tf_op jit(solution)/shard_map/ppermute | solution.py:332
  343.7 3.4 collective-permute-done.38
  (200 shorter events, 93.6 us)
Async XLA Ops:
  5.3 33.4 %collective-permute-start.2 = (bf16[1024,256]{1,0:T(8,128)(2,1)}, bf16[1024,256]{1,0:T(8,128)(2,1)}, u32[]{:S(2)}, u32[]{:S(2)}) collective-permute-start(bf16[1024,256]{1,0:T(8,128)(2,1)} %slice.187), channel_id=1, source_target_pairs={{0,16},{2,18},{4,20},{6,22},{8,24},{10,26},{12,28},{14,30},{16,0},... | collective-permute-start | bytes 1572872 | tf_op jit(solution)/shard_map/ppermute | solution.py:320
  38.7 13.7 %all-to-all-start = ((bf16[16,32,256]{2,1,0:T(8,128)(2,1)}), bf16[16,32,256]{2,1,0:T(8,128)(2,1)S(1)}, u32[]{:S(2)}, u32[]{:S(2)}) async-start(bf16[16,32,256]{2,1,0:T(8,128)(2,1)} %get-tuple-element.42), calls=%async_computation | async-start | bytes 524288 | tf_op jit(solution)/shard_map/all_to_all | solution.py:437
  54.8 11.4 %all-to-all-start.1 = ((bf16[16,16,256]{2,1,0:T(8,128)(2,1)}), bf16[16,16,256]{2,1,0:T(8,128)(2,1)S(1)}, u32[]{:S(2)}, u32[]{:S(2)}) async-start(bf16[16,16,256]{2,1,0:T(8,128)(2,1)} %carries.1), calls=%async_computation.1 | async-start | bytes 262144 | tf_op jit(solution)/shard_map/all_to_all | solution.py:440
  67.3 25.5 %collective-permute-start.3 = (bf16[1024,256]{1,0:T(8,128)(2,1)S(1)}, bf16[1024,256]{1,0:T(8,128)(2,1)S(1)}, u32[]{:S(2)}, u32[]{:S(2)}) collective-permute-start(bf16[1024,256]{1,0:T(8,128)(2,1)S(1)} %slice.189), channel_id=1, source_target_pairs={{0,16},{2,18},{4,20},{6,22},{8,24},{10,26},{12,28},{14,30},{16,0},... | collective-permute-start | bytes 1572872 | tf_op jit(solution)/shard_map/ppermute | solution.py:320
  81.2 25.0 %collective-permute-start.5 = (bf16[128,3072]{1,0:T(8,128)(2,1)S(1)}, bf16[128,3072]{1,0:T(8,128)(2,1)S(1)}, u32[]{:S(2)}, u32[]{:S(2)}) collective-permute-start(bf16[128,3072]{1,0:T(8,128)(2,1)S(1)} %scan_gated.2), channel_id=1, source_target_pairs={{0,4},{2,6},{4,0},{6,2},{8,12},{10,14},{12,8},{14,10},{16,20},{18,... | collective-permute-start | bytes 2359304 | tf_op jit(solution)/shard_map/ppermute | solution.py:320
  82.0 33.6 %collective-permute-start.6 = (bf16[128,3072]{1,0:T(8,128)(2,1)S(1)}, bf16[128,3072]{1,0:T(8,128)(2,1)}, u32[]{:S(2)}, u32[]{:S(2)}) collective-permute-start(bf16[128,3072]{1,0:T(8,128)(2,1)S(1)} %scan_gated.2), channel_id=1, source_target_pairs={{0,8},{2,10},{4,12},{6,14},{8,0},{10,2},{12,4},{14,6},{16,24},{18,... | collective-permute-start | bytes 2359304 | tf_op jit(solution)/shard_map/ppermute | solution.py:320
  89.1 17.0 %collective-permute-start.7 = (bf16[128,1024]{1,0:T(8,128)(2,1)S(1)}, bf16[128,1024]{1,0:T(8,128)(2,1)S(1)}, u32[]{:S(2)}, u32[]{:S(2)}) collective-permute-start(bf16[128,1024]{1,0:T(8,128)(2,1)S(1)} %scan_gated.3), channel_id=1, source_target_pairs={{0,4},{2,6},{4,0},{6,2},{8,12},{10,14},{12,8},{14,10},{16,20},{18,... | collective-permute-start | bytes 786440 | tf_op jit(solution)/shard_map/ppermute | solution.py:320
  92.8 51.1 %collective-permute-start.4 = (bf16[2048,256]{1,0:T(8,128)(2,1)}, bf16[2048,256]{1,0:T(8,128)(2,1)S(1)}, u32[]{:S(2)}, u32[]{:S(2)}) collective-permute-start(bf16[2048,256]{1,0:T(8,128)(2,1)} %slice.188), channel_id=1, source_target_pairs={{0,16},{2,18},{4,20},{6,22},{8,24},{10,26},{12,28},{14,30},{16,0},... | collective-permute-start | bytes 3145736 | tf_op jit(solution)/shard_map/ppermute | solution.py:320
  115.6 28.3 %collective-permute-start.8 = (bf16[128,3072]{1,0:T(8,128)(2,1)}, bf16[128,3072]{1,0:T(8,128)(2,1)S(1)}, u32[]{:S(2)}, u32[]{:S(2)}) collective-permute-start(bf16[128,3072]{1,0:T(8,128)(2,1)} %collective-permute-done.6), channel_id=1, source_target_pairs={{0,4},{2,6},{4,0},{6,2},{8,12},{10,14},{12,8},{14,10},{16,20},{18,... | collective-permute-start | bytes 2359304 | tf_op jit(solution)/shard_map/ppermute | solution.py:320
  117.0 29.0 %collective-permute-start.14 = (bf16[3072,256]{1,0:T(8,128)(2,1)}, bf16[3072,256]{1,0:T(8,128)(2,1)}, u32[]{:S(2)}, u32[]{:S(2)}) collective-permute-start(bf16[3072,256]{1,0:T(8,128)(2,1)} %slice.174), channel_id=1, source_target_pairs={{0,2},{2,0},{4,6},{6,4},{8,10},{10,8},{12,14},{14,12},{16,18},{18,... | collective-permute-start | bytes 4718600 | tf_op jit(solution)/shard_map/ppermute | solution.py:320
  117.0 35.9 %collective-permute-start.13 = (bf16[1024,256]{1,0:T(8,128)(2,1)}, bf16[1024,256]{1,0:T(8,128)(2,1)}, u32[]{:S(2)}, u32[]{:S(2)}) collective-permute-start(bf16[1024,256]{1,0:T(8,128)(2,1)} %slice.187), channel_id=1, source_target_pairs={{0,2},{2,0},{4,6},{6,4},{8,10},{10,8},{12,14},{14,12},{16,18},{18,... | collective-permute-start | bytes 1572872 | tf_op jit(solution)/shard_map/ppermute | solution.py:320
  119.0 24.9 %collective-permute-start.9 = (bf16[128,1024]{1,0:T(8,128)(2,1)S(1)}, bf16[128,1024]{1,0:T(8,128)(2,1)}, u32[]{:S(2)}, u32[]{:S(2)}) collective-permute-start(bf16[128,1024]{1,0:T(8,128)(2,1)S(1)} %scan_gated.3), channel_id=1, source_target_pairs={{0,8},{2,10},{4,12},{6,14},{8,0},{10,2},{12,4},{14,6},{16,24},{18,... | collective-permute-start | bytes 786440 | tf_op jit(solution)/shard_map/ppermute | solution.py:320
  143.9 12.7 %collective-permute-start.11 = (bf16[1024,256]{1,0:T(8,128)(2,1)}, bf16[1024,256]{1,0:T(8,128)(2,1)S(1)}, u32[]{:S(2)}, u32[]{:S(2)}) collective-permute-start(bf16[1024,256]{1,0:T(8,128)(2,1)} %collective-permute-done.2), channel_id=1, source_target_pairs={{0,2},{2,0},{4,6},{6,4},{8,10},{10,8},{12,14},{14,12},{16,18},{18,... | collective-permute-start | bytes 1572872 | tf_op jit(solution)/shard_map/ppermute | solution.py:320
  144.1 10.7 %collective-permute-start.12 = (bf16[3072,256]{1,0:T(8,128)(2,1)S(1)}, bf16[3072,256]{1,0:T(8,128)(2,1)S(1)}, u32[]{:S(2)}, u32[]{:S(2)}) collective-permute-start(bf16[3072,256]{1,0:T(8,128)(2,1)S(1)} %constant_dynamic-update-slice_fusion.8), channel_id=1, source_target_pairs={{0,2},{2,0},{4,6},{6,4},{8,10},{10,8},{12,14},{14,12},{16,18},{18,... | collective-permute-start | bytes 4718600 | tf_op jit(solution)/shard_map/ppermute | solution.py:320
  158.5 13.5 %collective-permute-start.15 = (bf16[512,512]{1,0:T(8,128)(2,1)S(1)}, bf16[512,512]{1,0:T(8,128)(2,1)S(1)}, u32[]{:S(2)}, u32[]{:S(2)}) collective-permute-start(bf16[512,512]{1,0:T(8,128)(2,1)S(1)} %get-tuple-element.110), channel_id=1, source_target_pairs={{0,1},{1,0},{2,3},{3,2},{4,5},{5,4},{6,7},{7,6},{8,9},{9,8},{10,11... | collective-permute-start | bytes 1572872 | tf_op jit(solution)/shard_map/ppermute | solution.py:33
  183.7 10.5 %collective-permute-start.20 = (bf16[40,2048]{1,0:T(8,128)(2,1)S(1)}, bf16[40,2048]{1,0:T(8,128)(2,1)S(1)}, u32[]{:S(2)}, u32[]{:S(2)}) collective-permute-start(bf16[40,2048]{1,0:T(8,128)(2,1)S(1)} %get-tuple-element.90), channel_id=1, source_target_pairs={{0,8},{2,10},{4,12},{6,14},{8,0},{10,2},{12,4},{14,6},{16,24},{18,... | collective-permute-start | bytes 491528 | tf_op jit(solution)/shard_map/ppermute | solution.py:332
  184.7 11.9 %collective-permute-start.19 = (bf16[40,2048]{1,0:T(8,128)(2,1)S(1)}, bf16[40,2048]{1,0:T(8,128)(2,1)S(1)}, u32[]{:S(2)}, u32[]{:S(2)}) collective-permute-start(bf16[40,2048]{1,0:T(8,128)(2,1)S(1)} %get-tuple-element.91), channel_id=1, source_target_pairs={{0,4},{2,6},{4,0},{6,2},{8,12},{10,14},{12,8},{14,10},{16,20},{18,... | collective-permute-start | bytes 491528 | tf_op jit(solution)/shard_map/ppermute | solution.py:332
  186.0 20.7 %collective-permute-start.23 = (bf16[40,2048]{1,0:T(8,128)(2,1)S(1)}, bf16[40,2048]{1,0:T(8,128)(2,1)S(1)}, u32[]{:S(2)}, u32[]{:S(2)}) collective-permute-start(bf16[40,2048]{1,0:T(8,128)(2,1)S(1)} %get-tuple-element.88), channel_id=1, source_target_pairs={{0,16},{2,18},{4,20},{6,22},{8,24},{10,26},{12,28},{14,30},{16,0},... | collective-permute-start | bytes 491528 | tf_op jit(solution)/shard_map/ppermute | solution.py:332
  187.2 23.8 %collective-permute-start.24 = (bf16[40,2048]{1,0:T(8,128)(2,1)S(1)}, bf16[40,2048]{1,0:T(8,128)(2,1)S(1)}, u32[]{:S(2)}, u32[]{:S(2)}) collective-permute-start(bf16[40,2048]{1,0:T(8,128)(2,1)S(1)} %get-tuple-element.87), channel_id=1, source_target_pairs={{0,20},{2,22},{4,16},{6,18},{8,28},{10,30},{12,24},{14,26},{16,4},... | collective-permute-start | bytes 491528 | tf_op jit(solution)/shard_map/ppermute | solution.py:332
  192.3 18.7 %collective-permute-start.25 = (bf16[40,2048]{1,0:T(8,128)(2,1)S(1)}, bf16[40,2048]{1,0:T(8,128)(2,1)S(1)}, u32[]{:S(2)}, u32[]{:S(2)}) collective-permute-start(bf16[40,2048]{1,0:T(8,128)(2,1)S(1)} %get-tuple-element.86), channel_id=1, source_target_pairs={{0,24},{2,26},{4,28},{6,30},{8,16},{10,18},{12,20},{14,22},{16,8},... | collective-permute-start | bytes 491528 | tf_op jit(solution)/shard_map/ppermute | solution.py:332
  194.2 16.9 %collective-permute-start.26 = (bf16[40,2048]{1,0:T(8,128)(2,1)S(1)}, bf16[40,2048]{1,0:T(8,128)(2,1)S(1)}, u32[]{:S(2)}, u32[]{:S(2)}) collective-permute-start(bf16[40,2048]{1,0:T(8,128)(2,1)S(1)} %get-tuple-element.85), channel_id=1, source_target_pairs={{0,28},{2,30},{4,24},{6,26},{8,20},{10,22},{12,16},{14,18},{16,12}... | collective-permute-start | bytes 491528 | tf_op jit(solution)/shard_map/ppermute | solution.py:332
  197.7 15.2 %collective-permute-start.22 = (bf16[160,2048]{1,0:T(8,128)(2,1)}, bf16[160,2048]{1,0:T(8,128)(2,1)}, u32[]{:S(2)}, u32[]{:S(2)}) collective-permute-start(bf16[160,2048]{1,0:T(8,128)(2,1)} %get-tuple-element.101), channel_id=1, source_target_pairs={{0,1},{1,0},{2,3},{3,2},{4,5},{5,4},{6,7},{7,6},{8,9},{9,8},{10,11... | collective-permute-start | bytes 1966088 | tf_op jit(solution)/shard_map/ppermute | solution.py:33
  211.1 11.7 %collective-permute-start.27 = (bf16[160,2048]{1,0:T(8,128)(2,1)S(1)}, bf16[160,2048]{1,0:T(8,128)(2,1)}, u32[]{:S(2)}, u32[]{:S(2)}) collective-permute-start(bf16[160,2048]{1,0:T(8,128)(2,1)S(1)} %constant_dynamic-update-slice_fusion.10), channel_id=1, source_target_pairs={{0,1},{1,0},{2,3},{3,2},{4,5},{5,4},{6,7},{7,6},{8,9},{9,8},{10,11... | collective-permute-start | bytes 1966088 | tf_op jit(solution)/shard_map/ppermute | solution.py:33
  214.0 9.9 %collective-permute-start.28 = (bf16[160,4096]{1,0:T(8,128)(2,1)S(1)}, bf16[160,4096]{1,0:T(8,128)(2,1)S(1)}, u32[]{:S(2)}, u32[]{:S(2)}) collective-permute-start(bf16[160,4096]{1,0:T(8,128)(2,1)S(1)} %constant_dynamic-update-slice_fusion.22.refs_0_), channel_id=1, source_target_pairs={{0,2},{2,0},{4,6},{6,4},{8,10},{10,8},{12,14},{14,12},{16,18},{18,... | collective-permute-start | bytes 3932168 | tf_op jit(solution)/shard_map/ppermute | solution.py:527
  285.3 16.8 %collective-permute-start.31 = (bf16[160,2048]{1,0:T(8,128)(2,1)S(1)}, bf16[160,2048]{1,0:T(8,128)(2,1)S(1)}, u32[]{:S(2)}, u32[]{:S(2)}) collective-permute-start(bf16[160,2048]{1,0:T(8,128)(2,1)S(1)} %get-tuple-element.84), channel_id=1, source_target_pairs={{0,1},{1,0},{2,3},{3,2},{4,5},{5,4},{6,7},{7,6},{8,9},{9,8},{10,11... | collective-permute-start | bytes 1966088 | tf_op jit(solution)/shard_map/ppermute | solution.py:33
  302.1 25.3 %collective-permute-start.33 = (bf16[160,2048]{1,0:T(8,128)(2,1)S(1)}, bf16[160,2048]{1,0:T(8,128)(2,1)S(1)}, u32[]{:S(2)}, u32[]{:S(2)}) collective-permute-start(bf16[160,2048]{1,0:T(8,128)(2,1)S(1)} %get-tuple-element.73), channel_id=1, source_target_pairs={{0,1},{1,0},{2,3},{3,2},{4,5},{5,4},{6,7},{7,6},{8,9},{9,8},{10,11... | collective-permute-start | bytes 1966088 | tf_op jit(solution)/shard_map/ppermute | solution.py:33
  305.9 19.4 %collective-permute-start.35 = (bf16[40,2048]{1,0:T(8,128)(2,1)S(1)}, bf16[40,2048]{1,0:T(8,128)(2,1)S(1)}, u32[]{:S(2)}, u32[]{:S(2)}) collective-permute-start(bf16[40,2048]{1,0:T(8,128)(2,1)S(1)} %get-tuple-element.95), channel_id=1, source_target_pairs={{0,20},{2,22},{4,16},{6,18},{8,28},{10,30},{12,24},{14,26},{16,4},... | collective-permute-start | bytes 491528 | tf_op jit(solution)/shard_map/ppermute | solution.py:332
  313.3 14.1 %collective-permute-start.34 = (bf16[40,2048]{1,0:T(8,128)(2,1)S(1)}, bf16[40,2048]{1,0:T(8,128)(2,1)S(1)}, u32[]{:S(2)}, u32[]{:S(2)}) collective-permute-start(bf16[40,2048]{1,0:T(8,128)(2,1)S(1)} %get-tuple-element.96), channel_id=1, source_target_pairs={{0,16},{2,18},{4,20},{6,22},{8,24},{10,26},{12,28},{14,30},{16,0},... | collective-permute-start | bytes 491528 | tf_op jit(solution)/shard_map/ppermute | solution.py:332
  329.2 17.9 %collective-permute-start.39 = (bf16[40,2048]{1,0:T(8,128)(2,1)S(1)}, bf16[40,2048]{1,0:T(8,128)(2,1)S(1)}, u32[]{:S(2)}, u32[]{:S(2)}) collective-permute-start(bf16[40,2048]{1,0:T(8,128)(2,1)S(1)} %get-tuple-element.94), channel_id=1, source_target_pairs={{0,24},{2,26},{4,28},{6,30},{8,16},{10,18},{12,20},{14,22},{16,8},... | collective-permute-start | bytes 491528 | tf_op jit(solution)/shard_map/ppermute | solution.py:332
  330.5 16.6 %collective-permute-start.40 = (bf16[40,2048]{1,0:T(8,128)(2,1)S(1)}, bf16[40,2048]{1,0:T(8,128)(2,1)S(1)}, u32[]{:S(2)}, u32[]{:S(2)}) collective-permute-start(bf16[40,2048]{1,0:T(8,128)(2,1)S(1)} %get-tuple-element.93), channel_id=1, source_target_pairs={{0,28},{2,30},{4,24},{6,26},{8,20},{10,22},{12,16},{14,18},{16,12}... | collective-permute-start | bytes 491528 | tf_op jit(solution)/shard_map/ppermute | solution.py:332
  333.0 10.7 %collective-permute-start.37 = (bf16[40,2048]{1,0:T(8,128)(2,1)S(1)}, bf16[40,2048]{1,0:T(8,128)(2,1)S(1)}, u32[]{:S(2)}, u32[]{:S(2)}) collective-permute-start(bf16[40,2048]{1,0:T(8,128)(2,1)S(1)} %get-tuple-element.98), channel_id=1, source_target_pairs={{0,8},{2,10},{4,12},{6,14},{8,0},{10,2},{12,4},{14,6},{16,24},{18,... | collective-permute-start | bytes 491528 | tf_op jit(solution)/shard_map/ppermute | solution.py:332
  333.0 14.1 %collective-permute-start.38 = (bf16[40,2048]{1,0:T(8,128)(2,1)S(1)}, bf16[40,2048]{1,0:T(8,128)(2,1)S(1)}, u32[]{:S(2)}, u32[]{:S(2)}) collective-permute-start(bf16[40,2048]{1,0:T(8,128)(2,1)S(1)} %get-tuple-element.97), channel_id=1, source_target_pairs={{0,12},{2,14},{4,8},{6,10},{8,4},{10,6},{12,0},{14,2},{16,28},{18,... | collective-permute-start | bytes 491528 | tf_op jit(solution)/shard_map/ppermute | solution.py:332
  (40 other events, 337.2 us)

commit v8 on v7

--- a/solution.py
+++ b/solution.py
@@ -439,7 +439,7 @@
     own_rates = lax.dynamic_slice_in_dim(decay_rate, position * chunk, chunk, 1)
     carry = lax.all_to_all(carries(ends, own_rates), "loop", 0, 0, tiled=True)
     later_rows, carry = lax.optimization_barrier((out_proj[first_rows:], carry))
-    middle_rows = channels // EIGHTHS * 2
+    middle_rows = channels // EIGHTHS * 3
     far_middle = [across(later_rows[:middle_rows], low * high) for high in range(1, shards)]
     last_rows, far_middle = lax.optimization_barrier((later_rows[middle_rows:], far_middle))
     far_last = [across(last_rows, low * high) for high in range(1, shards)]

time: 350 us -> 351 us (level)
  waiting for transfers between devices: 141 us -> 147 us
  local copies, waits for them, and re-layouts: 31.9 us -> 27.7 us
    unnamed x74 -> x72, local copies, waits for them, and re-layouts: 13.6 us -> 9.31 us
    ppermute x16, waiting for transfers between devices: 54.3 us -> 58.4 us  [across(): lax.ppermute(x, 'loop', [(i, i ^ mask) for i in range(lax.axis_size('loop...]
  transfers between devices with their start and end apart: 43 -> 43, of which waited for: 24 -> 23; matrix products, arithmetic and copies ran while one was open for 11% -> 11% of each run, Pallas kernels for 10% -> 10%
where the time goes in v8:
time: 351 us; the launch traced here: 350 us
  waiting for transfers between devices  147 us (42%)
  Pallas kernels  89.5 us (25%)
  starting transfers between devices  58.6 us (17%)
  local copies, waits for them, and re-layouts  27.7 us (8%)
  matrix products  14.8 us (4%)
  other arithmetic  11.6 us (3%)
    ppermute x16, waiting for transfers between devices, across(): lax.ppermute(x, 'loop', [(i, i ^ mask) for i in range(lax.axis_size('loop...  58.4 us
    pallas_call x1, Pallas kernels, raised(): pl.pallas_call(functools.partial(raise_kernel, pieces=len(pieces), member...  51.8 us
    ppermute x14, waiting for transfers between devices, teams_swapped(): out.append(lax.ppermute(x[k], 'loop', pairs))  42 us
    ppermute x6, waiting for transfers between devices, rotated(): return lax.ppermute(x, axis, [(i, (i + by) % size) for i in range(size)])  27.4 us
    ppermute x14, starting transfers between devices, teams_swapped(): out.append(lax.ppermute(x[k], 'loop', pairs))  25.7 us
    ppermute x16, starting transfers between devices, across(): lax.ppermute(x, 'loop', [(i, i ^ mask) for i in range(lax.axis_size('loop...  13.4 us
    pallas_call x2, Pallas kernels, scan_gated(): pl.pallas_call(scan_kernel, grid=(steps,), in_specs=[part(tokens), part(N...  13.3 us
    pallas_call x1, Pallas kernels, scan_end(): pl.pallas_call(scan_end_kernel, grid=(channels // width,), in_specs=[whol...  11.2 us
  transfers between devices with their start and end apart: 43, of which 23 were waited for; matrix products, arithmetic and copies ran while one was open for 11% of the time, Pallas kernels for 10%

profile of v8, /device:TPU:0, one launch (start us, length us, event | category | flops | bytes accessed | tf_op | source)
XLA Modules:
  0.0 350.4 jit_solution(17503321304148693662)
XLA Ops:
  5.2 3.6 %collective-permute-start.2 = (bf16[1024,256]{1,0:T(8,128)(2,1)}, bf16[1024,256]{1,0:T(8,128)(2,1)}, u32[]{:S(2)}, u32[]{:S(2)}) collective-permute-start(bf16[1024,256]{1,0:T(8,128)(2,1)} %slice.187), channel_id=1, source_target_pairs={{0,16},{2,18},{4,20},{6,22},{8,24},{10,26},{12,28},{14,30},{16,0},... | collective-permute-start | bytes 1572872 | tf_op jit(solution)/shard_map/ppermute | solution.py:320
  9.9 3.9 %multiply_convert_fusion.conved_ref = bf16[128,4096]{1,0:T(8,128)(2,1)S(1)} fusion(bf16[128,4096]{1,0:T(8,128)(2,1)} %param.18, bf16[3,4096]{1,0:T(4,128)(2,1)S(1)} %collective-permute-done, f32[4096]{0:T(1024)S(1)} %bitcast.35, f32[4096]{0:T(1024)S(1)} %bitcast.36, f32[4096]{0:T(1024)S(1)} %bitcast.34, f32[4096]{0:T(1024)S(1)} %bitcast.33, f32[4096]{0:T(1024)} %param.22), kind=kLoop, calls=%fused_computation.12 | loop fusion | flops 13631488 | bytes 2203648 | tf_op jit(solution)/shard_map/convert_element_type | solution.py:407
  20.6 2.6 collective-permute-done.1
  26.2 11.2 %scan_end.1 = (f32[128,4096]{1,0:T(8,128)S(1)}, bf16[16,32,256]{2,1,0:T(8,128)(2,1)}) custom-call(bf16[128,256]{1,0:T(8,128)(2,1)S(1)} %slice.220.low_ref, bf16[256,4096]{1,0:T(8,128)(2,1)S(1)} %copy-done.14, f32[1,4096]{1,0:T(1,128)S(1)} %bitcast.32, f32[16,4096]{1,0:T(8,128)S(1)} %copy-done.9, bf16[128,4096]{1,0:T(8,128)(2,1)S(1)} %multiply_convert_fusion.conved_ref, ...), custom_call_target="tpu_custom_call" | custom-call | flops 41943040 | bytes 4194304 | tf_op jit(solution)/shard_map/scan_end/pallas_call | solution.py:128
  38.7 3.7 %all-to-all-start = ((bf16[16,32,256]{2,1,0:T(8,128)(2,1)}), bf16[16,32,256]{2,1,0:T(8,128)(2,1)S(1)}, u32[]{:S(2)}, u32[]{:S(2)}) async-start(bf16[16,32,256]{2,1,0:T(8,128)(2,1)} %get-tuple-element.42), calls=%async_computation | async-start | bytes 524288 | tf_op jit(solution)/shard_map/all_to_all | solution.py:437
  43.0 9.4 %all-to-all-done.ends_ref = bf16[16,32,256]{2,1,0:T(8,128)(2,1)S(1)} async-done(((bf16[16,32,256]{2,1,0:T(8,128)(2,1)}), bf16[16,32,256]{2,1,0:T(8,128)(2,1)S(1)}, u32[]{:S(2)}, u32[]{:S(2)}) %all-to-all-start) | async-done | bytes 262176 | tf_op jit(solution)/shard_map/all_to_all | solution.py:437
  54.8 3.7 %all-to-all-start.1 = ((bf16[16,16,256]{2,1,0:T(8,128)(2,1)}), bf16[16,16,256]{2,1,0:T(8,128)(2,1)S(1)}, u32[]{:S(2)}, u32[]{:S(2)}) async-start(bf16[16,16,256]{2,1,0:T(8,128)(2,1)} %carries.1), calls=%async_computation.1 | async-start | bytes 262144 | tf_op jit(solution)/shard_map/all_to_all | solution.py:440
  58.5 2.7 slice.174
  63.2 3.1 all-to-all-done.1.carry_ref
  66.3 2.5 fusion.37
  69.1 10.0 %scan_gated.2 = bf16[128,3072]{1,0:T(8,128)(2,1)S(1)} custom-call(f32[128,4096]{1,0:T(8,128)S(1)} %copy-done.3, f32[16,4096]{1,0:T(8,128)S(1)} %copy-done.9, bf16[128,4096]{1,0:T(8,128)(2,1)S(1)} %multiply_convert_fusion.conved_ref, f32[128,16,128]{2,1,0:T(8,128)S(1)} %broadcast_in_dim.48.gain_ref, f32[128,1]{1,0:T(8,128)S(1)} %copy-done.12, ...), custom_call_target="tpu_custom_call" | custom-call | flops 44040192 | bytes 4718592 | tf_op jit(solution)/shard_map/scan_gated/pallas_call | solution.py:171
  81.4 3.3 scan_gated.3
  85.6 20.0 %collective-permute-done.3 = bf16[1536,256]{1,0:T(8,128)(2,1)} collective-permute-done((bf16[1536,256]{1,0:T(8,128)(2,1)S(1)}, bf16[1536,256]{1,0:T(8,128)(2,1)}, u32[]{:S(2)}, u32[]{:S(2)}) %collective-permute-start.3) | collective-permute-done | bytes 786464 | tf_op jit(solution)/shard_map/ppermute | solution.py:320
  105.6 10.2 %collective-permute-done.6 = bf16[128,3072]{1,0:T(8,128)(2,1)} collective-permute-done((bf16[128,3072]{1,0:T(8,128)(2,1)S(1)}, bf16[128,3072]{1,0:T(8,128)(2,1)}, u32[]{:S(2)}, u32[]{:S(2)}) %collective-permute-start.6) | collective-permute-done | bytes 786464 | tf_op jit(solution)/shard_map/ppermute | solution.py:320
  120.9 23.6 %collective-permute-done.9 = bf16[128,1024]{1,0:T(8,128)(2,1)S(1)} collective-permute-done((bf16[128,1024]{1,0:T(8,128)(2,1)S(1)}, bf16[128,1024]{1,0:T(8,128)(2,1)S(1)}, u32[]{:S(2)}, u32[]{:S(2)}) %collective-permute-start.9) | collective-permute-done | bytes 262176 | tf_op jit(solution)/shard_map/ppermute | solution.py:320
  148.1 3.7 %fusion.4 = f32[512,512]{1,0:T(8,128)S(1)} fusion(bf16[512,3072]{1,0:T(8,128)(2,1)S(1)} %constant_dynamic-update-slice_fusion.4, bf16[3072,256]{1,0:T(8,128)(2,1)} %collective-permute-done.14, bf16[3072,256]{1,0:T(8,128)(2,1)} %slice.174), kind=kOutput, calls=%fused_computation.4 | convolution fusion | flops 1616904192 | bytes 7340032 | tf_op jit(solution)/shard_map/dot_general | solution.py:482
  160.6 11.7 %collective-permute-done.15 = bf16[512,512]{1,0:T(8,128)(2,1)S(1)} collective-permute-done((bf16[512,512]{1,0:T(8,128)(2,1)S(1)}, bf16[512,512]{1,0:T(8,128)(2,1)S(1)}, u32[]{:S(2)}, u32[]{:S(2)}) %collective-permute-start.15) | collective-permute-done | bytes 524320 | tf_op jit(solution)/shard_map/ppermute | solution.py:33
  174.5 2.7 collective-permute-start.18
  189.4 2.9 collective-permute-done.21
  194.4 2.8 collective-permute-start.26
  199.9 7.9 %collective-permute-done.23 = bf16[40,2048]{1,0:T(8,128)(2,1)S(1)} collective-permute-done((bf16[40,2048]{1,0:T(8,128)(2,1)S(1)}, bf16[40,2048]{1,0:T(8,128)(2,1)S(1)}, u32[]{:S(2)}, u32[]{:S(2)}) %collective-permute-start.23) | collective-permute-done | bytes 163872 | tf_op jit(solution)/shard_map/ppermute | solution.py:332
  207.8 3.7 %collective-permute-done.24 = bf16[40,2048]{1,0:T(8,128)(2,1)S(1)} collective-permute-done((bf16[40,2048]{1,0:T(8,128)(2,1)S(1)}, bf16[40,2048]{1,0:T(8,128)(2,1)S(1)}, u32[]{:S(2)}, u32[]{:S(2)}) %collective-permute-start.24) | collective-permute-done | bytes 163872 | tf_op jit(solution)/shard_map/ppermute | solution.py:332
  214.6 8.7 %collective-permute-done.27 = bf16[160,2048]{1,0:T(8,128)(2,1)} collective-permute-done((bf16[160,2048]{1,0:T(8,128)(2,1)S(1)}, bf16[160,2048]{1,0:T(8,128)(2,1)}, u32[]{:S(2)}, u32[]{:S(2)}) %collective-permute-start.27) | collective-permute-done | bytes 655392 | tf_op jit(solution)/shard_map/ppermute | solution.py:33
  228.6 51.8 %raised.1 = (bf16[640,3072]{1,0:T(8,128)(2,1)}, bf16[320,2048]{1,0:T(8,128)(2,1)}, bf16[320,2048]{1,0:T(8,128)(2,1)}) custom-call(s32[1]{0:T(128)} %bitcast.12.shard_ref, bf16[160,4096]{1,0:T(8,128)(2,1)} %copy-done.17, bf16[160,4096]{1,0:T(8,128)(2,1)} %copy-done.18, bf16[160,4096]{1,0:T(8,128)(2,1)} %copy-done.25, bf16[160,4096]{1,0:T(8,128)(2,1)} %copy-done.26, ...), custom_call_target="tpu_custom_call" | custom-call | flops 40265318400 | bytes 62914560 | tf_op jit(solution)/shard_map/raised/pallas_call | solution.py:234
  280.6 3.1 collective-permute-done.30
  287.5 10.8 %lowered.1 = (bf16[320,2048]{1,0:T(8,128)(2,1)S(1)}, bf16[320,2048]{1,0:T(8,128)(2,1)S(1)}) custom-call(s32[1]{0:T(128)} %bitcast.13.shard_ref, bf16[640,3072]{1,0:T(8,128)(2,1)S(1)} %copy-done.16, bf16[1,3072,4096]{2,1,0:T(8,128)(2,1)} %weight_ref.1), custom_call_target="tpu_custom_call" | custom-call | flops 8053063680 | bytes 12582912 | tf_op jit(solution)/shard_map/lowered/pallas_call | solution.py:279
  298.3 4.3 %collective-permute-done.31 = bf16[160,2048]{1,0:T(8,128)(2,1)S(1)} collective-permute-done((bf16[160,2048]{1,0:T(8,128)(2,1)S(1)}, bf16[160,2048]{1,0:T(8,128)(2,1)S(1)}, u32[]{:S(2)}, u32[]{:S(2)}) %collective-permute-start.31) | collective-permute-done | bytes 655392 | tf_op jit(solution)/shard_map/ppermute | solution.py:33
  306.4 7.1 %collective-permute-start.35 = (bf16[40,2048]{1,0:T(8,128)(2,1)S(1)}, bf16[40,2048]{1,0:T(8,128)(2,1)S(1)}, u32[]{:S(2)}, u32[]{:S(2)}) collective-permute-start(bf16[40,2048]{1,0:T(8,128)(2,1)S(1)} %get-tuple-element.97), channel_id=1, source_target_pairs={{0,20},{2,22},{4,16},{6,18},{8,28},{10,30},{12,24},{14,26},{16,4},... | collective-permute-start | bytes 491528 | tf_op jit(solution)/shard_map/ppermute | solution.py:332
  313.8 11.7 %collective-permute-done.35 = bf16[40,2048]{1,0:T(8,128)(2,1)S(1)} collective-permute-done((bf16[40,2048]{1,0:T(8,128)(2,1)S(1)}, bf16[40,2048]{1,0:T(8,128)(2,1)S(1)}, u32[]{:S(2)}, u32[]{:S(2)}) %collective-permute-start.35) | collective-permute-done | bytes 163872 | tf_op jit(solution)/shard_map/ppermute | solution.py:332
  325.6 3.2 collective-permute-done.34
  336.2 7.7 %collective-permute-done.37 = bf16[40,2048]{1,0:T(8,128)(2,1)S(1)} collective-permute-done((bf16[40,2048]{1,0:T(8,128)(2,1)S(1)}, bf16[40,2048]{1,0:T(8,128)(2,1)S(1)}, u32[]{:S(2)}, u32[]{:S(2)}) %collective-permute-start.37) | collective-permute-done | bytes 163872 | tf_op jit(solution)/shard_map/ppermute | solution.py:332
  344.0 4.5 %collective-permute-done.38 = bf16[40,2048]{1,0:T(8,128)(2,1)S(1)} collective-permute-done((bf16[40,2048]{1,0:T(8,128)(2,1)S(1)}, bf16[40,2048]{1,0:T(8,128)(2,1)S(1)}, u32[]{:S(2)}, u32[]{:S(2)}) %collective-permute-start.38) | collective-permute-done | bytes 163872 | tf_op jit(solution)/shard_map/ppermute | solution.py:332
  (197 shorter events, 87.1 us)
Async XLA Ops:
  5.2 33.5 %collective-permute-start.2 = (bf16[1024,256]{1,0:T(8,128)(2,1)}, bf16[1024,256]{1,0:T(8,128)(2,1)}, u32[]{:S(2)}, u32[]{:S(2)}) collective-permute-start(bf16[1024,256]{1,0:T(8,128)(2,1)} %slice.187), channel_id=1, source_target_pairs={{0,16},{2,18},{4,20},{6,22},{8,24},{10,26},{12,28},{14,30},{16,0},... | collective-permute-start | bytes 1572872 | tf_op jit(solution)/shard_map/ppermute | solution.py:320
  38.7 13.7 %all-to-all-start = ((bf16[16,32,256]{2,1,0:T(8,128)(2,1)}), bf16[16,32,256]{2,1,0:T(8,128)(2,1)S(1)}, u32[]{:S(2)}, u32[]{:S(2)}) async-start(bf16[16,32,256]{2,1,0:T(8,128)(2,1)} %get-tuple-element.42), calls=%async_computation | async-start | bytes 524288 | tf_op jit(solution)/shard_map/all_to_all | solution.py:437
  54.8 11.4 %all-to-all-start.1 = ((bf16[16,16,256]{2,1,0:T(8,128)(2,1)}), bf16[16,16,256]{2,1,0:T(8,128)(2,1)S(1)}, u32[]{:S(2)}, u32[]{:S(2)}) async-start(bf16[16,16,256]{2,1,0:T(8,128)(2,1)} %carries.1), calls=%async_computation.1 | async-start | bytes 262144 | tf_op jit(solution)/shard_map/all_to_all | solution.py:440
  68.8 36.8 %collective-permute-start.3 = (bf16[1536,256]{1,0:T(8,128)(2,1)S(1)}, bf16[1536,256]{1,0:T(8,128)(2,1)}, u32[]{:S(2)}, u32[]{:S(2)}) collective-permute-start(bf16[1536,256]{1,0:T(8,128)(2,1)S(1)} %get-tuple-element.83), channel_id=1, source_target_pairs={{0,16},{2,18},{4,20},{6,22},{8,24},{10,26},{12,28},{14,30},{16,0},... | collective-permute-start | bytes 2359304 | tf_op jit(solution)/shard_map/ppermute | solution.py:320
  79.2 26.4 %collective-permute-start.5 = (bf16[128,3072]{1,0:T(8,128)(2,1)S(1)}, bf16[128,3072]{1,0:T(8,128)(2,1)S(1)}, u32[]{:S(2)}, u32[]{:S(2)}) collective-permute-start(bf16[128,3072]{1,0:T(8,128)(2,1)S(1)} %scan_gated.2), channel_id=1, source_target_pairs={{0,4},{2,6},{4,0},{6,2},{8,12},{10,14},{12,8},{14,10},{16,20},{18,... | collective-permute-start | bytes 2359304 | tf_op jit(solution)/shard_map/ppermute | solution.py:320
  79.9 35.9 %collective-permute-start.6 = (bf16[128,3072]{1,0:T(8,128)(2,1)S(1)}, bf16[128,3072]{1,0:T(8,128)(2,1)}, u32[]{:S(2)}, u32[]{:S(2)}) collective-permute-start(bf16[128,3072]{1,0:T(8,128)(2,1)S(1)} %scan_gated.2), channel_id=1, source_target_pairs={{0,8},{2,10},{4,12},{6,14},{8,0},{10,2},{12,4},{14,6},{16,24},{18,... | collective-permute-start | bytes 2359304 | tf_op jit(solution)/shard_map/ppermute | solution.py:320
  84.7 20.8 %collective-permute-start.7 = (bf16[128,1024]{1,0:T(8,128)(2,1)S(1)}, bf16[128,1024]{1,0:T(8,128)(2,1)S(1)}, u32[]{:S(2)}, u32[]{:S(2)}) collective-permute-start(bf16[128,1024]{1,0:T(8,128)(2,1)S(1)} %scan_gated.3), channel_id=1, source_target_pairs={{0,4},{2,6},{4,0},{6,2},{8,12},{10,14},{12,8},{14,10},{16,20},{18,... | collective-permute-start | bytes 786440 | tf_op jit(solution)/shard_map/ppermute | solution.py:320
  105.5 38.9 %collective-permute-start.4 = (bf16[1536,256]{1,0:T(8,128)(2,1)}, bf16[1536,256]{1,0:T(8,128)(2,1)}, u32[]{:S(2)}, u32[]{:S(2)}) collective-permute-start(bf16[1536,256]{1,0:T(8,128)(2,1)} %get-tuple-element.44), channel_id=1, source_target_pairs={{0,16},{2,18},{4,20},{6,22},{8,24},{10,26},{12,28},{14,30},{16,0},... | collective-permute-start | bytes 2359304 | tf_op jit(solution)/shard_map/ppermute | solution.py:320
  115.7 28.7 %collective-permute-start.8 = (bf16[128,3072]{1,0:T(8,128)(2,1)}, bf16[128,3072]{1,0:T(8,128)(2,1)S(1)}, u32[]{:S(2)}, u32[]{:S(2)}) collective-permute-start(bf16[128,3072]{1,0:T(8,128)(2,1)} %collective-permute-done.6), channel_id=1, source_target_pairs={{0,4},{2,6},{4,0},{6,2},{8,12},{10,14},{12,8},{14,10},{16,20},{18,... | collective-permute-start | bytes 2359304 | tf_op jit(solution)/shard_map/ppermute | solution.py:320
  117.0 31.1 %collective-permute-start.14 = (bf16[3072,256]{1,0:T(8,128)(2,1)}, bf16[3072,256]{1,0:T(8,128)(2,1)}, u32[]{:S(2)}, u32[]{:S(2)}) collective-permute-start(bf16[3072,256]{1,0:T(8,128)(2,1)} %slice.174), channel_id=1, source_target_pairs={{0,2},{2,0},{4,6},{6,4},{8,10},{10,8},{12,14},{14,12},{16,18},{18,... | collective-permute-start | bytes 4718600 | tf_op jit(solution)/shard_map/ppermute | solution.py:320
  117.0 36.2 %collective-permute-start.13 = (bf16[1024,256]{1,0:T(8,128)(2,1)}, bf16[1024,256]{1,0:T(8,128)(2,1)}, u32[]{:S(2)}, u32[]{:S(2)}) collective-permute-start(bf16[1024,256]{1,0:T(8,128)(2,1)} %slice.187), channel_id=1, source_target_pairs={{0,2},{2,0},{4,6},{6,4},{8,10},{10,8},{12,14},{14,12},{16,18},{18,... | collective-permute-start | bytes 1572872 | tf_op jit(solution)/shard_map/ppermute | solution.py:320
  119.4 25.0 %collective-permute-start.9 = (bf16[128,1024]{1,0:T(8,128)(2,1)S(1)}, bf16[128,1024]{1,0:T(8,128)(2,1)S(1)}, u32[]{:S(2)}, u32[]{:S(2)}) collective-permute-start(bf16[128,1024]{1,0:T(8,128)(2,1)S(1)} %scan_gated.3), channel_id=1, source_target_pairs={{0,8},{2,10},{4,12},{6,14},{8,0},{10,2},{12,4},{14,6},{16,24},{18,... | collective-permute-start | bytes 786440 | tf_op jit(solution)/shard_map/ppermute | solution.py:320
  144.5 12.5 %collective-permute-start.11 = (bf16[1024,256]{1,0:T(8,128)(2,1)}, bf16[1024,256]{1,0:T(8,128)(2,1)S(1)}, u32[]{:S(2)}, u32[]{:S(2)}) collective-permute-start(bf16[1024,256]{1,0:T(8,128)(2,1)} %collective-permute-done.2), channel_id=1, source_target_pairs={{0,2},{2,0},{4,6},{6,4},{8,10},{10,8},{12,14},{14,12},{16,18},{18,... | collective-permute-start | bytes 1572872 | tf_op jit(solution)/shard_map/ppermute | solution.py:320
  158.8 13.5 %collective-permute-start.15 = (bf16[512,512]{1,0:T(8,128)(2,1)S(1)}, bf16[512,512]{1,0:T(8,128)(2,1)S(1)}, u32[]{:S(2)}, u32[]{:S(2)}) collective-permute-start(bf16[512,512]{1,0:T(8,128)(2,1)S(1)} %get-tuple-element.112), channel_id=1, source_target_pairs={{0,1},{1,0},{2,3},{3,2},{4,5},{5,4},{6,7},{7,6},{8,9},{9,8},{10,11... | collective-permute-start | bytes 1572872 | tf_op jit(solution)/shard_map/ppermute | solution.py:33
  182.7 9.6 %collective-permute-start.21 = (bf16[40,2048]{1,0:T(8,128)(2,1)S(1)}, bf16[40,2048]{1,0:T(8,128)(2,1)S(1)}, u32[]{:S(2)}, u32[]{:S(2)}) collective-permute-start(bf16[40,2048]{1,0:T(8,128)(2,1)S(1)} %get-tuple-element.91), channel_id=1, source_target_pairs={{0,12},{2,14},{4,8},{6,10},{8,4},{10,6},{12,0},{14,2},{16,28},{18,... | collective-permute-start | bytes 491528 | tf_op jit(solution)/shard_map/ppermute | solution.py:332
  184.0 10.3 %collective-permute-start.20 = (bf16[40,2048]{1,0:T(8,128)(2,1)S(1)}, bf16[40,2048]{1,0:T(8,128)(2,1)S(1)}, u32[]{:S(2)}, u32[]{:S(2)}) collective-permute-start(bf16[40,2048]{1,0:T(8,128)(2,1)S(1)} %get-tuple-element.92), channel_id=1, source_target_pairs={{0,8},{2,10},{4,12},{6,14},{8,0},{10,2},{12,4},{14,6},{16,24},{18,... | collective-permute-start | bytes 491528 | tf_op jit(solution)/shard_map/ppermute | solution.py:332
  185.0 12.1 %collective-permute-start.19 = (bf16[40,2048]{1,0:T(8,128)(2,1)S(1)}, bf16[40,2048]{1,0:T(8,128)(2,1)S(1)}, u32[]{:S(2)}, u32[]{:S(2)}) collective-permute-start(bf16[40,2048]{1,0:T(8,128)(2,1)S(1)} %get-tuple-element.93), channel_id=1, source_target_pairs={{0,4},{2,6},{4,0},{6,2},{8,12},{10,14},{12,8},{14,10},{16,20},{18,... | collective-permute-start | bytes 491528 | tf_op jit(solution)/shard_map/ppermute | solution.py:332
  186.3 21.4 %collective-permute-start.23 = (bf16[40,2048]{1,0:T(8,128)(2,1)S(1)}, bf16[40,2048]{1,0:T(8,128)(2,1)S(1)}, u32[]{:S(2)}, u32[]{:S(2)}) collective-permute-start(bf16[40,2048]{1,0:T(8,128)(2,1)S(1)} %get-tuple-element.90), channel_id=1, source_target_pairs={{0,16},{2,18},{4,20},{6,22},{8,24},{10,26},{12,28},{14,30},{16,0},... | collective-permute-start | bytes 491528 | tf_op jit(solution)/shard_map/ppermute | solution.py:332
  187.9 23.6 %collective-permute-start.24 = (bf16[40,2048]{1,0:T(8,128)(2,1)S(1)}, bf16[40,2048]{1,0:T(8,128)(2,1)S(1)}, u32[]{:S(2)}, u32[]{:S(2)}) collective-permute-start(bf16[40,2048]{1,0:T(8,128)(2,1)S(1)} %get-tuple-element.89), channel_id=1, source_target_pairs={{0,20},{2,22},{4,16},{6,18},{8,28},{10,30},{12,24},{14,26},{16,4},... | collective-permute-start | bytes 491528 | tf_op jit(solution)/shard_map/ppermute | solution.py:332
  192.4 19.1 %collective-permute-start.25 = (bf16[40,2048]{1,0:T(8,128)(2,1)S(1)}, bf16[40,2048]{1,0:T(8,128)(2,1)S(1)}, u32[]{:S(2)}, u32[]{:S(2)}) collective-permute-start(bf16[40,2048]{1,0:T(8,128)(2,1)S(1)} %get-tuple-element.88), channel_id=1, source_target_pairs={{0,24},{2,26},{4,28},{6,30},{8,16},{10,18},{12,20},{14,22},{16,8},... | collective-permute-start | bytes 491528 | tf_op jit(solution)/shard_map/ppermute | solution.py:332
  194.4 17.2 %collective-permute-start.26 = (bf16[40,2048]{1,0:T(8,128)(2,1)S(1)}, bf16[40,2048]{1,0:T(8,128)(2,1)S(1)}, u32[]{:S(2)}, u32[]{:S(2)}) collective-permute-start(bf16[40,2048]{1,0:T(8,128)(2,1)S(1)} %get-tuple-element.87), channel_id=1, source_target_pairs={{0,28},{2,30},{4,24},{6,26},{8,20},{10,22},{12,16},{14,18},{16,12}... | collective-permute-start | bytes 491528 | tf_op jit(solution)/shard_map/ppermute | solution.py:332
  198.3 15.0 %collective-permute-start.22 = (bf16[160,2048]{1,0:T(8,128)(2,1)}, bf16[160,2048]{1,0:T(8,128)(2,1)}, u32[]{:S(2)}, u32[]{:S(2)}) collective-permute-start(bf16[160,2048]{1,0:T(8,128)(2,1)} %get-tuple-element.103), channel_id=1, source_target_pairs={{0,1},{1,0},{2,3},{3,2},{4,5},{5,4},{6,7},{7,6},{8,9},{9,8},{10,11... | collective-permute-start | bytes 1966088 | tf_op jit(solution)/shard_map/ppermute | solution.py:33
  211.6 11.7 %collective-permute-start.27 = (bf16[160,2048]{1,0:T(8,128)(2,1)S(1)}, bf16[160,2048]{1,0:T(8,128)(2,1)}, u32[]{:S(2)}, u32[]{:S(2)}) collective-permute-start(bf16[160,2048]{1,0:T(8,128)(2,1)S(1)} %constant_dynamic-update-slice_fusion.10), channel_id=1, source_target_pairs={{0,1},{1,0},{2,3},{3,2},{4,5},{5,4},{6,7},{7,6},{8,9},{9,8},{10,11... | collective-permute-start | bytes 1966088 | tf_op jit(solution)/shard_map/ppermute | solution.py:33
  214.5 10.0 %collective-permute-start.28 = (bf16[160,4096]{1,0:T(8,128)(2,1)S(1)}, bf16[160,4096]{1,0:T(8,128)(2,1)S(1)}, u32[]{:S(2)}, u32[]{:S(2)}) collective-permute-start(bf16[160,4096]{1,0:T(8,128)(2,1)S(1)} %constant_dynamic-update-slice_fusion.22.refs_0_), channel_id=1, source_target_pairs={{0,2},{2,0},{4,6},{6,4},{8,10},{10,8},{12,14},{14,12},{16,18},{18,... | collective-permute-start | bytes 3932168 | tf_op jit(solution)/shard_map/ppermute | solution.py:527
  285.8 16.8 %collective-permute-start.31 = (bf16[160,2048]{1,0:T(8,128)(2,1)S(1)}, bf16[160,2048]{1,0:T(8,128)(2,1)S(1)}, u32[]{:S(2)}, u32[]{:S(2)}) collective-permute-start(bf16[160,2048]{1,0:T(8,128)(2,1)S(1)} %get-tuple-element.86), channel_id=1, source_target_pairs={{0,1},{1,0},{2,3},{3,2},{4,5},{5,4},{6,7},{7,6},{8,9},{9,8},{10,11... | collective-permute-start | bytes 1966088 | tf_op jit(solution)/shard_map/ppermute | solution.py:33
  302.7 26.1 %collective-permute-start.33 = (bf16[160,2048]{1,0:T(8,128)(2,1)S(1)}, bf16[160,2048]{1,0:T(8,128)(2,1)S(1)}, u32[]{:S(2)}, u32[]{:S(2)}) collective-permute-start(bf16[160,2048]{1,0:T(8,128)(2,1)S(1)} %get-tuple-element.73), channel_id=1, source_target_pairs={{0,1},{1,0},{2,3},{3,2},{4,5},{5,4},{6,7},{7,6},{8,9},{9,8},{10,11... | collective-permute-start | bytes 1966088 | tf_op jit(solution)/shard_map/ppermute | solution.py:33
  306.4 19.1 %collective-permute-start.35 = (bf16[40,2048]{1,0:T(8,128)(2,1)S(1)}, bf16[40,2048]{1,0:T(8,128)(2,1)S(1)}, u32[]{:S(2)}, u32[]{:S(2)}) collective-permute-start(bf16[40,2048]{1,0:T(8,128)(2,1)S(1)} %get-tuple-element.97), channel_id=1, source_target_pairs={{0,20},{2,22},{4,16},{6,18},{8,28},{10,30},{12,24},{14,26},{16,4},... | collective-permute-start | bytes 491528 | tf_op jit(solution)/shard_map/ppermute | solution.py:332
  313.5 15.2 %collective-permute-start.34 = (bf16[40,2048]{1,0:T(8,128)(2,1)S(1)}, bf16[40,2048]{1,0:T(8,128)(2,1)S(1)}, u32[]{:S(2)}, u32[]{:S(2)}) collective-permute-start(bf16[40,2048]{1,0:T(8,128)(2,1)S(1)} %get-tuple-element.98), channel_id=1, source_target_pairs={{0,16},{2,18},{4,20},{6,22},{8,24},{10,26},{12,28},{14,30},{16,0},... | collective-permute-start | bytes 491528 | tf_op jit(solution)/shard_map/ppermute | solution.py:332
  329.5 19.0 %collective-permute-start.39 = (bf16[40,2048]{1,0:T(8,128)(2,1)S(1)}, bf16[40,2048]{1,0:T(8,128)(2,1)S(1)}, u32[]{:S(2)}, u32[]{:S(2)}) collective-permute-start(bf16[40,2048]{1,0:T(8,128)(2,1)S(1)} %get-tuple-element.96), channel_id=1, source_target_pairs={{0,24},{2,26},{4,28},{6,30},{8,16},{10,18},{12,20},{14,22},{16,8},... | collective-permute-start | bytes 491528 | tf_op jit(solution)/shard_map/ppermute | solution.py:332
  331.9 16.6 %collective-permute-start.40 = (bf16[40,2048]{1,0:T(8,128)(2,1)S(1)}, bf16[40,2048]{1,0:T(8,128)(2,1)S(1)}, u32[]{:S(2)}, u32[]{:S(2)}) collective-permute-start(bf16[40,2048]{1,0:T(8,128)(2,1)S(1)} %get-tuple-element.95), channel_id=1, source_target_pairs={{0,28},{2,30},{4,24},{6,26},{8,20},{10,22},{12,16},{14,18},{16,12}... | collective-permute-start | bytes 491528 | tf_op jit(solution)/shard_map/ppermute | solution.py:332
  334.4 9.6 %collective-permute-start.37 = (bf16[40,2048]{1,0:T(8,128)(2,1)S(1)}, bf16[40,2048]{1,0:T(8,128)(2,1)S(1)}, u32[]{:S(2)}, u32[]{:S(2)}) collective-permute-start(bf16[40,2048]{1,0:T(8,128)(2,1)S(1)} %get-tuple-element.100), channel_id=1, source_target_pairs={{0,8},{2,10},{4,12},{6,14},{8,0},{10,2},{12,4},{14,6},{16,24},{18,... | collective-permute-start | bytes 491528 | tf_op jit(solution)/shard_map/ppermute | solution.py:332
  334.4 14.1 %collective-permute-start.38 = (bf16[40,2048]{1,0:T(8,128)(2,1)S(1)}, bf16[40,2048]{1,0:T(8,128)(2,1)S(1)}, u32[]{:S(2)}, u32[]{:S(2)}) collective-permute-start(bf16[40,2048]{1,0:T(8,128)(2,1)S(1)} %get-tuple-element.99), channel_id=1, source_target_pairs={{0,12},{2,14},{4,8},{6,10},{8,4},{10,6},{12,0},{14,2},{16,28},{18,... | collective-permute-start | bytes 491528 | tf_op jit(solution)/shard_map/ppermute | solution.py:332
  (39 other events, 328.7 us)
